TPU v7x, 128 devices: a whole 4x4x4 slice. The times are simulated.
128 devices in a mesh: freq: 4 (over z), tile: 32 (over x, y, core).
Axes of the slice: x: 4, y: 4, z: 4, core: 2. Of those that a mesh axis runs over, the one named last changes fastest.
Arguments:
- data_vec: float32 [2, 64, 4, 2048], P(None, 'freq', None, 'tile'), may hold values from -40 to 40
- direction: float32 [2, 64, 4, 15360], P(None, 'freq', None, 'tile'), may hold values from -40 to 40
- model: float32 [2, 64, 4, 15360], P(None, 'freq', None, 'tile'), may hold values from -6 to 6
- alpha: float32 [], replicated, may hold values from 0.5 to 2
- u_factor: bfloat16 [64, 480, 2, 48, 256], P('freq', 'tile'), may hold values from -0.125 to 0.125
- v_factor: bfloat16 [64, 480, 2, 48, 256], P('freq', 'tile'), may hold values from -0.375 to 0.375
- ranks: int32 [64, 480], P('freq', 'tile'), may hold values from 16 to 48
- tile_source_block: int32 [480], P('tile'), may hold values from 0 to 7, as said below
- tile_receiver_block: int32 [480], P('tile'), may hold values from 0 to 59
- time_lo: int32 [15360], P('tile'), may hold values from 0 to 255
- time_len: int32 [15360], P('tile'), may hold values from 128 to 256
Outputs:
- u_next: float32 [2, 64, 4, 2048], P(None, 'freq', None, 'tile')
- v_next: float32 [2, 64, 4, 15360], P(None, 'freq', None, 'tile')
- model_next: float32 [2, 64, 4, 15360], P(None, 'freq', None, 'tile')
Inputs may be any that keep to these rules, and one draw needn't show every extreme that they name: tile_source_block and tile_receiver_block together name each tile of the 8 x 60 grid exactly once, in the order of a Hilbert curve over the grid placed in the smallest power-of-two square that holds it (cells outside the grid skipped), with the grid's rows, its columns or both possibly reversed first and the start of the order moved cyclically by any number of slots; a device's slots are consecutive in that order.
All inputs are finite; a program needn't handle non-finite values.
Results may differ from a plain program's by a relative error of at most 0.0038.
Values may be sent and summed in bfloat16 or wider, within the bound.
No kernel may reach another device: no remote copies, remote signals or barrier semaphores. Data moves between devices by JAX's collectives and lax.ppermute only.
A program may use at most 192 MiB of HBM per device.

v0:
```python
import math

import jax
import jax.numpy as jnp
from jax import lax
from jax.sharding import PartitionSpec as P

WINDOW_FREQS = 64
NT = 512
FLO = 8
TILE_EXTENT = 256
RMAX = 48
RECEIVER_BLOCKS = 60


shrink_level = 0.5
eps = 1e-06


def tile_apply(first, second, keep, tile_pieces):
    fr = first[:, :, 0]
    fi = first[:, :, 1]
    sr = second[:, :, 0]
    si = second[:, :, 1]
    zr = jnp.einsum(
        "ftrk,fvtk->fvtr", fr, tile_pieces[0], preferred_element_type=jnp.float32
    ) + jnp.einsum("ftrk,fvtk->fvtr", fi, tile_pieces[1], preferred_element_type=jnp.float32)
    zi = jnp.einsum(
        "ftrk,fvtk->fvtr", fr, tile_pieces[1], preferred_element_type=jnp.float32
    ) - jnp.einsum("ftrk,fvtk->fvtr", fi, tile_pieces[0], preferred_element_type=jnp.float32)
    zr = (zr * keep).astype(jnp.bfloat16)
    zi = (zi * keep).astype(jnp.bfloat16)
    cr = jnp.einsum("ftrk,fvtr->fvtk", sr, zr, preferred_element_type=jnp.float32) - jnp.einsum(
        "ftrk,fvtr->fvtk", si, zi, preferred_element_type=jnp.float32
    )
    ci = jnp.einsum("ftrk,fvtr->fvtk", sr, zi, preferred_element_type=jnp.float32) + jnp.einsum(
        "ftrk,fvtr->fvtk", si, zr, preferred_element_type=jnp.float32
    )
    return (cr, ci)


def place(real_component, imag_part, index, block_list):
    onehot = (index[:, None] == jnp.arange(block_list, dtype=jnp.int32)[None, :]).astype(
        jnp.float32
    )
    hp = lax.Precision.HIGHEST
    output_real = jnp.einsum("fvtk,tb->fvbk", real_component, onehot, precision=hp)
    output_imaginary = jnp.einsum("fvtk,tb->fvbk", imag_part, onehot, precision=hp)
    leading_extent = real_component.shape[0]
    virtual_source = real_component.shape[1]
    return jnp.stack([output_real, output_imaginary]).reshape(
        2, leading_extent, virtual_source, block_list * real_component.shape[3]
    )


def shrink(wide, lo, length):
    hp = lax.Precision.HIGHEST
    steps = jnp.arange(NT, dtype=jnp.int32)
    bins = FLO + jnp.arange(WINDOW_FREQS, dtype=jnp.int32)
    phase = (bins[:, None] * steps[None, :] % NT).astype(jnp.float32) * (2.0 * math.pi / NT)
    cosine = jnp.cos(phase)
    sine = jnp.sin(phase)
    signal = (
        jnp.einsum("kn,kvr->nvr", cosine, wide[0], precision=hp)
        - jnp.einsum("kn,kvr->nvr", sine, wide[1], precision=hp)
    ) / math.sqrt(WINDOW_FREQS)
    moment = steps[:, None, None]
    inside = (moment >= lo[None, None, :]) & (moment < (lo + length)[None, None, :])
    kept = jnp.where(
        inside, jnp.sign(signal) * jnp.maximum(jnp.abs(signal) - shrink_level, 0.0), 0.0
    )
    factor = 2.0 * math.sqrt(WINDOW_FREQS) / NT
    back_re = factor * jnp.einsum("kn,nvr->kvr", cosine, kept, precision=hp)
    back_im = -factor * jnp.einsum("kn,nvr->kvr", sine, kept, precision=hp)
    return jnp.stack([back_re, back_im])


def direction_scale(v_raw, count):
    total = lax.psum(jnp.sum(v_raw * v_raw), ("freq", "tile"))
    return jnp.sqrt(total / count + eps)


def on_device(
    data_vec,
    direction,
    model,
    alpha,
    u_factor,
    v_factor,
    ranks,
    tile_source_block,
    tile_receiver_block,
    time_lo,
    time_len,
):
    frequency_group = direction.shape[1]
    virtual_source = direction.shape[2]
    tiles_n = lax.axis_size("tile")
    freq_n = lax.axis_size("freq")
    keep = (jnp.arange(RMAX, dtype=jnp.int32)[None, None, :] < ranks[:, :, None]).astype(
        jnp.float32
    )[:, None]
    collected_rows = lax.all_gather(direction.astype(jnp.bfloat16), "tile", axis=3, tiled=True)
    tile_pieces = jnp.take(
        collected_rows.reshape(2, frequency_group, virtual_source, RECEIVER_BLOCKS, TILE_EXTENT),
        tile_receiver_block,
        axis=3,
    )
    cr, ci = tile_apply(v_factor, u_factor, keep, tile_pieces)
    source_row_blocks = data_vec.shape[3] * tiles_n // TILE_EXTENT
    partial_value = place(cr, ci, tile_source_block, source_row_blocks)
    summed = lax.psum_scatter(partial_value, "tile", scatter_dimension=3, tiled=True)
    u_raw = summed - alpha * data_vec
    left_count = 2 * WINDOW_FREQS * virtual_source * source_row_blocks * TILE_EXTENT
    beta = jnp.sqrt(lax.psum(jnp.sum(u_raw * u_raw), ("freq", "tile")) / left_count + eps)
    u_next = u_raw / beta
    every_row = lax.all_gather(u_next.astype(jnp.bfloat16), "tile", axis=3, tiled=True)
    piece_rows = jnp.take(
        every_row.reshape(2, frequency_group, virtual_source, source_row_blocks, TILE_EXTENT),
        tile_source_block,
        axis=3,
    )
    dr, di = tile_apply(u_factor, v_factor, keep, piece_rows)
    back = place(dr, di, tile_receiver_block, RECEIVER_BLOCKS)
    right_count = 2 * WINDOW_FREQS * virtual_source * RECEIVER_BLOCKS * TILE_EXTENT
    quarter = RECEIVER_BLOCKS * TILE_EXTENT // (tiles_n * freq_n)
    v_raw = (
        lax.psum_scatter(back.astype(jnp.bfloat16), "tile", scatter_dimension=3, tiled=True).astype(
            jnp.float32
        )
        - beta * direction
    )
    alpha_next = direction_scale(v_raw, right_count)
    v_next = v_raw / alpha_next
    wide = model + v_next
    local = lax.all_to_all(wide, "freq", split_axis=3, concat_axis=1, tiled=True)
    start = lax.axis_index("freq") * quarter
    lo = lax.dynamic_slice_in_dim(time_lo, start, quarter, 0)
    length = lax.dynamic_slice_in_dim(time_len, start, quarter, 0)
    shrunk = shrink(local, lo, length)
    model_next = lax.all_to_all(shrunk, "freq", split_axis=1, concat_axis=3, tiled=True)
    return (u_next, v_next, model_next)


def solution(mesh):
    placed = (
        P(None, "freq", None, "tile"),
        P(None, "freq", None, "tile"),
        P(None, "freq", None, "tile"),
        P(),
        P("freq", "tile", None, None, None),
        P("freq", "tile", None, None, None),
        P("freq", "tile"),
        P("tile"),
        P("tile"),
        P("tile"),
        P("tile"),
    )
    return jax.shard_map(
        on_device,
        mesh=mesh,
        in_specs=placed,
        out_specs=(
            P(None, "freq", None, "tile"),
            P(None, "freq", None, "tile"),
            P(None, "freq", None, "tile"),
        ),
        check_vma=False,
    )
```

profile of v0, /device:TPU:0, one launch (start us, length us, event | category | flops | bytes accessed | tf_op | source)
XLA Modules:
  0.0 745.6 jit_solution(326856561566253357)
XLA Ops:
  11.8 109.2 %all-gather.2.cloned.1.call-done = bf16[2,16,4,15360]{1,2,0,3:T(4,128)(2,1)} async-done(((bf16[2,16,4,480]{1,2,0,3:T(4,128)(2,1)}), bf16[2,16,4,15360]{1,2,0,3:T(4,128)(2,1)}) %all-gather.2.cloned.1.call-update) | async-done | bytes 3932176 | tf_op jit(solution)/shard_map/all_gather | solution.py:103
  121.0 36.0 %copy.84 = bf16[2,16,4,60,256]{4,1,3,2,0:T(8,128)(2,1)} copy(bf16[2,16,4,60,256]{1,2,0,4,3:T(4,128)(2,1)} %bitcast.206) | data formatting | bytes 7864320 | tf_op jit(solution)/shard_map/reshape | solution.py:105
  157.0 3.9 gather_fusion
  162.7 4.5 fusion.22
  167.2 4.5 fusion.20
  171.7 4.5 fusion.118
  181.9 3.6 fusion.64
  186.7 26.2 %copy.115 = f32[2,16,4,2048]{2,1,0,3:T(8,128)} copy(f32[2,16,4,2048]{3,2,1,0:T(4,128)S(1)} %pad_maximum_fusion.1) | data formatting | bytes 2097152
  212.9 39.2 %reshape.119 = f32[2048,128]{1,0:T(8,128)} reshape(f32[2048,2,16,4]{3,2,1,0:T(8,128)} %bitcast.196) | data formatting | bytes 2097152
  252.8 76.2 %reduce-scatter.7.cloned.1.call-done = f32[64,128]{1,0:T(8,128)} async-done(((f32[2048,128]{1,0:T(8,128)}), f32[64,128]{1,0:T(8,128)}) %reduce-scatter.7.cloned.1.call-update) | async-done | bytes 32784
  332.1 65.0 %psum.14 = f32[]{:T(128)} all-reduce(f32[]{:T(128)} %multiply_reduce_fusion.1), channel_id=1, replica_groups=mesh['freq'=4,'tile'=32] {'freq','tile'}, use_global_device_ids=true, to_apply=%region_2.3 | all-reduce | flops 1 | bytes 8 | tf_op jit(solution)/shard_map/psum | solution.py:115
  398.6 27.9 %all_gather.7 = bf16[2,16,4,2048]{1,2,0,3:T(4,128)(2,1)} all-gather(bf16[2,16,4,64]{1,2,0,3:T(4,128)(2,1)S(1)} %copy.92), channel_id=1, replica_groups=mesh['freq'=4,'tile'=32] {'tile'}, dimensions={3}, use_global_device_ids=true | all-gather | bytes 540672 | tf_op jit(solution)/shard_map/all_gather | solution.py:117
  426.4 6.7 copy.94
  437.8 4.5 fusion.2
  442.3 4.4 fusion
  449.0 3.8 fusion.16
  464.4 3.6 fusion.52
  474.1 3.8 pad_maximum_fusion
  477.9 35.4 %copy.117 = bf16[2,16,4,15360]{1,2,0,3:T(4,128)(2,1)} copy(bf16[2,16,4,15360]{3,1,2,0:T(8,128)(2,1)} %pad_maximum_fusion) | data formatting | bytes 7864320
  513.3 40.4 %reshape.121 = bf16[15360,128]{1,0:T(8,128)(2,1)} reshape(bf16[15360,2,4,16]{3,2,1,0:T(4,128)(2,1)} %bitcast.197) | data formatting | bytes 7864320
  554.6 78.6 %reduce-scatter.9.cloned.1.call-done = bf16[480,128]{1,0:T(8,128)(2,1)} async-done(((bf16[15360,128]{1,0:T(8,128)(2,1)}), bf16[480,128]{1,0:T(8,128)(2,1)}) %reduce-scatter.9.cloned.1.call-update) | async-done | bytes 122896
  637.2 64.8 %psum.15 = f32[]{:T(128)} all-reduce(f32[]{:T(128)} %multiply_reduce_fusion), channel_id=1, replica_groups=mesh['freq'=4,'tile'=32] {'freq','tile'}, use_global_device_ids=true, to_apply=%region_5.6 | all-reduce | flops 1 | bytes 8 | tf_op jit(solution)/shard_map/psum | solution.py:79
  709.7 6.4 all-to-all-done
  732.0 5.8 all-to-all-done.1
  (113 shorter events, 70.6 us)
Async XLA Ops:
  7.2 113.8 %all-gather.2.cloned.1.call-start = ((), (), s32[]{:S(2)}) async-start(), calls=%async_computation.4 | async-start | bytes 32440320 | tf_op jit(solution)/shard_map/all_gather | solution.py:103
  9.6 319.4 %reduce-scatter.7.cloned.1.call-start = ((), (), s32[]{:S(2)}) async-start(), calls=%async_computation.5 | async-start | bytes 1081344
  157.0 19.2 %slice-start.6 = ((s8[11796480]{0:T(1024)(128)(4,1)}), s8[3407872]{0:T(1024)(128)(4,1)S(1)}, s32[]{:S(2)}) async-start(s8[11796480]{0:T(1024)(128)(4,1)} %bitcast.202), calls=%async_computation.13 | async-start | bytes 6815744
  162.7 13.5 %slice-start.7 = ((s8[11796480]{0:T(1024)(128)(4,1)}), s8[4194304]{0:T(1024)(128)(4,1)S(1)}, s32[]{:S(2)}) async-start(s8[11796480]{0:T(1024)(128)(4,1)} %bitcast.202), calls=%async_computation.14 | async-start | bytes 8388608
  167.2 9.0 %slice-start.8 = ((s8[11796480]{0:T(1024)(128)(4,1)}), s8[4194304]{0:T(1024)(128)(4,1)S(1)}, s32[]{:S(2)}) async-start(s8[11796480]{0:T(1024)(128)(4,1)} %bitcast.202), calls=%async_computation.15 | async-start | bytes 8388608
  167.2 10.8 %slice-start = ((s8[11796480]{0:T(1024)(128)(4,1)}), s8[4194304]{0:T(1024)(128)(4,1)S(1)}, s32[]{:S(2)}) async-start(s8[11796480]{0:T(1024)(128)(4,1)} %bitcast.198), calls=%async_computation.7 | async-start | bytes 8388608
  171.7 6.3 slice-start.1
  176.2 2.9 copy-start.3
  176.3 2.1 slice-start.2
  179.2 1.8 copy-start.7
  180.1 1.8 copy-start.4
  212.9 118.6 %copy-start.5 = (f32[2,16,4,64]{3,2,1,0:T(4,128)S(1)}, f32[2,16,4,64]{3,2,1,0:T(4,128)}, u32[]{:S(2)}) copy-start(f32[2,16,4,64]{3,2,1,0:T(4,128)} %param.11) | copy-start | bytes 98308
  252.1 381.1 %reduce-scatter.9.cloned.1.call-start = ((), (), s32[]{:S(2)}) async-start(), calls=%async_computation.6 | async-start | bytes 4055040
  426.4 20.2 %slice-start.3 = ((s8[11796480]{0:T(1024)(128)(4,1)}), s8[3407872]{0:T(1024)(128)(4,1)S(1)}, s32[]{:S(2)}) async-start(s8[11796480]{0:T(1024)(128)(4,1)} %bitcast.200), calls=%async_computation.10 | async-start | bytes 6815744
  435.8 10.8 %slice-start.4 = ((s8[11796480]{0:T(1024)(128)(4,1)}), s8[4194304]{0:T(1024)(128)(4,1)S(1)}, s32[]{:S(2)}) async-start(s8[11796480]{0:T(1024)(128)(4,1)} %bitcast.200), calls=%async_computation.11 | async-start | bytes 8388608
  437.8 8.9 %slice-start.5 = ((s8[11796480]{0:T(1024)(128)(4,1)}), s8[4194304]{0:T(1024)(128)(4,1)S(1)}, s32[]{:S(2)}) async-start(s8[11796480]{0:T(1024)(128)(4,1)} %bitcast.200), calls=%async_computation.12 | async-start | bytes 8388608
  446.6 7.8 %slice-start.9 = ((s8[11796480]{0:T(1024)(128)(4,1)}), s8[4194304]{0:T(1024)(128)(4,1)S(1)}, s32[]{:S(2)}) async-start(s8[11796480]{0:T(1024)(128)(4,1)} %bitcast.204), calls=%async_computation.16 | async-start | bytes 8388608
  446.7 7.8 %slice-start.10 = ((s8[11796480]{0:T(1024)(128)(4,1)}), s8[4194304]{0:T(1024)(128)(4,1)S(1)}, s32[]{:S(2)}) async-start(s8[11796480]{0:T(1024)(128)(4,1)} %bitcast.204), calls=%async_computation.17 | async-start | bytes 8388608
  452.8 2.0 slice-start.11
  456.5 7.8 %copy-start.2 = (bf16[16,4,15,48]{3,1,2,0:T(4,128)(2,1)S(1)}, bf16[16,4,15,48]{3,1,2,0:T(4,128)(2,1)}, u32[]{:S(2)}) copy-start(bf16[16,4,15,48]{3,1,2,0:T(4,128)(2,1)} %copy-done.1) | copy-start | bytes 276484
  553.7 82.7 %copy-start = (f32[2,16,4,480]{3,2,1,0:T(4,128)S(1)}, f32[2,16,4,480]{3,2,1,0:T(4,128)}, u32[]{:S(2)}) copy-start(f32[2,16,4,480]{3,2,1,0:T(4,128)} %param.12) | copy-start | bytes 737284
  553.7 148.9 %copy-start.6 = (f32[2,16,4,480]{3,2,1,0:T(4,128)S(1)}, f32[2,16,4,480]{3,2,1,0:T(4,128)}, u32[]{:S(2)}) copy-start(f32[2,16,4,480]{3,2,1,0:T(4,128)} %param.13) | copy-start | bytes 737284
  706.0 10.1 %all-to-all-start = ((f32[4,1,15360]{2,1,0:T(1,128)}), f32[4,1,15360]{2,1,0:T(1,128)S(1)}, u32[]{:S(2)}, u32[]{:S(2)}) async-start(f32[4,1,15360]{2,1,0:T(1,128)} %reshape.123), calls=%async_computation | async-start | bytes 491520 | tf_op jit(solution)/shard_map/all_to_all | solution.py:136
  727.7 10.1 %all-to-all-start.1 = ((f32[2,64,4,120]{3,2,0,1:T(4,128)}), f32[2,64,4,120]{3,2,0,1:T(4,128)S(1)}, u32[]{:S(2)}, u32[]{:S(2)}) async-start(f32[2,64,4,120]{3,2,0,1:T(4,128)} %copy.104), calls=%async_computation.1 | async-start | bytes 524288 | tf_op jit(solution)/shard_map/all_to_all | solution.py:141
  (2 other events, 2.5 us)
Sparse Core Ops, SparseCore 0:
  10.3 110.6 all-gather.1
  252.2 76.7 reduce-scatter.6
  553.9 79.2 reduce-scatter.8
where the time goes:
time: 754 us; the launch traced here: 746 us
  waiting for transfers between devices  276 us (37%)
  local copies, waits for them, and re-layouts  220 us (29%)
  blocking collectives  158 us (21%)
  matrix products  54.1 us (7%)
  between operations  16.4 us (2%)
  other arithmetic  14.6 us (2%)
    unnamed x5, waiting for transfers between devices  155 us
    unnamed x54, local copies, waits for them, and re-layouts  154 us
    all_gather x1, waiting for transfers between devices, on_device(): lax.all_gather(direction.astype(jnp.bfloat16), 'tile', axis=3, tiled=True)  109 us
    psum x1, blocking collectives, on_device(): lax.psum(jnp.sum(u_raw * u_raw), ('freq', 'tile')) / left_count + eps  65 us
    psum x1, blocking collectives, direction_scale(): total = lax.psum(jnp.sum(v_raw * v_raw), ('freq', 'tile'))  64.8 us
    reshape x1, local copies, waits for them, and re-layouts, on_device(): collected_rows.reshape(2, frequency_group, virtual_source, RECEIVER_BLOCK...  36 us
    all_gather x1, blocking collectives, on_device(): lax.all_gather(u_next.astype(jnp.bfloat16), 'tile', axis=3, tiled=True)  27.9 us
  transfers between devices with their start and end apart: 5, of which 5 were waited for; matrix products, arithmetic and copies ran while one was open for 1% of the time, Pallas kernels for 0%

commit v1 on v0

v1 whole, which is shorter than its diff:
```python
import math

import jax
import jax.numpy as jnp
import ml_dtypes
import numpy as np
from jax import lax
from jax.experimental import pallas as pl
from jax.experimental.pallas import tpu as pltpu
from jax.sharding import PartitionSpec as P

WINDOW_FREQS = 64
NT = 512
FLO = 8
TILE_EXTENT = 256
RMAX = 48
RECEIVER_BLOCKS = 60
NVS = 4
SLOTS = 8

shrink_level = 0.5
eps = 1e-06

F32 = jnp.float32
BF16 = jnp.bfloat16
VMEM = pltpu.VMEM
SMEM = pltpu.SMEM
LIMIT = 50 * 1024 * 1024


def iota(shape, axis):
    return lax.broadcasted_iota(jnp.int32, shape, axis)


def low_rows():
    return iota((8, 128), 0) < 4


def swap(x):
    return pltpu.roll(x, 4, 0)


def call(body, outs, ins, scratch=(), out_spaces=None, **kw):
    out_spaces = out_spaces or [VMEM] * len(outs)
    return pl.pallas_call(
        body,
        out_shape=outs,
        in_specs=[pl.BlockSpec(memory_space=s) for s in ins],
        out_specs=[pl.BlockSpec(memory_space=s) for s in out_spaces],
        scratch_shapes=list(scratch),
        compiler_params=pltpu.CompilerParams(vmem_limit_bytes=LIMIT),
        **kw,
    )


def pack_body(rb, direction, data, out, slot_of, mark, ids):
    def clear(b, _):
        mark[b] = -1
        return 0

    lax.fori_loop(0, 64, clear, 0)
    for m in range(SLOTS):
        ids[m] = 0
    count = jnp.int32(0)
    for t in range(rb.shape[0]):
        b = rb[t]
        seen = mark[b]
        slot = jnp.minimum(jnp.where(seen < 0, count, seen), SLOTS - 1)
        mark[b] = slot
        ids[slot] = b
        slot_of[t] = slot
        count = count + jnp.where(seen < 0, 1, 0)
    lane = iota((4, 128), 1)
    listed = jnp.zeros((4, 128), F32)
    for m in range(SLOTS):
        listed = jnp.where(lane == 64 + m, ids[m].astype(F32), listed)
    for f in range(direction.shape[1]):
        for c in range(2):
            k = 2 * f + c
            out[k, :, 0:480] = direction[c, f]
            out[k, :, 512:640] = listed
            out[k, :, 512:576] = data[c, f]


def split_model_body(model, out):
    for f in range(model.shape[1]):
        both = jnp.concatenate([model[0, f], model[1, f]], axis=0)
        both = jnp.concatenate([both, jnp.zeros((8, 32), F32)], axis=1)
        for g in range(4):
            part = pltpu.roll(both, 512 - 120 * g, 1) if g else both
            part = part[:, 0:128]
            out[g, 2 * f] = part[0:4]
            out[g, 2 * f + 1] = part[4:8]


def blocks_of(chunks, half):
    low = low_rows()
    blocks = [None] * (2 * half)
    for b in range(half):
        even, odd = chunks[2 * b], chunks[2 * b + 1]
        blocks[b] = jnp.where(low, even, swap(odd))
        blocks[b + half] = jnp.where(low, swap(even), odd)
    return blocks


def spread_body(ids, rows, out, direction, data):
    lane = iota((8, 640), 1)
    chunks = [None] * 60
    tails = []
    for j in range(16):
        both = jnp.concatenate([rows[j], rows[j + 16]], axis=0)
        tails.append(both[:, 512:640])
        shift, first = 480 * j % 128, 480 * j // 128
        moved = jnp.where(lane < 480, both, 0.0)
        if shift:
            moved = pltpu.roll(moved, shift, 1)
        for q in range((shift + 479) // 128 + 1):
            piece = moved[:, 128 * q : 128 * q + 128]
            n = first + q
            chunks[n] = piece if chunks[n] is None else chunks[n] + piece
    for b, block in enumerate(blocks_of(chunks, 30)):
        direction[b] = block
    left = iota((8, 128), 1) < 64
    ends = [jnp.where(left, tails[2 * n], pltpu.roll(tails[2 * n + 1], 64, 1)) for n in range(8)]
    for b, block in enumerate(blocks_of(ends, 4)):
        data[b] = block

    def one(i, _):
        picked = [direction[ids[i, m]] for m in range(SLOTS)]
        out[i] = jnp.concatenate(picked, axis=0).astype(BF16)
        return 0

    lax.fori_loop(0, 32, one, 0, unroll=4)


def tiles_body(slot_in, slot_out, ranks, x, first, second, out, xs, acc):
    f = pl.program_id(0)
    low = low_rows()
    xr = x[0, 0:64].astype(F32)
    xi = x[1, 0:64].astype(F32)
    for m in range(SLOTS):
        tr = xr[8 * m : 8 * m + 8]
        ti = xi[8 * m : 8 * m + 8]
        tr4, ti4 = swap(tr), swap(ti)
        top = jnp.concatenate(
            [
                jnp.where(low, tr, ti4),
                jnp.where(low, tr4, ti),
                jnp.where(low, ti, -tr4),
                jnp.where(low, ti4, -tr),
            ],
            axis=1,
        )
        bottom = jnp.concatenate(
            [
                jnp.where(low, -ti, tr4),
                jnp.where(low, -ti4, tr),
                jnp.where(low, tr, ti4),
                jnp.where(low, tr4, ti),
            ],
            axis=1,
        )
        xs[m] = jnp.concatenate([top, bottom], axis=0).astype(BF16)
    acc[...] = jnp.zeros_like(acc)
    tiles = first.shape[1]
    lane = iota((16, RMAX), 1)
    for t in range(tiles):
        both = jnp.concatenate([first[0, t, 0], first[0, t, 1]], axis=1)
        z = lax.dot_general(
            xs[slot_in[t]], both, (((1,), (1,)), ((), ())), preferred_element_type=F32
        )
        z = jnp.where(lane < ranks[f, t], z, 0.0).astype(BF16)
        c = jnp.dot(z[0:8], second[0, t, 0], preferred_element_type=F32) + jnp.dot(
            z[8:16], second[0, t, 1], preferred_element_type=F32
        )
        at = slot_out[t]
        acc[at] = acc[at] + c
    for p in range(SLOTS // 2):
        real, imag = [], []
        for m in (2 * p, 2 * p + 1):
            left, right = acc[m, :, 0:128], acc[m, :, 128:256]
            real.append(jnp.where(low, left, swap(right)))
            imag.append(jnp.where(low, swap(left), right))
        out[0, 16 * p : 16 * p + 16] = jnp.concatenate(real, axis=0).astype(out.dtype)
        out[1, 16 * p : 16 * p + 16] = jnp.concatenate(imag, axis=0).astype(out.dtype)


def tile_products(slot_in, slot_out, ranks, x, first, second):
    freqs, tiles = first.shape[0], first.shape[1]
    factor = pl.BlockSpec((1, tiles, 2, RMAX, TILE_EXTENT), lambda f: (f, 0, 0, 0, 0))
    smem = pl.BlockSpec(memory_space=SMEM)
    return pl.pallas_call(
        tiles_body,
        grid=(freqs,),
        out_shape=jax.ShapeDtypeStruct((2 * freqs, 64, 128), BF16),
        in_specs=[
            smem,
            smem,
            smem,
            pl.BlockSpec((2, x.shape[1], 128), lambda f: (f, 0, 0)),
            factor,
            factor,
        ],
        out_specs=pl.BlockSpec((2, 64, 128), lambda f: (f, 0, 0)),
        scratch_shapes=[VMEM((SLOTS, 16, 512), BF16), VMEM((SLOTS, 8, 256), F32)],
        compiler_params=pltpu.CompilerParams(vmem_limit_bytes=LIMIT),
    )(slot_in, slot_out, ranks, x, first, second)


def residual_body(alpha, parts, data, out):
    total = parts[0].astype(F32)
    for i in range(1, 32):
        total = total + parts[i].astype(F32)
    u = total - alpha[0] * data[...].reshape(64, 128)
    square = u * u
    power = jnp.sum(jnp.sum(square, axis=0, keepdims=True), axis=1, keepdims=True)
    power = jnp.broadcast_to(power, (8, 128))
    s1 = power.astype(BF16).astype(F32)
    s2 = (power - s1).astype(BF16).astype(F32)
    s3 = power - s1 - s2
    row = iota((8, 128), 0)
    sums = jnp.where(row == 0, s1, jnp.where(row == 1, s2, jnp.where(row == 2, s3, 0.0)))
    ub = u.astype(BF16)
    high = ub.astype(F32)
    rest = u - high
    low = low_rows()
    for i in range(32):
        out[i, 0:64] = ub
    for b in range(8):
        hb, rb = high[8 * b : 8 * b + 8], rest[8 * b : 8 * b + 8]
        even = jnp.concatenate([jnp.where(low, hb, swap(rb)), sums], axis=0).astype(BF16)
        odd = jnp.concatenate([jnp.where(low, swap(hb), rb), sums], axis=0).astype(BF16)
        for n, tail in ((2 * b, even), (2 * b + 1, odd)):
            out[2 * n, 64:80] = tail
            out[2 * n + 1, 64:80] = tail


def update_body(ids, beta, parts, direction, out, acc):
    acc[...] = jnp.zeros_like(acc)

    def one(i, _):
        part = parts[i].astype(F32)
        for m in range(SLOTS):
            b = ids[i, m]
            acc[b] = acc[b] + part[8 * m : 8 * m + 8]
        return 0

    lax.fori_loop(0, 32, one, 0, unroll=2)
    low = low_rows()
    lane = iota((8, 128), 1)
    inverse, scale = beta[1], beta[0]
    chunks = [None] * 60
    power = jnp.zeros((8, 128), F32)
    for b in range(30):
        head = acc[b] * inverse - scale * direction[b]
        tail = acc[b + 30] * inverse - scale * direction[b + 30]
        power = power + head * head + tail * tail
        chunks[2 * b] = jnp.where(low, head, swap(tail))
        chunks[2 * b + 1] = jnp.where(low, swap(head), tail)
    power = jnp.sum(jnp.sum(power, axis=0, keepdims=True), axis=1, keepdims=True)
    power = jnp.broadcast_to(power, (8, 128))
    for d in range(64):
        n, off = 120 * d // 128, 120 * d % 128
        value = chunks[n]
        if off:
            value = pltpu.roll(value, 128 - off, 1)
        if off > 8:
            value = jnp.where(lane < 128 - off, value, pltpu.roll(chunks[n + 1], 128 - off, 1))
        value = jnp.where(lane == 120, power, value)
        j, g = d // 4, d % 4
        out[32 * g + j] = value[0:4]
        out[32 * g + j + 16] = value[4:8]


def split_dot(a_high, a_low, b):
    b_high = b.astype(BF16)
    b_low = (b - b_high.astype(F32)).astype(BF16)
    return (
        jnp.dot(a_high, b_high, preferred_element_type=F32)
        + jnp.dot(a_high, b_low, preferred_element_type=F32)
        + jnp.dot(a_low, b_high, preferred_element_type=F32)
    )


def shrink_body(raw, model, lo, hi, fh, fl, bh, bl, out):
    lane = iota((128, 128), 1)
    count = 2 * WINDOW_FREQS * NVS * RECEIVER_BLOCKS * TILE_EXTENT
    sums = jnp.where(lane == 120, raw[:, 0, :], 0.0)
    power = jnp.sum(jnp.sum(sums, axis=0, keepdims=True), axis=1, keepdims=True)
    alpha = jnp.sqrt(power / count + eps)
    moment = iota((NT, 128), 0)
    inside = (moment >= lo[...]) & (moment < hi[...])
    for v in range(NVS):
        step = raw[:, v, :] / alpha
        out[:, v, :] = step
        signal = split_dot(fh[...], fl[...], model[:, v, :] + step)
        kept = signal - jnp.clip(signal, -shrink_level, shrink_level)
        kept = jnp.where(inside, kept, 0.0)
        out[:, NVS + v, :] = split_dot(bh[...], bl[...], kept)


def finish_body(place, beta, back, tails, u_next, v_next, m_next):
    lane = iota((8, 128), 1)
    inverse = beta[1]
    odd = place[0] == 1
    for k in range(32):
        f, c = k // 2, k % 2
        quarter = [back[g, k] for g in range(4)]
        for q in range(4):
            value = quarter[q]
            if q:
                value = pltpu.roll(value, 128 - 8 * q, 1)
            if q < 3:
                value = jnp.where(
                    lane < 120 - 8 * q, value, pltpu.roll(quarter[q + 1], 120 - 8 * q, 1)
                )
            width = 128 if q < 3 else 96
            v_next[c, f, :, 128 * q : 128 * q + width] = value[0:4, 0:width]
            m_next[c, f, :, 128 * q : 128 * q + width] = value[4:8, 0:width]
        part = tails[k, 64:80].astype(F32)[0:8]
        part = (part + swap(part)) * inverse
        part = jnp.where(odd, pltpu.roll(part, 64, 1), part)
        u_next[c, f] = part[0:4, 0:64]


def transform_tables():
    steps = np.arange(NT)
    bins = FLO + np.arange(WINDOW_FREQS)
    phase = (bins[None, :] * steps[:, None] % NT) * (2.0 * math.pi / NT)
    table = np.stack([np.cos(phase), -np.sin(phase)], axis=2).reshape(NT, 2 * WINDOW_FREQS)
    forward = (table / math.sqrt(WINDOW_FREQS)).astype(np.float32)
    backward = (table.T * (2.0 * math.sqrt(WINDOW_FREQS) / NT)).astype(np.float32)
    out = []
    for a in (forward, backward):
        high = a.astype(ml_dtypes.bfloat16)
        out += [high, (a - high.astype(np.float32)).astype(ml_dtypes.bfloat16)]
    return out


def on_device(
    data_vec,
    direction,
    model,
    alpha,
    u_factor,
    v_factor,
    ranks,
    tile_source_block,
    tile_receiver_block,
    time_lo,
    time_len,
):
    shape = jax.ShapeDtypeStruct
    both = ("freq", "tile")
    g = lax.axis_index("freq")
    place = lax.axis_index("tile")

    def exchange(x, axis):
        return lax.all_to_all(x, axis, split_axis=0, concat_axis=0, tiled=True)

    packed, slots = call(
        pack_body,
        [shape((32, 4, 640), F32), shape((15,), jnp.int32)],
        [SMEM, VMEM, VMEM],
        [SMEM((64,), jnp.int32), SMEM((SLOTS,), jnp.int32)],
        [VMEM, SMEM],
    )(tile_receiver_block, direction, data_vec)
    rows = exchange(packed, "tile")

    (model_parts,) = call(split_model_body, [shape((4, 32, 4, 128), F32)], [VMEM])(model)
    model_all = exchange(model_parts, "freq").reshape(128, 4, 128)

    ids = rows[:, 0, 576 : 576 + SLOTS].astype(jnp.int32)
    picked, direction_rows, data_rows = call(
        spread_body,
        [shape((32, 64, 128), BF16), shape((60, 8, 128), F32), shape((8, 8, 128), F32)],
        [SMEM, VMEM],
    )(ids, rows)
    x = exchange(picked, "tile")
    parts = tile_products(slots, tile_source_block, ranks, x, v_factor, u_factor)
    parts = exchange(parts, "tile")
    (residual,) = call(residual_body, [shape((32, 80, 128), BF16)], [SMEM, VMEM, VMEM])(
        alpha.reshape(1), parts, data_rows
    )
    u_all = exchange(residual, "tile")

    left_count = 2 * WINDOW_FREQS * NVS * data_vec.shape[3] * 32
    power = jnp.sum(u_all[:, 72:75, 0].astype(F32))
    mine = jnp.broadcast_to(power, (8, 128))
    others = [
        lax.ppermute(mine, "freq", [(i, (i + d) % 4) for i in range(4)])[0, 0] for d in (1, 2, 3)
    ]
    total = (power + others[1]) + (others[0] + others[2])
    beta = jnp.sqrt(total / left_count + eps)
    beta = jnp.stack([beta, 1.0 / beta])

    back = tile_products(tile_source_block, slots, ranks, u_all, u_factor, v_factor)
    back = exchange(back, "tile")
    (raw,) = call(
        update_body,
        [shape((128, 4, 128), F32)],
        [SMEM, SMEM, VMEM, VMEM],
        [VMEM((64, 8, 128), F32)],
    )(ids, beta, back, direction_rows)
    raw = exchange(raw, both)

    lo = lax.dynamic_slice_in_dim(time_lo, g * 120, 120, 0)
    hi = lo + lax.dynamic_slice_in_dim(time_len, g * 120, 120, 0)
    lo = jnp.pad(lo, (0, 8)).reshape(1, 128)
    hi = jnp.pad(hi, (0, 8)).reshape(1, 128)
    tables = [jnp.asarray(a) for a in transform_tables()]
    (shrunk,) = call(shrink_body, [shape((128, 8, 128), F32)], [VMEM] * 8)(
        raw, model_all, lo, hi, *tables
    )
    shrunk = exchange(shrunk, "freq").reshape(4, 32, 8, 128)
    return call(
        finish_body,
        [
            shape(data_vec.shape, F32),
            shape(direction.shape, F32),
            shape(direction.shape, F32),
        ],
        [SMEM, SMEM, VMEM, VMEM],
    )((place % 2).reshape(1), beta, shrunk, u_all)


def solution(mesh):
    vector = P(None, "freq", None, "tile")
    factor = P("freq", "tile", None, None, None)
    placed = (
        vector,
        vector,
        vector,
        P(),
        factor,
        factor,
        P("freq", "tile"),
        P("tile"),
        P("tile"),
        P("tile"),
        P("tile"),
    )
    return jax.shard_map(
        on_device,
        mesh=mesh,
        in_specs=placed,
        out_specs=(vector, vector, vector),
        check_vma=False,
    )
```

time: 754 us -> 224 us (0.30)
  waiting for transfers between devices: 276 us -> 40.5 us
  local copies, waits for them, and re-layouts: 220 us -> 6.1 us
  blocking collectives: 158 us -> 47.8 us
  Pallas kernels: 0 us -> 92.6 us
  matrix products: 54.1 us -> 0 us
  starting transfers between devices: 7.1 us -> 30.1 us
  other arithmetic: 14.6 us -> 1.49 us
  between operations: 16.4 us -> 4.14 us
    unnamed x5 -> x0, waiting for transfers between devices: 155 us -> none
    unnamed x54 -> x24, local copies, waits for them, and re-layouts: 154 us -> 3.82 us
    psum x2 -> x0, blocking collectives: 130 us -> none  [the longest x1 65 us: on_device(): lax.psum(jnp.sum(u_raw * u_raw), ('freq', 'tile')) / left_count + eps]
    all_gather x1 -> x0, waiting for transfers between devices: 109 us -> none  [on_device(): lax.all_gather(direction.astype(jnp.bfloat16), 'tile', axis=3, tiled=True)]
    pallas_call x0 -> x9, Pallas kernels: none -> 92.6 us  [the longest x2 81.7 us: tile_products(): pl.pallas_call(tiles_body, grid=(freqs,), out_shape=jax.ShapeDtypeStruct(...]
    dot_general x24 -> x0, matrix products: 54.1 us -> none  [the longest x2 8.96 us: tile_apply(): jnp.einsum('ftrk,fvtk->fvtr', fi, tile_pieces[1], preferred_element_type=...]
    all_to_all x0 -> x3, blocking collectives: none -> 47.8 us  [exchange(): return lax.all_to_all(x, axis, split_axis=0, concat_axis=0, tiled=True)]
    reshape x2 -> x1, local copies, waits for them, and re-layouts: 42.7 us -> 0.01 us  [on_device(): hi = jnp.pad(hi, (0, 8)).reshape(1, 128)]
  transfers between devices with their start and end apart: 5 -> 8, of which waited for: 5 -> 4; matrix products, arithmetic and copies ran while one was open for 1% -> 2% of each run, Pallas kernels for 0% -> 2%
where the time goes in v1:
time: 224 us; the launch traced here: 223 us
  Pallas kernels  92.6 us (41%)
  blocking collectives  47.8 us (21%)
  waiting for transfers between devices  40.5 us (18%)
  starting transfers between devices  30.1 us (13%)
  local copies, waits for them, and re-layouts  6.1 us (3%)
  between operations  4.14 us (2%)
    pallas_call x2, Pallas kernels, tile_products(): pl.pallas_call(tiles_body, grid=(freqs,), out_shape=jax.ShapeDtypeStruct(...  81.7 us
    all_to_all x3, blocking collectives, exchange(): return lax.all_to_all(x, axis, split_axis=0, concat_axis=0, tiled=True)  47.8 us
    all_to_all x5, waiting for transfers between devices, exchange(): return lax.all_to_all(x, axis, split_axis=0, concat_axis=0, tiled=True)  40.5 us
    all_to_all x5, starting transfers between devices, exchange(): return lax.all_to_all(x, axis, split_axis=0, concat_axis=0, tiled=True)  23.2 us
    ppermute x3, starting transfers between devices, on_device(): lax.ppermute(mine, 'freq', [(i, (i + d) % 4) for i in range(4)])[0, 0]  6.84 us
  transfers between devices with their start and end apart: 8, of which 4 were waited for; matrix products, arithmetic and copies ran while one was open for 2% of the time, Pallas kernels for 2%

profile of v1, /device:TPU:0, one launch (start us, length us, event | category | flops | bytes accessed | tf_op | source)
XLA Modules:
  0.0 222.7 jit_solution(4278759332743406460)
XLA Ops:
  0.6 0.9 copy-done
  1.6 0.8 copy-done.6
  3.1 1.7 shard_map.166
  4.7 16.6 %all_to_all.40.rows = f32[32,4,640]{2,1,0:T(4,128)S(1)} all-to-all(f32[32,4,640]{2,1,0:T(4,128)S(1)} %get-tuple-element.9), channel_id=1, replica_groups=mesh['freq'=4,'tile'=32] {'tile'}, dimensions={0} | all-to-all | bytes 655360 | tf_op jit(solution)/shard_map/all_to_all | solution.py:359
  21.5 1.2 shard_map.167
  22.7 14.8 %all_to_all.41.x = bf16[32,64,128]{2,1,0:T(8,128)(2,1)S(1)} all-to-all(bf16[32,64,128]{2,1,0:T(8,128)(2,1)S(1)} %get-tuple-element.10), channel_id=1, replica_groups=mesh['freq'=4,'tile'=32] {'tile'}, dimensions={0} | all-to-all | bytes 1048576 | tf_op jit(solution)/shard_map/all_to_all | solution.py:359
  38.9 40.8 %shard_map.168 = bf16[32,64,128]{2,1,0:T(8,128)(2,1)} custom-call(s32[15]{0:T(128)S(1)} %get-tuple-element.8.slot_in.slot_out, s32[15]{0:T(128)S(1)} %copy-done.9, s32[16,15]{1,0:T(8,128)S(1)} %copy-done.7, bf16[32,64,128]{2,1,0:T(8,128)(2,1)S(1)} %all_to_all.41.x, bf16[16,15,2,48,256]{4,3,2,1,0:T(8,128)(2,1)} %second.3, bf16[16,15,2,48,256]{4,3,2,1,0:T(8,128)(2,1)} %first.3), custom_call_target="tpu_custom_call" | custom-call | tf_op jit(solution)/shard_map/pallas_call | solution.py:192
  79.7 4.1 %all-to-all-start.2 = ((bf16[32,64,128]{2,1,0:T(8,128)(2,1)}), bf16[32,64,128]{2,1,0:T(8,128)(2,1)S(1)}, u32[]{:S(2)}, u32[]{:S(2)}) async-start(bf16[32,64,128]{2,1,0:T(8,128)(2,1)} %shard_map.168), calls=%async_computation.2 | async-start | bytes 1048576 | tf_op jit(solution)/shard_map/all_to_all | solution.py:359
  84.5 10.5 %all-to-all-done.2.parts = bf16[32,64,128]{2,1,0:T(8,128)(2,1)S(1)} async-done(((bf16[32,64,128]{2,1,0:T(8,128)(2,1)}), bf16[32,64,128]{2,1,0:T(8,128)(2,1)S(1)}, u32[]{:S(2)}, u32[]{:S(2)}) %all-to-all-start.2) | async-done | bytes 524320 | tf_op jit(solution)/shard_map/all_to_all | solution.py:359
  95.2 16.4 %all_to_all.42.x.tails = bf16[32,80,128]{2,1,0:T(8,128)(2,1)S(1)} all-to-all(bf16[32,80,128]{2,1,0:T(8,128)(2,1)S(1)} %shard_map.169), channel_id=1, replica_groups=mesh['freq'=4,'tile'=32] {'tile'}, dimensions={0} | all-to-all | bytes 1310720 | tf_op jit(solution)/shard_map/all_to_all | solution.py:359
  111.6 40.9 %shard_map.170 = bf16[32,64,128]{2,1,0:T(8,128)(2,1)} custom-call(s32[15]{0:T(128)S(1)} %copy-done.10, s32[15]{0:T(128)S(1)} %get-tuple-element.8.slot_in.slot_out, s32[16,15]{1,0:T(8,128)S(1)} %copy-done.8, bf16[32,80,128]{2,1,0:T(8,128)(2,1)S(1)} %all_to_all.42.x.tails, bf16[16,15,2,48,256]{4,3,2,1,0:T(8,128)(2,1)} %first.3, ...), custom_call_target="tpu_custom_call" | custom-call | tf_op jit(solution)/shard_map/pallas_call | solution.py:192
  152.5 4.2 %all-to-all-start.4 = ((bf16[32,64,128]{2,1,0:T(8,128)(2,1)}), bf16[32,64,128]{2,1,0:T(8,128)(2,1)S(1)}, u32[]{:S(2)}, u32[]{:S(2)}) async-start(bf16[32,64,128]{2,1,0:T(8,128)(2,1)} %shard_map.170), calls=%async_computation.4 | async-start | bytes 1048576 | tf_op jit(solution)/shard_map/all_to_all | solution.py:359
  156.7 0.9 shard_map.172
  157.6 10.3 %all-to-all-done.4.parts = bf16[32,64,128]{2,1,0:T(8,128)(2,1)S(1)} async-done(((bf16[32,64,128]{2,1,0:T(8,128)(2,1)}), bf16[32,64,128]{2,1,0:T(8,128)(2,1)S(1)}, u32[]{:S(2)}, u32[]{:S(2)}) %all-to-all-start.4) | async-done | bytes 524320 | tf_op jit(solution)/shard_map/all_to_all | solution.py:359
  167.9 5.3 %all-to-all-start.6 = ((f32[4,32,4,128]{3,2,1,0:T(4,128)}), f32[4,32,4,128]{3,2,1,0:T(4,128)S(1)}, u32[]{:S(2)}, u32[]{:S(2)}) async-start(f32[4,32,4,128]{3,2,1,0:T(4,128)} %shard_map.172), calls=%async_computation.6 | async-start | bytes 524288 | tf_op jit(solution)/shard_map/all_to_all | solution.py:359
  174.5 3.6 %collective-permute-start = (f32[8,128]{1,0:T(8,128)S(1)}, f32[8,128]{1,0:T(8,128)S(1)}, u32[]{:S(2)}, u32[]{:S(2)}) collective-permute-start(f32[8,128]{1,0:T(8,128)S(1)} %broadcast_in_dim.3), channel_id=1, source_target_pairs={{0,64},{32,96},{64,0},{96,32},{1,65},{33,97},{65,1},{97,33},{2,66}... | collective-permute-start | bytes 12296 | tf_op jit(solution)/shard_map/ppermute | solution.py:391
  178.6 2.7 %collective-permute-start.2 = (f32[8,128]{1,0:T(8,128)S(1)}, f32[8,128]{1,0:T(8,128)S(1)}, u32[]{:S(2)}, u32[]{:S(2)}) collective-permute-start(f32[8,128]{1,0:T(8,128)S(1)} %broadcast_in_dim.3), channel_id=1, source_target_pairs={{0,96},{32,0},{64,32},{96,64},{1,97},{33,1},{65,33},{97,65},{2,98}... | collective-permute-start | bytes 12296 | tf_op jit(solution)/shard_map/ppermute | solution.py:391
  185.6 2.7 %shard_map.171 = f32[128,4,128]{2,1,0:T(4,128)} custom-call(s32[32,8]{1,0:T(8,128)S(1)} %convert_bitcast_fusion.ids, f32[2]{0:T(128)S(1)} %pad_maximum_fusion.beta, bf16[32,64,128]{2,1,0:T(8,128)(2,1)S(1)} %all-to-all-done.4.parts, f32[60,8,128]{2,1,0:T(8,128)S(1)} %get-tuple-element.12.direction), custom_call_target="tpu_custom_call" | custom-call | tf_op jit(solution)/shard_map/pallas_call | solution.py:399
  188.3 6.2 %all-to-all-start.5 = ((f32[128,4,128]{2,1,0:T(4,128)}), f32[128,4,128]{2,1,0:T(4,128)S(1)}, u32[]{:S(2)}, u32[]{:S(2)}) async-start(f32[128,4,128]{2,1,0:T(4,128)} %shard_map.171), calls=%async_computation.5 | async-start | bytes 524288 | tf_op jit(solution)/shard_map/all_to_all | solution.py:359
  195.3 9.9 %all-to-all-done.5.raw = f32[128,4,128]{2,1,0:T(4,128)S(1)} async-done(((f32[128,4,128]{2,1,0:T(4,128)}), f32[128,4,128]{2,1,0:T(4,128)S(1)}, u32[]{:S(2)}, u32[]{:S(2)}) %all-to-all-start.5) | async-done | bytes 262176 | tf_op jit(solution)/shard_map/all_to_all | solution.py:359
  205.3 2.7 %shard_map.173 = f32[128,8,128]{2,1,0:T(8,128)} custom-call(f32[128,4,128]{2,1,0:T(4,128)S(1)} %all-to-all-done.5.raw, f32[128,4,128]{2,1,0:T(4,128)S(1)} %bitcast.17, s32[1,128]{1,0:T(1,128)S(1)} %get-tuple-element.16.lo, s32[1,128]{1,0:T(1,128)S(1)} %get-tuple-element.15.hi, bf16[512,128]{1,0:T(8,128)(2,1)S(1)} %copy-done.2, ...), custom_call_target="tpu_custom_call" | custom-call | tf_op jit(solution)/shard_map/pallas_call | solution.py:412
  208.0 3.5 %all-to-all-start.7 = ((f32[128,8,128]{2,1,0:T(8,128)}), f32[128,8,128]{2,1,0:T(8,128)S(1)}, u32[]{:S(2)}, u32[]{:S(2)}) async-start(f32[128,8,128]{2,1,0:T(8,128)} %shard_map.173), calls=%async_computation.7 | async-start | bytes 1048576 | tf_op jit(solution)/shard_map/all_to_all | solution.py:359
  211.5 9.7 %all-to-all-done.7 = f32[128,8,128]{2,1,0:T(8,128)S(1)} async-done(((f32[128,8,128]{2,1,0:T(8,128)}), f32[128,8,128]{2,1,0:T(8,128)S(1)}, u32[]{:S(2)}, u32[]{:S(2)}) %all-to-all-start.7) | async-done | bytes 524320 | tf_op jit(solution)/shard_map/all_to_all | solution.py:359
  221.2 1.5 shard_map.174
  (38 shorter events, 6.6 us)
Async XLA Ops:
  0.6 1.0 copy-start
  1.6 0.8 copy-start.6
  2.4 0.7 copy-start.11
  37.5 0.7 copy-start.7
  38.2 0.7 copy-start.9
  38.9 72.7 %copy-start.8 = (s32[16,15]{1,0:T(8,128)S(1)}, s32[16,15]{1,0:T(8,128)}, u32[]{:S(2)}) copy-start(s32[16,15]{1,0:T(8,128)} %ranks.3) | copy-start | bytes 2884
  38.9 72.7 %copy-start.10 = (s32[15]{0:T(128)S(1)}, s32[15]{0:T(128)}, u32[]{:S(2)}) copy-start(s32[15]{0:T(128)} %slot_in.1) | copy-start | bytes 184
  79.7 15.3 %all-to-all-start.2 = ((bf16[32,64,128]{2,1,0:T(8,128)(2,1)}), bf16[32,64,128]{2,1,0:T(8,128)(2,1)S(1)}, u32[]{:S(2)}, u32[]{:S(2)}) async-start(bf16[32,64,128]{2,1,0:T(8,128)(2,1)} %shard_map.168), calls=%async_computation.2 | async-start | bytes 1048576 | tf_op jit(solution)/shard_map/all_to_all | solution.py:359
  111.6 45.1 %copy-start.1 = (f32[2,16,4,480]{3,2,1,0:T(4,128)S(1)}, f32[2,16,4,480]{3,2,1,0:T(4,128)}, u32[]{:S(2)}) copy-start(f32[2,16,4,480]{3,2,1,0:T(4,128)} %model.1) | copy-start | bytes 737284
  111.6 93.7 %copy-start.2 = (bf16[512,128]{1,0:T(8,128)(2,1)S(1)}, bf16[512,128]{1,0:T(8,128)(2,1)}, u32[]{:S(2)}) copy-start(bf16[512,128]{1,0:T(8,128)(2,1)} %constant.44.clone.fh) | copy-start | bytes 393220
  111.6 93.7 %copy-start.3 = (bf16[512,128]{1,0:T(8,128)(2,1)S(1)}, bf16[512,128]{1,0:T(8,128)(2,1)}, u32[]{:S(2)}) copy-start(bf16[512,128]{1,0:T(8,128)(2,1)} %constant.45.clone.fl) | copy-start | bytes 393220
  111.6 93.7 %copy-start.4 = (bf16[128,512]{1,0:T(8,128)(2,1)S(1)}, bf16[128,512]{1,0:T(8,128)(2,1)}, u32[]{:S(2)}) copy-start(bf16[128,512]{1,0:T(8,128)(2,1)} %constant.46.clone.bh) | copy-start | bytes 393220
  111.6 93.7 %copy-start.5 = (bf16[128,512]{1,0:T(8,128)(2,1)S(1)}, bf16[128,512]{1,0:T(8,128)(2,1)}, u32[]{:S(2)}) copy-start(bf16[128,512]{1,0:T(8,128)(2,1)} %constant.47.clone.bl) | copy-start | bytes 393220
  152.5 15.3 %all-to-all-start.4 = ((bf16[32,64,128]{2,1,0:T(8,128)(2,1)}), bf16[32,64,128]{2,1,0:T(8,128)(2,1)S(1)}, u32[]{:S(2)}, u32[]{:S(2)}) async-start(bf16[32,64,128]{2,1,0:T(8,128)(2,1)} %shard_map.170), calls=%async_computation.4 | async-start | bytes 1048576 | tf_op jit(solution)/shard_map/all_to_all | solution.py:359
  167.9 20.4 %all-to-all-start.6 = ((f32[4,32,4,128]{3,2,1,0:T(4,128)}), f32[4,32,4,128]{3,2,1,0:T(4,128)S(1)}, u32[]{:S(2)}, u32[]{:S(2)}) async-start(f32[4,32,4,128]{3,2,1,0:T(4,128)} %shard_map.172), calls=%async_computation.6 | async-start | bytes 524288 | tf_op jit(solution)/shard_map/all_to_all | solution.py:359
  174.5 6.8 %collective-permute-start = (f32[8,128]{1,0:T(8,128)S(1)}, f32[8,128]{1,0:T(8,128)S(1)}, u32[]{:S(2)}, u32[]{:S(2)}) collective-permute-start(f32[8,128]{1,0:T(8,128)S(1)} %broadcast_in_dim.3), channel_id=1, source_target_pairs={{0,64},{32,96},{64,0},{96,32},{1,65},{33,97},{65,1},{97,33},{2,66}... | collective-permute-start | bytes 12296 | tf_op jit(solution)/shard_map/ppermute | solution.py:391
  178.1 5.1 %collective-permute-start.1 = (f32[8,128]{1,0:T(8,128)S(1)}, f32[8,128]{1,0:T(8,128)S(1)}, u32[]{:S(2)}, u32[]{:S(2)}) collective-permute-start(f32[8,128]{1,0:T(8,128)S(1)} %broadcast_in_dim.3), channel_id=1, source_target_pairs={{0,32},{32,64},{64,96},{96,0},{1,33},{33,65},{65,97},{97,1},{2,34}... | collective-permute-start | bytes 12296 | tf_op jit(solution)/shard_map/ppermute | solution.py:391
  178.6 5.0 %collective-permute-start.2 = (f32[8,128]{1,0:T(8,128)S(1)}, f32[8,128]{1,0:T(8,128)S(1)}, u32[]{:S(2)}, u32[]{:S(2)}) collective-permute-start(f32[8,128]{1,0:T(8,128)S(1)} %broadcast_in_dim.3), channel_id=1, source_target_pairs={{0,96},{32,0},{64,32},{96,64},{1,97},{33,1},{65,33},{97,65},{2,98}... | collective-permute-start | bytes 12296 | tf_op jit(solution)/shard_map/ppermute | solution.py:391
  188.3 17.0 %all-to-all-start.5 = ((f32[128,4,128]{2,1,0:T(4,128)}), f32[128,4,128]{2,1,0:T(4,128)S(1)}, u32[]{:S(2)}, u32[]{:S(2)}) async-start(f32[128,4,128]{2,1,0:T(4,128)} %shard_map.171), calls=%async_computation.5 | async-start | bytes 524288 | tf_op jit(solution)/shard_map/all_to_all | solution.py:359
  208.0 13.2 %all-to-all-start.7 = ((f32[128,8,128]{2,1,0:T(8,128)}), f32[128,8,128]{2,1,0:T(8,128)S(1)}, u32[]{:S(2)}, u32[]{:S(2)}) async-start(f32[128,8,128]{2,1,0:T(8,128)} %shard_map.173), calls=%async_computation.7 | async-start | bytes 1048576 | tf_op jit(solution)/shard_map/all_to_all | solution.py:359

commit v2 on v1

v2 whole, which is shorter than its diff:
```python
import functools
import math

import jax
import jax.numpy as jnp
import ml_dtypes
import numpy as np
from jax import lax
from jax.experimental import pallas as pl
from jax.experimental.pallas import tpu as pltpu
from jax.sharding import PartitionSpec as P

WINDOW_FREQS = 64
NT = 512
FLO = 8
TILE_EXTENT = 256
RMAX = 48
RECEIVER_BLOCKS = 60
NVS = 4
SLOTS = 8
GROUP = 4
LEFT_COUNT = 2 * WINDOW_FREQS * NVS * 2048

shrink_level = 0.5
eps = 1e-06

F32 = jnp.float32
BF16 = jnp.bfloat16
VMEM = pltpu.VMEM
SMEM = pltpu.SMEM
HBM = pltpu.HBM
LIMIT = 16 * 1024 * 1024
TILES_LIMIT = 50 * 1024 * 1024


def iota(shape, axis):
    return lax.broadcasted_iota(jnp.int32, shape, axis)


def low_rows():
    return iota((8, 128), 0) < 4


def swap(x):
    return pltpu.roll(x, 4, 0)


def call(body, outs, ins, scratch=(), out_spaces=None, limit=LIMIT):
    out_spaces = out_spaces or [VMEM] * len(outs)
    return pl.pallas_call(
        body,
        out_shape=outs,
        in_specs=[pl.BlockSpec(memory_space=s) for s in ins],
        out_specs=[pl.BlockSpec(memory_space=s) for s in out_spaces],
        scratch_shapes=list(scratch),
        compiler_params=pltpu.CompilerParams(vmem_limit_bytes=limit),
    )


def pack_body(rb, direction, data, model, out, slot_of, mark, ids, direction_in, data_in, model_in, sems):
    copies = [
        pltpu.make_async_copy(source, target, sems.at[n])
        for n, (source, target) in enumerate(
            ((direction, direction_in), (data, data_in), (model, model_in))
        )
    ]
    for copy in copies:
        copy.start()

    def clear(b, _):
        mark[b] = -1
        return 0

    lax.fori_loop(0, 64, clear, 0)
    for m in range(SLOTS):
        ids[m] = 0
    count = jnp.int32(0)
    for t in range(rb.shape[0]):
        b = rb[t]
        seen = mark[b]
        slot = jnp.minimum(jnp.where(seen < 0, count, seen), SLOTS - 1)
        mark[b] = slot
        ids[slot] = b
        slot_of[t] = slot
        count = count + jnp.where(seen < 0, 1, 0)
    lane = iota((4, 128), 1)
    listed = jnp.zeros((4, 128), F32)
    for m in range(SLOTS):
        listed = jnp.where(lane == 64 + m, ids[m].astype(F32), listed)
    for copy in copies:
        copy.wait()
    for f in range(direction.shape[1]):
        for c in range(2):
            k = 2 * f + c
            out[k, :, 0:480] = direction_in[c, f]
            out[k, :, 512:640] = listed
            out[k, :, 512:576] = data_in[c, f]
            out[k, :, 640:1120] = model_in[c, f]


def model_body(rows, out):
    lane = iota((8, 128), 1)
    for j in range(16):
        both = jnp.concatenate([rows[j, :, 640:1152], rows[j + 16, :, 640:1152]], axis=0)
        part = [both[:, 128 * q : 128 * q + 128] for q in range(4)]
        for g in range(4):
            value = part[0]
            if g:
                value = jnp.where(
                    lane < 8 * g,
                    pltpu.roll(part[g - 1], 8 * g, 1),
                    pltpu.roll(part[g], 8 * g, 1),
                )
            out[32 * g + j] = value[0:4]
            out[32 * g + j + 16] = value[4:8]


def blocks_of(chunks, half):
    low = low_rows()
    blocks = [None] * (2 * half)
    for b in range(half):
        even, odd = chunks[2 * b], chunks[2 * b + 1]
        blocks[b] = jnp.where(low, even, swap(odd))
        blocks[b + half] = jnp.where(low, swap(even), odd)
    return blocks


def spread_body(ids, rows, out, direction, data):
    lane = iota((8, 640), 1)
    chunks = [None] * 60
    tails = []
    for j in range(16):
        both = jnp.concatenate([rows[j, :, 0:640], rows[j + 16, :, 0:640]], axis=0)
        tails.append(both[:, 512:640])
        shift, first = 480 * j % 128, 480 * j // 128
        moved = jnp.where(lane < 480, both, 0.0)
        if shift:
            moved = pltpu.roll(moved, shift, 1)
        for q in range((shift + 479) // 128 + 1):
            piece = moved[:, 128 * q : 128 * q + 128]
            n = first + q
            chunks[n] = piece if chunks[n] is None else chunks[n] + piece
    for b, block in enumerate(blocks_of(chunks, 30)):
        direction[b] = block
    left = iota((8, 128), 1) < 64
    ends = [jnp.where(left, tails[2 * n], pltpu.roll(tails[2 * n + 1], 64, 1)) for n in range(8)]
    for b, block in enumerate(blocks_of(ends, 4)):
        data[b] = block

    def one(i, _):
        picked = [direction[ids[i, m]] for m in range(SLOTS)]
        out[i] = jnp.concatenate(picked, axis=0).astype(BF16)
        return 0

    lax.fori_loop(0, 32, one, 0, unroll=4)


def lanes_body(slots, blocks, ranks, lane_slot, lane_block, limit):
    tiles = ranks.shape[1]
    wide = RMAX * tiles
    lane = iota((8, wide), 1)
    for ref, out in ((slots, lane_slot), (blocks, lane_block)):
        value = jnp.full((8, wide), ref[0], jnp.int32)
        for t in range(1, tiles):
            value = jnp.where(lane >= RMAX * t, ref[t], value)
        out[...] = value
    tile, lane = iota((tiles, wide), 0), iota((tiles, wide), 1)
    within = lane - RMAX * tile
    spread = jnp.where((within >= 0) & (within < RMAX), 1.0, 0.0).astype(BF16)
    rank = jnp.dot(ranks[...].astype(F32).astype(BF16), spread, preferred_element_type=F32)
    start = jnp.zeros((1, wide), jnp.int32)
    lane = iota((1, wide), 1)
    for t in range(1, tiles):
        start = jnp.where(lane >= RMAX * t, RMAX * t, start)
    limit[...] = rank.astype(jnp.int32) + start


def tiles_body(extra, lane_in, lane_out, limits, x, first, second, *refs):
    rest, out = refs[:-1], refs[-1]
    tiles = first.shape[1]
    wide = RMAX * tiles
    low = low_rows()
    turned = (((1,), (1,)), ((), ()))
    source, target = lane_in[...], lane_out[...]
    lane = iota((8, wide), 1)
    upper = iota((8, wide), 0) < 4

    def one(f):
        xr = x[2 * f, 0:64].astype(F32)
        xi = x[2 * f + 1, 0:64].astype(F32)
        real, imag = [], []
        for m in range(SLOTS):
            tr = xr[8 * m : 8 * m + 8]
            ti = xi[8 * m : 8 * m + 8]
            tr4, ti4 = swap(tr), swap(ti)
            real.append(jnp.concatenate([jnp.where(low, tr, ti4), jnp.where(low, tr4, ti)], axis=1))
            imag.append(
                jnp.concatenate([jnp.where(low, ti, -tr4), jnp.where(low, ti4, -tr)], axis=1)
            )
        real = jnp.concatenate(real, axis=0).astype(BF16)
        imag = jnp.concatenate(imag, axis=0).astype(BF16)
        every = lax.dot_general(
            real, first[f, :, 0].reshape(wide, TILE_EXTENT), turned, preferred_element_type=F32
        ) + lax.dot_general(
            imag, first[f, :, 1].reshape(wide, TILE_EXTENT), turned, preferred_element_type=F32
        )
        z = every[0:8]
        for m in range(1, SLOTS):
            z = jnp.where(source == m, every[8 * m : 8 * m + 8], z)
        z = jnp.where(lane < limits[pl.ds(GROUP * pl.program_id(0) + f, 1)], z, 0.0)
        turn = pltpu.roll(z, 4, 0)
        turn = jnp.where(upper, -turn, turn)
        za = [jnp.where(target == m, z, 0.0) for m in range(SLOTS)]
        zb = [jnp.where(target == m, turn, 0.0) for m in range(SLOTS)]
        za = jnp.concatenate(za, axis=0).astype(BF16)
        zb = jnp.concatenate(zb, axis=0).astype(BF16)
        c = jnp.dot(
            za, second[f, :, 0].reshape(wide, TILE_EXTENT), preferred_element_type=F32
        ) + jnp.dot(zb, second[f, :, 1].reshape(wide, TILE_EXTENT), preferred_element_type=F32)
        real, imag = [], []
        for m in range(SLOTS):
            left, right = c[8 * m : 8 * m + 8, 0:128], c[8 * m : 8 * m + 8, 128:256]
            real.append(jnp.where(low, left, swap(right)))
            imag.append(jnp.where(low, swap(left), right))
        if extra:
            real[-1] = imag[-1] = rest[0][...]
        out[2 * f] = jnp.concatenate(real, axis=0).astype(out.dtype)
        out[2 * f + 1] = jnp.concatenate(imag, axis=0).astype(out.dtype)

    for f in range(GROUP):
        one(f)


def lane_tables(slots, blocks, ranks):
    wide = RMAX * ranks.shape[1]
    table = jax.ShapeDtypeStruct((8, wide), jnp.int32)
    limit = jax.ShapeDtypeStruct((ranks.shape[0], wide), jnp.int32)
    return call(lanes_body, [table, table, limit], [SMEM, SMEM, VMEM])(slots, blocks, ranks)


def tile_products(lane_in, lane_out, limits, x, first, second, *extra):
    freqs, tiles = first.shape[0], first.shape[1]
    whole = pl.BlockSpec(memory_space=VMEM)
    factor = pl.BlockSpec((GROUP, tiles, 2, RMAX, TILE_EXTENT), lambda f: (f, 0, 0, 0, 0))
    return pl.pallas_call(
        functools.partial(tiles_body, bool(extra)),
        grid=(freqs // GROUP,),
        out_shape=jax.ShapeDtypeStruct((2 * freqs, 64, 128), BF16),
        in_specs=[
            whole,
            whole,
            whole,
            pl.BlockSpec((2 * GROUP, x.shape[1], 128), lambda f: (f, 0, 0)),
            factor,
            factor,
        ]
        + [whole] * len(extra),
        out_specs=pl.BlockSpec((2 * GROUP, 64, 128), lambda f: (f, 0, 0)),
        compiler_params=pltpu.CompilerParams(vmem_limit_bytes=TILES_LIMIT),
    )(lane_in, lane_out, limits, x, first, second, *extra)


def residual_body(alpha, parts, data, out, power_out):
    total = parts[0].astype(F32)
    for i in range(1, 32):
        total = total + parts[i].astype(F32)
    u = total - alpha[0] * data[...].reshape(64, 128)
    power = jnp.sum(jnp.sum(u * u, axis=0, keepdims=True), axis=1, keepdims=True)
    power_out[...] = jnp.broadcast_to(power, (8, 128))
    ub = u.astype(BF16)
    high = ub.astype(F32)
    rest = u - high
    low = low_rows()
    empty = jnp.zeros((8, 128), F32)
    for i in range(32):
        out[i, 0:64] = ub
    for b in range(8):
        hb, rb = high[8 * b : 8 * b + 8], rest[8 * b : 8 * b + 8]
        even = jnp.concatenate([jnp.where(low, hb, swap(rb)), empty], axis=0).astype(BF16)
        odd = jnp.concatenate([jnp.where(low, swap(hb), rb), empty], axis=0).astype(BF16)
        for n, tail in ((2 * b, even), (2 * b + 1, odd)):
            out[2 * n, 64:80] = tail
            out[2 * n + 1, 64:80] = tail


def powers_body(own, p1, p2, p3, out):
    power = (own[...] + p2[...]) + (p1[...] + p3[...])
    s1 = power.astype(BF16).astype(F32)
    s2 = (power - s1).astype(BF16).astype(F32)
    s3 = power - s1 - s2
    row = iota((8, 128), 0)
    out[...] = jnp.where(row == 0, s1, jnp.where(row == 1, s2, jnp.where(row == 2, s3, 0.0)))


def update_body(ids, parts, direction, model, out, beta_out, acc):
    acc[...] = jnp.zeros_like(acc)

    def one(i, power):
        part = parts[i].astype(F32)
        for m in range(SLOTS - 1):
            b = ids[i, m]
            acc[b] = acc[b] + part[8 * m : 8 * m + 8]
        return power + part[56:64]

    power = lax.fori_loop(0, 32, one, jnp.zeros((8, 128), F32), unroll=2)
    power = jnp.broadcast_to(jnp.sum(power, axis=0, keepdims=True), (8, 128))
    scale = jnp.sqrt(power / LEFT_COUNT + eps)
    inverse = 1.0 / scale
    beta_out[...] = inverse
    low = low_rows()
    lane = iota((8, 128), 1)
    chunks = [None] * 60
    power = jnp.zeros((8, 128), F32)
    for b in range(30):
        head = acc[b] * inverse - scale * direction[b]
        tail = acc[b + 30] * inverse - scale * direction[b + 30]
        power = power + head * head + tail * tail
        chunks[2 * b] = jnp.where(low, head, swap(tail))
        chunks[2 * b + 1] = jnp.where(low, swap(head), tail)
    power = jnp.sum(jnp.sum(power, axis=0, keepdims=True), axis=1, keepdims=True)
    power = jnp.broadcast_to(power, (8, 128))
    for d in range(64):
        n, off = 120 * d // 128, 120 * d % 128
        value = chunks[n]
        if off:
            value = pltpu.roll(value, 128 - off, 1)
        if off > 8:
            value = jnp.where(lane < 128 - off, value, pltpu.roll(chunks[n + 1], 128 - off, 1))
        value = jnp.where(lane == 120, power, value)
        j, g = d // 4, d % 4
        for d, row in ((32 * g + j, value[0:4]), (32 * g + j + 16, value[4:8])):
            out[d, 0:4] = row
            out[d, 4:8] = model[d]


def split_dot(a_high, a_low, b):
    b_high = b.astype(BF16)
    b_low = (b - b_high.astype(F32)).astype(BF16)
    return (
        jnp.dot(a_high, b_high, preferred_element_type=F32)
        + jnp.dot(a_high, b_low, preferred_element_type=F32)
        + jnp.dot(a_low, b_high, preferred_element_type=F32)
    )


def shrink_body(raw, lo, hi, fh, fl, bh, bl, out):
    lane = iota((128, 128), 1)
    count = 2 * WINDOW_FREQS * NVS * RECEIVER_BLOCKS * TILE_EXTENT
    sums = jnp.where(lane == 120, raw[:, 0, :], 0.0)
    power = jnp.sum(jnp.sum(sums, axis=0, keepdims=True), axis=1, keepdims=True)
    alpha = jnp.sqrt(power / count + eps)
    moment = iota((NT, 128), 0)
    inside = (moment >= lo[...]) & (moment < hi[...])
    for v in range(NVS):
        step = raw[:, v, :] / alpha
        out[:, v, :] = step
        signal = split_dot(fh[...], fl[...], raw[:, NVS + v, :] + step)
        kept = signal - jnp.clip(signal, -shrink_level, shrink_level)
        kept = jnp.where(inside, kept, 0.0)
        out[:, NVS + v, :] = split_dot(bh[...], bl[...], kept)


def finish_body(place, beta, back, tails, u_next, v_next, m_next):
    lane = iota((8, 128), 1)
    inverse = beta[...]
    odd = place[0] == 1
    for k in range(32):
        f, c = k // 2, k % 2
        quarter = [back[g, k] for g in range(4)]
        for q in range(4):
            value = quarter[q]
            if q:
                value = pltpu.roll(value, 128 - 8 * q, 1)
            if q < 3:
                value = jnp.where(
                    lane < 120 - 8 * q, value, pltpu.roll(quarter[q + 1], 120 - 8 * q, 1)
                )
            width = 128 if q < 3 else 96
            v_next[c, f, :, 128 * q : 128 * q + width] = value[0:4, 0:width]
            m_next[c, f, :, 128 * q : 128 * q + width] = value[4:8, 0:width]
        part = tails[k, 64:80].astype(F32)[0:8]
        part = (part + swap(part)) * inverse
        part = jnp.where(odd, pltpu.roll(part, 64, 1), part)
        u_next[c, f] = part[0:4, 0:64]


def transform_tables():
    steps = np.arange(NT)
    bins = FLO + np.arange(WINDOW_FREQS)
    phase = (bins[None, :] * steps[:, None] % NT) * (2.0 * math.pi / NT)
    table = np.stack([np.cos(phase), -np.sin(phase)], axis=2).reshape(NT, 2 * WINDOW_FREQS)
    forward = (table / math.sqrt(WINDOW_FREQS)).astype(np.float32)
    backward = (table.T * (2.0 * math.sqrt(WINDOW_FREQS) / NT)).astype(np.float32)
    out = []
    for a in (forward, backward):
        high = a.astype(ml_dtypes.bfloat16)
        out += [high, (a - high.astype(np.float32)).astype(ml_dtypes.bfloat16)]
    return out


def on_device(
    data_vec,
    direction,
    model,
    alpha,
    u_factor,
    v_factor,
    ranks,
    tile_source_block,
    tile_receiver_block,
    time_lo,
    time_len,
):
    shape = jax.ShapeDtypeStruct
    both = ("freq", "tile")
    g = lax.axis_index("freq")
    place = lax.axis_index("tile")

    def exchange(x, axis):
        return lax.all_to_all(x, axis, split_axis=0, concat_axis=0, tiled=True)

    packed, slots = call(
        pack_body,
        [shape((32, 4, 1152), F32), shape((15,), jnp.int32)],
        [SMEM, HBM, HBM, HBM],
        [
            SMEM((64,), jnp.int32),
            SMEM((SLOTS,), jnp.int32),
            VMEM(direction.shape, F32),
            VMEM(data_vec.shape, F32),
            VMEM(model.shape, F32),
            pltpu.SemaphoreType.DMA((3,)),
        ],
        [VMEM, SMEM],
    )(tile_receiver_block, direction, data_vec, model)
    rows = exchange(packed, "tile")
    barrier = lax.optimization_barrier
    lanes = lane_tables(slots, tile_source_block, ranks)
    ids = rows[:, 0, 576 : 576 + SLOTS].astype(jnp.int32)
    ids, lanes = barrier((ids, lanes))
    lane_slot, lane_block, limits = lanes
    picked, direction_rows, data_rows = call(
        spread_body,
        [shape((32, 64, 128), BF16), shape((60, 8, 128), F32), shape((8, 8, 128), F32)],
        [SMEM, VMEM],
    )(ids, rows)
    x = exchange(picked, "tile")
    (model_rows,) = call(model_body, [shape((128, 4, 128), F32)], [VMEM])(rows)
    x, model_rows = barrier((x, model_rows))
    parts = tile_products(lane_slot, lane_block, limits, x, v_factor, u_factor)
    parts = exchange(parts, "tile")
    residual, power = call(
        residual_body,
        [shape((32, 80, 128), BF16), shape((8, 128), F32)],
        [SMEM, VMEM, VMEM],
    )(alpha.reshape(1), parts, data_rows)
    others = [lax.ppermute(power, "freq", [(i, (i + d) % 4) for i in range(4)]) for d in (1, 2, 3)]
    u_all = exchange(residual, "tile")
    (powers,) = call(powers_body, [shape((8, 128), F32)], [VMEM] * 4)(power, *others)

    back = tile_products(lane_block, lane_slot, limits, u_all, u_factor, v_factor, powers)
    back = exchange(back, "tile")
    raw, beta = call(
        update_body,
        [shape((128, 8, 128), F32), shape((8, 128), F32)],
        [SMEM, VMEM, VMEM, VMEM],
        [VMEM((64, 8, 128), F32)],
    )(ids, back, direction_rows, model_rows)
    raw = exchange(raw, both)

    lo = lax.dynamic_slice_in_dim(time_lo, g * 120, 120, 0)
    hi = lo + lax.dynamic_slice_in_dim(time_len, g * 120, 120, 0)
    lo = jnp.pad(lo, (0, 8)).reshape(1, 128)
    hi = jnp.pad(hi, (0, 8)).reshape(1, 128)
    tables = [jnp.asarray(a) for a in transform_tables()]
    (shrunk,) = call(shrink_body, [shape((128, 8, 128), F32)], [VMEM] * 7)(
        raw, lo, hi, *tables
    )
    shrunk = exchange(shrunk, "freq").reshape(4, 32, 8, 128)
    return call(
        finish_body,
        [
            shape(data_vec.shape, F32),
            shape(direction.shape, F32),
            shape(direction.shape, F32),
        ],
        [SMEM, VMEM, VMEM, VMEM],
    )((place % 2).reshape(1), beta, shrunk, u_all)


def solution(mesh):
    vector = P(None, "freq", None, "tile")
    factor = P("freq", "tile", None, None, None)
    placed = (
        vector,
        vector,
        vector,
        P(),
        factor,
        factor,
        P("freq", "tile"),
        P("tile"),
        P("tile"),
        P("tile"),
        P("tile"),
    )
    return jax.shard_map(
        on_device,
        mesh=mesh,
        in_specs=placed,
        out_specs=(vector, vector, vector),
        check_vma=False,
    )
```

time: 224 us -> 154 us (0.69)
  Pallas kernels: 92.6 us -> 34.5 us
  blocking collectives: 47.8 us -> 15.2 us
  waiting for transfers between devices: 40.5 us -> 59.2 us
  starting transfers between devices: 30.1 us -> 37.4 us
  between operations: 4.14 us -> 1.46 us
    pallas_call x7 -> x9, Pallas kernels: 89.8 us -> 31.4 us  [the longest x2 22.2 us: tile_products(): pl.pallas_call(functools.partial(tiles_body, bool(extra)), grid=(freqs //...]
    all_to_all x3 -> x1, blocking collectives: 47.8 us -> 15.2 us  [exchange(): return lax.all_to_all(x, axis, split_axis=0, concat_axis=0, tiled=True)]
    all_to_all x5 -> x6, waiting for transfers between devices: 40.5 us -> 56.6 us  [exchange(): return lax.all_to_all(x, axis, split_axis=0, concat_axis=0, tiled=True)]
    all_to_all x5 -> x6, starting transfers between devices: 23.2 us -> 30.9 us  [exchange(): return lax.all_to_all(x, axis, split_axis=0, concat_axis=0, tiled=True)]
    ppermute x3, waiting for transfers between devices: 0.01 us -> 2.59 us  [on_device(): lax.ppermute(power, 'freq', [(i, (i + d) % 4) for i in range(4)])]
    unnamed x24 -> x20, local copies, waits for them, and re-layouts: 3.82 us -> 4.76 us
  transfers between devices with their start and end apart: 8 -> 9, of which waited for: 4 -> 8; matrix products, arithmetic and copies ran while one was open for 2% -> 1% of each run, Pallas kernels for 2% -> 1%
where the time goes in v2:
time: 154 us; the launch traced here: 153 us
  waiting for transfers between devices  59.2 us (38%)
  starting transfers between devices  37.4 us (24%)
  Pallas kernels  34.5 us (22%)
  blocking collectives  15.2 us (10%)
  local copies, waits for them, and re-layouts  4.85 us (3%)
    all_to_all x6, waiting for transfers between devices, exchange(): return lax.all_to_all(x, axis, split_axis=0, concat_axis=0, tiled=True)  56.6 us
    all_to_all x6, starting transfers between devices, exchange(): return lax.all_to_all(x, axis, split_axis=0, concat_axis=0, tiled=True)  30.9 us
    pallas_call x2, Pallas kernels, tile_products(): pl.pallas_call(functools.partial(tiles_body, bool(extra)), grid=(freqs //...  22.2 us
    all_to_all x1, blocking collectives, exchange(): return lax.all_to_all(x, axis, split_axis=0, concat_axis=0, tiled=True)  15.2 us
    ppermute x3, starting transfers between devices, on_device(): lax.ppermute(power, 'freq', [(i, (i + d) % 4) for i in range(4)])  6.58 us
    unnamed x20, local copies, waits for them, and re-layouts  4.76 us
  transfers between devices with their start and end apart: 9, of which 8 were waited for; matrix products, arithmetic and copies ran while one was open for 1% of the time, Pallas kernels for 1%

profile of v2, /device:TPU:0, one launch (start us, length us, event | category | flops | bytes accessed | tf_op | source)
XLA Modules:
  0.0 153.4 jit_solution(7843441176382533673)
XLA Ops:
  4.0 2.1 %shard_map.166 = (f32[32,4,1152]{2,1,0:T(4,128)}, s32[15]{0:T(128)S(1)}) custom-call(s32[15]{0:T(128)S(1)} %copy-done.9, f32[2,16,4,480]{3,2,1,0:T(4,128)S(1)} %copy-done, f32[2,16,4,64]{3,2,1,0:T(4,128)S(1)} %copy-done.6, f32[2,16,4,480]{3,2,1,0:T(4,128)S(1)} %copy-done.1), custom_call_target="tpu_custom_call" | custom-call | tf_op jit(solution)/shard_map/pallas_call | solution.py:422
  6.1 7.4 %all-to-all-start = ((f32[32,4,1152]{2,1,0:T(4,128)}), f32[32,4,1152]{2,1,0:T(4,128)S(1)}, u32[]{:S(2)}, u32[]{:S(2)}) async-start(f32[32,4,1152]{2,1,0:T(4,128)} %get-tuple-element.21), calls=%async_computation | async-start | bytes 1179648 | tf_op jit(solution)/shard_map/all_to_all | solution.py:420
  15.6 9.8 %all-to-all-done.rows = f32[32,4,1152]{2,1,0:T(4,128)S(1)} async-done(((f32[32,4,1152]{2,1,0:T(4,128)}), f32[32,4,1152]{2,1,0:T(4,128)S(1)}, u32[]{:S(2)}, u32[]{:S(2)}) %all-to-all-start) | async-done | bytes 589856 | tf_op jit(solution)/shard_map/all_to_all | solution.py:420
  25.5 2.1 %shard_map.168 = (bf16[32,64,128]{2,1,0:T(8,128)(2,1)}, f32[60,8,128]{2,1,0:T(8,128)S(1)}, f32[8,8,128]{2,1,0:T(8,128)S(1)}) custom-call(s32[32,8]{1,0:T(8,128)S(1)} %convert_bitcast_fusion.ids, f32[32,4,1152]{2,1,0:T(4,128)S(1)} %all-to-all-done.rows), custom_call_target="tpu_custom_call" | custom-call | tf_op jit(solution)/shard_map/pallas_call | solution.py:442
  27.5 4.1 %all-to-all-start.1 = ((bf16[32,64,128]{2,1,0:T(8,128)(2,1)}), bf16[32,64,128]{2,1,0:T(8,128)(2,1)S(1)}, u32[]{:S(2)}, u32[]{:S(2)}) async-start(bf16[32,64,128]{2,1,0:T(8,128)(2,1)} %get-tuple-element.30), calls=%async_computation.1 | async-start | bytes 1048576 | tf_op jit(solution)/shard_map/all_to_all | solution.py:420
  31.8 11.0 %all-to-all-done.1.x = bf16[32,64,128]{2,1,0:T(8,128)(2,1)S(1)} async-done(((bf16[32,64,128]{2,1,0:T(8,128)(2,1)}), bf16[32,64,128]{2,1,0:T(8,128)(2,1)S(1)}, u32[]{:S(2)}, u32[]{:S(2)}) %all-to-all-start.1) | async-done | bytes 524320 | tf_op jit(solution)/shard_map/all_to_all | solution.py:420
  42.9 11.5 %shard_map.170 = bf16[32,64,128]{2,1,0:T(8,128)(2,1)} custom-call(s32[8,720]{1,0:T(8,128)S(1)} %get-tuple-element.28.lane_in.lane_out, s32[8,720]{1,0:T(8,128)S(1)} %get-tuple-element.27.lane_out.lane_in, s32[16,720]{1,0:T(8,128)S(1)} %get-tuple-element.29.limits, bf16[32,64,128]{2,1,0:T(8,128)(2,1)S(1)} %all-to-all-done.1.x, ...), custom_call_target="tpu_custom_call" | custom-call | tf_op jit(solution)/shard_map/pallas_call | solution.py:245
  54.3 4.1 %all-to-all-start.2 = ((bf16[32,64,128]{2,1,0:T(8,128)(2,1)}), bf16[32,64,128]{2,1,0:T(8,128)(2,1)S(1)}, u32[]{:S(2)}, u32[]{:S(2)}) async-start(bf16[32,64,128]{2,1,0:T(8,128)(2,1)} %shard_map.170), calls=%async_computation.2 | async-start | bytes 1048576 | tf_op jit(solution)/shard_map/all_to_all | solution.py:420
  59.0 10.5 %all-to-all-done.2.parts = bf16[32,64,128]{2,1,0:T(8,128)(2,1)S(1)} async-done(((bf16[32,64,128]{2,1,0:T(8,128)(2,1)}), bf16[32,64,128]{2,1,0:T(8,128)(2,1)S(1)}, u32[]{:S(2)}, u32[]{:S(2)}) %all-to-all-start.2) | async-done | bytes 524320 | tf_op jit(solution)/shard_map/all_to_all | solution.py:420
  70.5 4.1 %all-to-all-start.3 = ((bf16[32,80,128]{2,1,0:T(8,128)(2,1)}), bf16[32,80,128]{2,1,0:T(8,128)(2,1)S(1)}, u32[]{:S(2)}, u32[]{:S(2)}) async-start(bf16[32,80,128]{2,1,0:T(8,128)(2,1)} %get-tuple-element.33), calls=%async_computation.3 | async-start | bytes 1310720 | tf_op jit(solution)/shard_map/all_to_all | solution.py:420
  74.6 2.0 %collective-permute-start = (f32[8,128]{1,0:T(8,128)S(1)}, f32[8,128]{1,0:T(8,128)S(1)}, u32[]{:S(2)}, u32[]{:S(2)}) collective-permute-start(f32[8,128]{1,0:T(8,128)S(1)} %get-tuple-element.34.own), channel_id=1, source_target_pairs={{0,32},{32,64},{64,96},{96,0},{1,33},{33,65},{65,97},{97,1},{2,34}... | collective-permute-start | bytes 12296 | tf_op jit(solution)/shard_map/ppermute | solution.py:457
  76.6 3.6 %collective-permute-start.1 = (f32[8,128]{1,0:T(8,128)S(1)}, f32[8,128]{1,0:T(8,128)S(1)}, u32[]{:S(2)}, u32[]{:S(2)}) collective-permute-start(f32[8,128]{1,0:T(8,128)S(1)} %get-tuple-element.34.own), channel_id=1, source_target_pairs={{0,64},{32,96},{64,0},{96,32},{1,65},{33,97},{65,1},{97,33},{2,66}... | collective-permute-start | bytes 12296 | tf_op jit(solution)/shard_map/ppermute | solution.py:457
  80.1 1.0 collective-permute-start.2
  81.8 2.0 %collective-permute-done.2.p3 = f32[8,128]{1,0:T(8,128)S(1)} collective-permute-done((f32[8,128]{1,0:T(8,128)S(1)}, f32[8,128]{1,0:T(8,128)S(1)}, u32[]{:S(2)}, u32[]{:S(2)}) %collective-permute-start.2) | collective-permute-done | bytes 4128 | tf_op jit(solution)/shard_map/ppermute | solution.py:457
  83.8 3.3 %all-to-all-done.3.x.tails = bf16[32,80,128]{2,1,0:T(8,128)(2,1)S(1)} async-done(((bf16[32,80,128]{2,1,0:T(8,128)(2,1)}), bf16[32,80,128]{2,1,0:T(8,128)(2,1)S(1)}, u32[]{:S(2)}, u32[]{:S(2)}) %all-to-all-start.3) | async-done | bytes 655392 | tf_op jit(solution)/shard_map/all_to_all | solution.py:420
  87.1 10.7 %shard_map.173 = bf16[32,64,128]{2,1,0:T(8,128)(2,1)S(1)} custom-call(s32[8,720]{1,0:T(8,128)S(1)} %get-tuple-element.27.lane_out.lane_in, s32[8,720]{1,0:T(8,128)S(1)} %get-tuple-element.28.lane_in.lane_out, s32[16,720]{1,0:T(8,128)S(1)} %get-tuple-element.29.limits, bf16[32,80,128]{2,1,0:T(8,128)(2,1)S(1)} %all-to-all-done.3.x.tails, ...), custom_call_target="tpu_custom_call" | custom-call | tf_op jit(solution)/shard_map/pallas_call | solution.py:245
  97.8 15.2 %all_to_all.35.parts = bf16[32,64,128]{2,1,0:T(8,128)(2,1)S(1)} all-to-all(bf16[32,64,128]{2,1,0:T(8,128)(2,1)S(1)} %shard_map.173), channel_id=1, replica_groups=mesh['freq'=4,'tile'=32] {'tile'}, dimensions={0} | all-to-all | bytes 1048576 | tf_op jit(solution)/shard_map/all_to_all | solution.py:420
  113.0 2.6 %shard_map.174 = (f32[128,8,128]{2,1,0:T(8,128)}, f32[8,128]{1,0:T(8,128)S(1)}) custom-call(s32[32,8]{1,0:T(8,128)S(1)} %convert_bitcast_fusion.ids, bf16[32,64,128]{2,1,0:T(8,128)(2,1)S(1)} %all_to_all.35.parts, f32[60,8,128]{2,1,0:T(8,128)S(1)} %get-tuple-element.35.direction, f32[128,4,128]{2,1,0:T(4,128)S(1)} %shard_map.169.model), custom_call_target="tpu_custom_call" | custom-call | tf_op jit(solution)/shard_map/pallas_call | solution.py:463
  115.6 7.7 %all-to-all-start.5 = ((f32[128,8,128]{2,1,0:T(8,128)}), f32[128,8,128]{2,1,0:T(8,128)S(1)}, u32[]{:S(2)}, u32[]{:S(2)}) async-start(f32[128,8,128]{2,1,0:T(8,128)} %get-tuple-element.38), calls=%async_computation.5 | async-start | bytes 1048576 | tf_op jit(solution)/shard_map/all_to_all | solution.py:420
  124.2 12.7 %all-to-all-done.5.raw = f32[128,8,128]{2,1,0:T(8,128)S(1)} async-done(((f32[128,8,128]{2,1,0:T(8,128)}), f32[128,8,128]{2,1,0:T(8,128)S(1)}, u32[]{:S(2)}, u32[]{:S(2)}) %all-to-all-start.5) | async-done | bytes 524320 | tf_op jit(solution)/shard_map/all_to_all | solution.py:420
  136.9 2.7 %shard_map.175 = f32[128,8,128]{2,1,0:T(8,128)} custom-call(f32[128,8,128]{2,1,0:T(8,128)S(1)} %all-to-all-done.5.raw, s32[1,128]{1,0:T(1,128)S(1)} %get-tuple-element.42.lo, s32[1,128]{1,0:T(1,128)S(1)} %get-tuple-element.41.hi, bf16[512,128]{1,0:T(8,128)(2,1)S(1)} %copy-done.2, bf16[512,128]{1,0:T(8,128)(2,1)S(1)} %copy-done.3, ...), custom_call_target="tpu_custom_call" | custom-call | tf_op jit(solution)/shard_map/pallas_call | solution.py:476
  139.6 3.5 %all-to-all-start.6 = ((f32[128,8,128]{2,1,0:T(8,128)}), f32[128,8,128]{2,1,0:T(8,128)S(1)}, u32[]{:S(2)}, u32[]{:S(2)}) async-start(f32[128,8,128]{2,1,0:T(8,128)} %shard_map.175), calls=%async_computation.6 | async-start | bytes 1048576 | tf_op jit(solution)/shard_map/all_to_all | solution.py:420
  143.1 9.3 %all-to-all-done.6 = f32[128,8,128]{2,1,0:T(8,128)S(1)} async-done(((f32[128,8,128]{2,1,0:T(8,128)}), f32[128,8,128]{2,1,0:T(8,128)S(1)}, u32[]{:S(2)}, u32[]{:S(2)}) %all-to-all-start.6) | async-done | bytes 524320 | tf_op jit(solution)/shard_map/all_to_all | solution.py:420
  152.4 1.0 shard_map.176
  (30 shorter events, 8.0 us)
Async XLA Ops:
  0.6 1.0 copy-start
  1.6 0.9 copy-start.1
  2.5 0.8 copy-start.6
  3.4 0.7 copy-start.9
  6.1 19.2 %all-to-all-start = ((f32[32,4,1152]{2,1,0:T(4,128)}), f32[32,4,1152]{2,1,0:T(4,128)S(1)}, u32[]{:S(2)}, u32[]{:S(2)}) async-start(f32[32,4,1152]{2,1,0:T(4,128)} %get-tuple-element.21), calls=%async_computation | async-start | bytes 1179648 | tf_op jit(solution)/shard_map/all_to_all | solution.py:420
  13.5 0.7 copy-start.7
  14.2 0.7 copy-start.8
  27.5 15.3 %all-to-all-start.1 = ((bf16[32,64,128]{2,1,0:T(8,128)(2,1)}), bf16[32,64,128]{2,1,0:T(8,128)(2,1)S(1)}, u32[]{:S(2)}, u32[]{:S(2)}) async-start(bf16[32,64,128]{2,1,0:T(8,128)(2,1)} %get-tuple-element.30), calls=%async_computation.1 | async-start | bytes 1048576 | tf_op jit(solution)/shard_map/all_to_all | solution.py:420
  54.3 15.2 %all-to-all-start.2 = ((bf16[32,64,128]{2,1,0:T(8,128)(2,1)}), bf16[32,64,128]{2,1,0:T(8,128)(2,1)S(1)}, u32[]{:S(2)}, u32[]{:S(2)}) async-start(bf16[32,64,128]{2,1,0:T(8,128)(2,1)} %shard_map.170), calls=%async_computation.2 | async-start | bytes 1048576 | tf_op jit(solution)/shard_map/all_to_all | solution.py:420
  70.5 16.6 %all-to-all-start.3 = ((bf16[32,80,128]{2,1,0:T(8,128)(2,1)}), bf16[32,80,128]{2,1,0:T(8,128)(2,1)S(1)}, u32[]{:S(2)}, u32[]{:S(2)}) async-start(bf16[32,80,128]{2,1,0:T(8,128)(2,1)} %get-tuple-element.33), calls=%async_computation.3 | async-start | bytes 1310720 | tf_op jit(solution)/shard_map/all_to_all | solution.py:420
  74.6 6.6 %collective-permute-start = (f32[8,128]{1,0:T(8,128)S(1)}, f32[8,128]{1,0:T(8,128)S(1)}, u32[]{:S(2)}, u32[]{:S(2)}) collective-permute-start(f32[8,128]{1,0:T(8,128)S(1)} %get-tuple-element.34.own), channel_id=1, source_target_pairs={{0,32},{32,64},{64,96},{96,0},{1,33},{33,65},{65,97},{97,1},{2,34}... | collective-permute-start | bytes 12296 | tf_op jit(solution)/shard_map/ppermute | solution.py:457
  76.6 5.2 %collective-permute-start.1 = (f32[8,128]{1,0:T(8,128)S(1)}, f32[8,128]{1,0:T(8,128)S(1)}, u32[]{:S(2)}, u32[]{:S(2)}) collective-permute-start(f32[8,128]{1,0:T(8,128)S(1)} %get-tuple-element.34.own), channel_id=1, source_target_pairs={{0,64},{32,96},{64,0},{96,32},{1,65},{33,97},{65,1},{97,33},{2,66}... | collective-permute-start | bytes 12296 | tf_op jit(solution)/shard_map/ppermute | solution.py:457
  80.1 3.6 %collective-permute-start.2 = (f32[8,128]{1,0:T(8,128)S(1)}, f32[8,128]{1,0:T(8,128)S(1)}, u32[]{:S(2)}, u32[]{:S(2)}) collective-permute-start(f32[8,128]{1,0:T(8,128)S(1)} %get-tuple-element.34.own), channel_id=1, source_target_pairs={{0,96},{32,0},{64,32},{96,64},{1,97},{33,1},{65,33},{97,65},{2,98}... | collective-permute-start | bytes 12296 | tf_op jit(solution)/shard_map/ppermute | solution.py:457
  83.8 53.1 %copy-start.2 = (bf16[512,128]{1,0:T(8,128)(2,1)S(1)}, bf16[512,128]{1,0:T(8,128)(2,1)}, u32[]{:S(2)}) copy-start(bf16[512,128]{1,0:T(8,128)(2,1)} %constant.35.clone.fh) | copy-start | bytes 393220
  83.8 53.1 %copy-start.3 = (bf16[512,128]{1,0:T(8,128)(2,1)S(1)}, bf16[512,128]{1,0:T(8,128)(2,1)}, u32[]{:S(2)}) copy-start(bf16[512,128]{1,0:T(8,128)(2,1)} %constant.36.clone.fl) | copy-start | bytes 393220
  83.8 53.1 %copy-start.4 = (bf16[128,512]{1,0:T(8,128)(2,1)S(1)}, bf16[128,512]{1,0:T(8,128)(2,1)}, u32[]{:S(2)}) copy-start(bf16[128,512]{1,0:T(8,128)(2,1)} %constant.37.clone.bh) | copy-start | bytes 393220
  83.8 53.1 %copy-start.5 = (bf16[128,512]{1,0:T(8,128)(2,1)S(1)}, bf16[128,512]{1,0:T(8,128)(2,1)}, u32[]{:S(2)}) copy-start(bf16[128,512]{1,0:T(8,128)(2,1)} %constant.38.clone.bl) | copy-start | bytes 393220
  115.6 21.2 %all-to-all-start.5 = ((f32[128,8,128]{2,1,0:T(8,128)}), f32[128,8,128]{2,1,0:T(8,128)S(1)}, u32[]{:S(2)}, u32[]{:S(2)}) async-start(f32[128,8,128]{2,1,0:T(8,128)} %get-tuple-element.38), calls=%async_computation.5 | async-start | bytes 1048576 | tf_op jit(solution)/shard_map/all_to_all | solution.py:420
  139.6 12.8 %all-to-all-start.6 = ((f32[128,8,128]{2,1,0:T(8,128)}), f32[128,8,128]{2,1,0:T(8,128)S(1)}, u32[]{:S(2)}, u32[]{:S(2)}) async-start(f32[128,8,128]{2,1,0:T(8,128)} %shard_map.175), calls=%async_computation.6 | async-start | bytes 1048576 | tf_op jit(solution)/shard_map/all_to_all | solution.py:420

commit v3 on v2

--- a/solution.py
+++ b/solution.py
@@ -28,7 +28,6 @@
 BF16 = jnp.bfloat16
 VMEM = pltpu.VMEM
 SMEM = pltpu.SMEM
-HBM = pltpu.HBM
 LIMIT = 16 * 1024 * 1024
 TILES_LIMIT = 50 * 1024 * 1024
 
@@ -57,16 +56,7 @@
     )
 
 
-def pack_body(rb, direction, data, model, out, slot_of, mark, ids, direction_in, data_in, model_in, sems):
-    copies = [
-        pltpu.make_async_copy(source, target, sems.at[n])
-        for n, (source, target) in enumerate(
-            ((direction, direction_in), (data, data_in), (model, model_in))
-        )
-    ]
-    for copy in copies:
-        copy.start()
-
+def pack_body(rb, direction, data, out, slot_of, mark, ids):
     def clear(b, _):
         mark[b] = -1
         return 0
@@ -87,32 +77,34 @@
     listed = jnp.zeros((4, 128), F32)
     for m in range(SLOTS):
         listed = jnp.where(lane == 64 + m, ids[m].astype(F32), listed)
-    for copy in copies:
-        copy.wait()
     for f in range(direction.shape[1]):
         for c in range(2):
             k = 2 * f + c
-            out[k, :, 0:480] = direction_in[c, f]
+            out[k, :, 0:480] = direction[c, f]
             out[k, :, 512:640] = listed
-            out[k, :, 512:576] = data_in[c, f]
-            out[k, :, 640:1120] = model_in[c, f]
-
-
-def model_body(rows, out):
+            out[k, :, 512:576] = data[c, f]
+
+
+def model_body(group, model, out):
     lane = iota((8, 128), 1)
-    for j in range(16):
-        both = jnp.concatenate([rows[j, :, 640:1152], rows[j + 16, :, 640:1152]], axis=0)
-        part = [both[:, 128 * q : 128 * q + 128] for q in range(4)]
-        for g in range(4):
-            value = part[0]
-            if g:
+    for q in range(4):
+        d = lax.rem(q + 4 - group[0], 4)
+        for f in range(model.shape[1]):
+            lo = max(q - 1, 0) * 128
+            both = [model[c, f, :, lo : lo + (256 if 0 < q < 3 else 128 if q == 0 else 224)] for c in range(2)]
+            both = jnp.concatenate(both, axis=0)
+            if q == 0:
+                value = both
+            else:
+                if q == 3:
+                    both = jnp.concatenate([both, jnp.zeros((8, 32), F32)], axis=1)
                 value = jnp.where(
-                    lane < 8 * g,
-                    pltpu.roll(part[g - 1], 8 * g, 1),
-                    pltpu.roll(part[g], 8 * g, 1),
+                    lane < 8 * q,
+                    pltpu.roll(both[:, 0:128], 8 * q, 1),
+                    pltpu.roll(both[:, 128:256], 8 * q, 1),
                 )
-            out[32 * g + j] = value[0:4]
-            out[32 * g + j + 16] = value[4:8]
+            out[d, 2 * f] = value[0:4]
+            out[d, 2 * f + 1] = value[4:8]
 
 
 def blocks_of(chunks, half):
@@ -130,7 +122,7 @@
     chunks = [None] * 60
     tails = []
     for j in range(16):
-        both = jnp.concatenate([rows[j, :, 0:640], rows[j + 16, :, 0:640]], axis=0)
+        both = jnp.concatenate([rows[j], rows[j + 16]], axis=0)
         tails.append(both[:, 512:640])
         shift, first = 480 * j % 128, 480 * j // 128
         moved = jnp.where(lane < 480, both, 0.0)
@@ -268,19 +260,8 @@
     power = jnp.sum(jnp.sum(u * u, axis=0, keepdims=True), axis=1, keepdims=True)
     power_out[...] = jnp.broadcast_to(power, (8, 128))
     ub = u.astype(BF16)
-    high = ub.astype(F32)
-    rest = u - high
-    low = low_rows()
-    empty = jnp.zeros((8, 128), F32)
     for i in range(32):
-        out[i, 0:64] = ub
-    for b in range(8):
-        hb, rb = high[8 * b : 8 * b + 8], rest[8 * b : 8 * b + 8]
-        even = jnp.concatenate([jnp.where(low, hb, swap(rb)), empty], axis=0).astype(BF16)
-        odd = jnp.concatenate([jnp.where(low, swap(hb), rb), empty], axis=0).astype(BF16)
-        for n, tail in ((2 * b, even), (2 * b + 1, odd)):
-            out[2 * n, 64:80] = tail
-            out[2 * n + 1, 64:80] = tail
+        out[i] = ub
 
 
 def powers_body(own, p1, p2, p3, out):
@@ -292,7 +273,7 @@
     out[...] = jnp.where(row == 0, s1, jnp.where(row == 1, s2, jnp.where(row == 2, s3, 0.0)))
 
 
-def update_body(ids, parts, direction, model, out, beta_out, acc):
+def update_body(ids, parts, direction, out, beta_out, acc):
     acc[...] = jnp.zeros_like(acc)
 
     def one(i, power):
@@ -328,9 +309,8 @@
             value = jnp.where(lane < 128 - off, value, pltpu.roll(chunks[n + 1], 128 - off, 1))
         value = jnp.where(lane == 120, power, value)
         j, g = d // 4, d % 4
-        for d, row in ((32 * g + j, value[0:4]), (32 * g + j + 16, value[4:8])):
-            out[d, 0:4] = row
-            out[d, 4:8] = model[d]
+        out[32 * g + j] = value[0:4]
+        out[32 * g + j + 16] = value[4:8]
 
 
 def split_dot(a_high, a_low, b):
@@ -343,7 +323,10 @@
     )
 
 
-def shrink_body(raw, lo, hi, fh, fl, bh, bl, out):
+def shrink_body(group, raw, m0, m1, m2, m3, lo, hi, fh, fl, bh, bl, out, model, both):
+    for d, part in enumerate((m0, m1, m2, m3)):
+        source = lax.rem(group[0] + 4 - d, 4)
+        model[pl.ds(source * 32, 32)] = part[...]
     lane = iota((128, 128), 1)
     count = 2 * WINDOW_FREQS * NVS * RECEIVER_BLOCKS * TILE_EXTENT
     sums = jnp.where(lane == 120, raw[:, 0, :], 0.0)
@@ -353,35 +336,40 @@
     inside = (moment >= lo[...]) & (moment < hi[...])
     for v in range(NVS):
         step = raw[:, v, :] / alpha
-        out[:, v, :] = step
-        signal = split_dot(fh[...], fl[...], raw[:, NVS + v, :] + step)
+        both[:, v, :] = step
+        signal = split_dot(fh[...], fl[...], model[:, v, :] + step)
         kept = signal - jnp.clip(signal, -shrink_level, shrink_level)
         kept = jnp.where(inside, kept, 0.0)
-        out[:, NVS + v, :] = split_dot(bh[...], bl[...], kept)
-
-
-def finish_body(place, beta, back, tails, u_next, v_next, m_next):
+        both[:, NVS + v, :] = split_dot(bh[...], bl[...], kept)
+    out[...] = both[...].reshape(WINDOW_FREQS, 16, 128).astype(BF16)
+
+
+def finish_body(place, beta, back, u, u_next, v_next, m_next):
     lane = iota((8, 128), 1)
     inverse = beta[...]
-    odd = place[0] == 1
-    for k in range(32):
-        f, c = k // 2, k % 2
-        quarter = [back[g, k] for g in range(4)]
-        for q in range(4):
-            value = quarter[q]
-            if q:
-                value = pltpu.roll(value, 128 - 8 * q, 1)
-            if q < 3:
-                value = jnp.where(
-                    lane < 120 - 8 * q, value, pltpu.roll(quarter[q + 1], 120 - 8 * q, 1)
-                )
-            width = 128 if q < 3 else 96
-            v_next[c, f, :, 128 * q : 128 * q + width] = value[0:4, 0:width]
-            m_next[c, f, :, 128 * q : 128 * q + width] = value[4:8, 0:width]
-        part = tails[k, 64:80].astype(F32)[0:8]
-        part = (part + swap(part)) * inverse
-        part = jnp.where(odd, pltpu.roll(part, 64, 1), part)
-        u_next[c, f] = part[0:4, 0:64]
+    block, half, odd = place[0] // 4, place[0] // 2 % 2 == 1, place[0] % 2 == 1
+    for f in range(16):
+        quarters = [back[g, f].astype(F32) for g in range(4)]
+        for c in range(2):
+            quarter = [x[8 * c : 8 * c + 8] for x in quarters]
+            for q in range(4):
+                value = quarter[q]
+                if q:
+                    value = pltpu.roll(value, 128 - 8 * q, 1)
+                if q < 3:
+                    value = jnp.where(
+                        lane < 120 - 8 * q, value, pltpu.roll(quarter[q + 1], 120 - 8 * q, 1)
+                    )
+                width = 128 if q < 3 else 96
+                v_next[c, f, :, 128 * q : 128 * q + width] = value[0:4, 0:width]
+                m_next[c, f, :, 128 * q : 128 * q + width] = value[4:8, 0:width]
+            every = u[2 * f + c].astype(F32)
+            part = every[0:8]
+            for b in range(1, 8):
+                part = jnp.where(block == b, every[8 * b : 8 * b + 8], part)
+            part = jnp.where(half, swap(part), part)
+            part = jnp.where(odd, pltpu.roll(part, 64, 1), part)
+            u_next[c, f] = (part * inverse)[0:4, 0:64]
 
 
 def transform_tables():
@@ -421,18 +409,11 @@
 
     packed, slots = call(
         pack_body,
-        [shape((32, 4, 1152), F32), shape((15,), jnp.int32)],
-        [SMEM, HBM, HBM, HBM],
-        [
-            SMEM((64,), jnp.int32),
-            SMEM((SLOTS,), jnp.int32),
-            VMEM(direction.shape, F32),
-            VMEM(data_vec.shape, F32),
-            VMEM(model.shape, F32),
-            pltpu.SemaphoreType.DMA((3,)),
-        ],
+        [shape((32, 4, 640), F32), shape((15,), jnp.int32)],
+        [SMEM, VMEM, VMEM],
+        [SMEM((64,), jnp.int32), SMEM((SLOTS,), jnp.int32)],
         [VMEM, SMEM],
-    )(tile_receiver_block, direction, data_vec, model)
+    )(tile_receiver_block, direction, data_vec)
     rows = exchange(packed, "tile")
     barrier = lax.optimization_barrier
     lanes = lane_tables(slots, tile_source_block, ranks)
@@ -445,13 +426,17 @@
         [SMEM, VMEM],
     )(ids, rows)
     x = exchange(picked, "tile")
-    (model_rows,) = call(model_body, [shape((128, 4, 128), F32)], [VMEM])(rows)
-    x, model_rows = barrier((x, model_rows))
+    model, data_rows = barrier((model, data_rows))
+    (model_parts,) = call(model_body, [shape((4, 32, 4, 128), F32)], [SMEM, VMEM])(g.reshape(1), model)
+    models = [model_parts[0]] + [
+        lax.ppermute(model_parts[d], "freq", [(i, (i + d) % 4) for i in range(4)]) for d in (1, 2, 3)
+    ]
+    x, models = barrier((x, models))
     parts = tile_products(lane_slot, lane_block, limits, x, v_factor, u_factor)
     parts = exchange(parts, "tile")
     residual, power = call(
         residual_body,
-        [shape((32, 80, 128), BF16), shape((8, 128), F32)],
+        [shape((32, 64, 128), BF16), shape((8, 128), F32)],
         [SMEM, VMEM, VMEM],
     )(alpha.reshape(1), parts, data_rows)
     others = [lax.ppermute(power, "freq", [(i, (i + d) % 4) for i in range(4)]) for d in (1, 2, 3)]
@@ -462,10 +447,10 @@
     back = exchange(back, "tile")
     raw, beta = call(
         update_body,
-        [shape((128, 8, 128), F32), shape((8, 128), F32)],
-        [SMEM, VMEM, VMEM, VMEM],
+        [shape((128, 4, 128), F32), shape((8, 128), F32)],
+        [SMEM, VMEM, VMEM],
         [VMEM((64, 8, 128), F32)],
-    )(ids, back, direction_rows, model_rows)
+    )(ids, back, direction_rows)
     raw = exchange(raw, both)
 
     lo = lax.dynamic_slice_in_dim(time_lo, g * 120, 120, 0)
@@ -473,10 +458,13 @@
     lo = jnp.pad(lo, (0, 8)).reshape(1, 128)
     hi = jnp.pad(hi, (0, 8)).reshape(1, 128)
     tables = [jnp.asarray(a) for a in transform_tables()]
-    (shrunk,) = call(shrink_body, [shape((128, 8, 128), F32)], [VMEM] * 7)(
-        raw, lo, hi, *tables
-    )
-    shrunk = exchange(shrunk, "freq").reshape(4, 32, 8, 128)
+    (shrunk,) = call(
+        shrink_body,
+        [shape((WINDOW_FREQS, 16, 128), BF16)],
+        [SMEM] + [VMEM] * 11,
+        [VMEM((128, 4, 128), F32), VMEM((128, 8, 128), F32)],
+    )(g.reshape(1), raw, *models, lo, hi, *tables)
+    shrunk = exchange(shrunk, "freq").reshape(4, 16, 16, 128)
     return call(
         finish_body,
         [
@@ -485,7 +473,7 @@
             shape(direction.shape, F32),
         ],
         [SMEM, VMEM, VMEM, VMEM],
-    )((place % 2).reshape(1), beta, shrunk, u_all)
+    )(place.reshape(1), beta, shrunk, u_all)
 
 
 def solution(mesh):

time: 154 us -> 145 us (0.942)
  waiting for transfers between devices: 59.2 us -> 45.1 us
  starting transfers between devices: 37.4 us -> 42.7 us
    all_to_all x6, waiting for transfers between devices: 56.6 us -> 38.7 us  [exchange(): return lax.all_to_all(x, axis, split_axis=0, concat_axis=0, tiled=True)]
    ppermute x0 -> x3, starting transfers between devices: none -> 6.58 us  [on_device(): lax.ppermute(model_parts[d], 'freq', [(i, (i + d) % 4) for i in range(4)])]
    ppermute x0 -> x3, waiting for transfers between devices: none -> 3.26 us  [on_device(): lax.ppermute(model_parts[d], 'freq', [(i, (i + d) % 4) for i in range(4)])]
    ppermute x3, starting transfers between devices: 6.58 us -> 4.2 us  [on_device(): lax.ppermute(power, 'freq', [(i, (i + d) % 4) for i in range(4)])]
  transfers between devices with their start and end apart: 9 -> 12, of which waited for: 8 -> 12; matrix products, arithmetic and copies ran while one was open for 1% -> 1% of each run, Pallas kernels for 1% -> 1%
where the time goes in v3:
time: 145 us; the launch traced here: 144 us
  waiting for transfers between devices  45.1 us (31%)
  starting transfers between devices  42.7 us (29%)
  Pallas kernels  33.9 us (23%)
  blocking collectives  15 us (10%)
  local copies, waits for them, and re-layouts  4.87 us (3%)
  between operations  1.48 us (1%)
    all_to_all x6, waiting for transfers between devices, exchange(): return lax.all_to_all(x, axis, split_axis=0, concat_axis=0, tiled=True)  38.7 us
    all_to_all x6, starting transfers between devices, exchange(): return lax.all_to_all(x, axis, split_axis=0, concat_axis=0, tiled=True)  32 us
    pallas_call x2, Pallas kernels, tile_products(): pl.pallas_call(functools.partial(tiles_body, bool(extra)), grid=(freqs //...  22.2 us
    all_to_all x1, blocking collectives, exchange(): return lax.all_to_all(x, axis, split_axis=0, concat_axis=0, tiled=True)  15 us
    ppermute x3, starting transfers between devices, on_device(): lax.ppermute(model_parts[d], 'freq', [(i, (i + d) % 4) for i in range(4)])  6.58 us
    unnamed x20, local copies, waits for them, and re-layouts  4.76 us
    ppermute x3, starting transfers between devices, on_device(): lax.ppermute(power, 'freq', [(i, (i + d) % 4) for i in range(4)])  4.2 us
    ppermute x3, waiting for transfers between devices, on_device(): lax.ppermute(model_parts[d], 'freq', [(i, (i + d) % 4) for i in range(4)])  3.26 us
  transfers between devices with their start and end apart: 12, of which 12 were waited for; matrix products, arithmetic and copies ran while one was open for 1% of the time, Pallas kernels for 1%

profile of v3, /device:TPU:0, one launch (start us, length us, event | category | flops | bytes accessed | tf_op | source)
XLA Modules:
  0.0 143.9 jit_solution(2191358929317538637)
XLA Ops:
  3.1 1.8 %shard_map.166 = (f32[32,4,640]{2,1,0:T(4,128)}, s32[15]{0:T(128)S(1)}) custom-call(s32[15]{0:T(128)S(1)} %copy-done.8, f32[2,16,4,480]{3,2,1,0:T(4,128)S(1)} %copy-done, f32[2,16,4,64]{3,2,1,0:T(4,128)S(1)} %copy-done.6), custom_call_target="tpu_custom_call" | custom-call | tf_op jit(solution)/shard_map/pallas_call | solution.py:410
  4.9 7.4 %all-to-all-start = ((f32[32,4,640]{2,1,0:T(4,128)}), f32[32,4,640]{2,1,0:T(4,128)S(1)}, u32[]{:S(2)}, u32[]{:S(2)}) async-start(f32[32,4,640]{2,1,0:T(4,128)} %get-tuple-element.26), calls=%async_computation | async-start | bytes 655360 | tf_op jit(solution)/shard_map/all_to_all | solution.py:408
  14.4 7.4 %all-to-all-done.rows = f32[32,4,640]{2,1,0:T(4,128)S(1)} async-done(((f32[32,4,640]{2,1,0:T(4,128)}), f32[32,4,640]{2,1,0:T(4,128)S(1)}, u32[]{:S(2)}, u32[]{:S(2)}) %all-to-all-start) | async-done | bytes 327712 | tf_op jit(solution)/shard_map/all_to_all | solution.py:408
  21.9 2.0 %shard_map.168 = (bf16[32,64,128]{2,1,0:T(8,128)(2,1)}, f32[60,8,128]{2,1,0:T(8,128)S(1)}, f32[8,8,128]{2,1,0:T(8,128)S(1)}) custom-call(s32[32,8]{1,0:T(8,128)S(1)} %convert_bitcast_fusion.ids, f32[32,4,640]{2,1,0:T(4,128)S(1)} %all-to-all-done.rows), custom_call_target="tpu_custom_call" | custom-call | tf_op jit(solution)/shard_map/pallas_call | solution.py:423
  23.9 3.9 %all-to-all-start.1 = ((bf16[32,64,128]{2,1,0:T(8,128)(2,1)}), bf16[32,64,128]{2,1,0:T(8,128)(2,1)S(1)}, u32[]{:S(2)}, u32[]{:S(2)}) async-start(bf16[32,64,128]{2,1,0:T(8,128)(2,1)} %get-tuple-element.35), calls=%async_computation.1 | async-start | bytes 1048576 | tf_op jit(solution)/shard_map/all_to_all | solution.py:408
  28.9 2.0 %collective-permute-start = (f32[32,4,128]{2,1,0:T(4,128)S(1)}, f32[32,4,128]{2,1,0:T(4,128)S(1)}, u32[]{:S(2)}, u32[]{:S(2)}) collective-permute-start(f32[32,4,128]{2,1,0:T(4,128)S(1)} %get-tuple-element.53), channel_id=1, source_target_pairs={{0,32},{32,64},{64,96},{96,0},{1,33},{33,65},{65,97},{97,1},{2,34}... | collective-permute-start | bytes 196616 | tf_op jit(solution)/shard_map/ppermute | solution.py:432
  30.9 3.6 %collective-permute-start.1 = (f32[32,4,128]{2,1,0:T(4,128)S(1)}, f32[32,4,128]{2,1,0:T(4,128)S(1)}, u32[]{:S(2)}, u32[]{:S(2)}) collective-permute-start(f32[32,4,128]{2,1,0:T(4,128)S(1)} %get-tuple-element.52), channel_id=1, source_target_pairs={{0,64},{32,96},{64,0},{96,32},{1,65},{33,97},{65,1},{97,33},{2,66}... | collective-permute-start | bytes 196616 | tf_op jit(solution)/shard_map/ppermute | solution.py:432
  34.5 1.0 collective-permute-start.2
  35.6 2.6 %collective-permute-done.1.m2 = f32[32,4,128]{2,1,0:T(4,128)S(1)} collective-permute-done((f32[32,4,128]{2,1,0:T(4,128)S(1)}, f32[32,4,128]{2,1,0:T(4,128)S(1)}, u32[]{:S(2)}, u32[]{:S(2)}) %collective-permute-start.1) | collective-permute-done | bytes 65568 | tf_op jit(solution)/shard_map/ppermute | solution.py:432
  39.0 11.4 %shard_map.170 = bf16[32,64,128]{2,1,0:T(8,128)(2,1)} custom-call(s32[8,720]{1,0:T(8,128)S(1)} %get-tuple-element.33.lane_in.lane_out, s32[8,720]{1,0:T(8,128)S(1)} %get-tuple-element.32.lane_out.lane_in, s32[16,720]{1,0:T(8,128)S(1)} %get-tuple-element.34.limits, bf16[32,64,128]{2,1,0:T(8,128)(2,1)S(1)} %all-to-all-done.1.x, ...), custom_call_target="tpu_custom_call" | custom-call | tf_op jit(solution)/shard_map/pallas_call | solution.py:237
  50.4 7.2 %all-to-all-start.2 = ((bf16[32,64,128]{2,1,0:T(8,128)(2,1)}), bf16[32,64,128]{2,1,0:T(8,128)(2,1)S(1)}, u32[]{:S(2)}, u32[]{:S(2)}) async-start(bf16[32,64,128]{2,1,0:T(8,128)(2,1)} %shard_map.170), calls=%async_computation.2 | async-start | bytes 1048576 | tf_op jit(solution)/shard_map/all_to_all | solution.py:408
  58.3 10.5 %all-to-all-done.2.parts = bf16[32,64,128]{2,1,0:T(8,128)(2,1)S(1)} async-done(((bf16[32,64,128]{2,1,0:T(8,128)(2,1)}), bf16[32,64,128]{2,1,0:T(8,128)(2,1)S(1)}, u32[]{:S(2)}, u32[]{:S(2)}) %all-to-all-start.2) | async-done | bytes 524320 | tf_op jit(solution)/shard_map/all_to_all | solution.py:408
  69.7 4.1 %all-to-all-start.3 = ((bf16[32,64,128]{2,1,0:T(8,128)(2,1)}), bf16[32,64,128]{2,1,0:T(8,128)(2,1)S(1)}, u32[]{:S(2)}, u32[]{:S(2)}) async-start(bf16[32,64,128]{2,1,0:T(8,128)(2,1)} %get-tuple-element.40), calls=%async_computation.3 | async-start | bytes 1048576 | tf_op jit(solution)/shard_map/all_to_all | solution.py:408
  74.3 3.2 %collective-permute-start.4 = (f32[8,128]{1,0:T(8,128)S(1)}, f32[8,128]{1,0:T(8,128)S(1)}, u32[]{:S(2)}, u32[]{:S(2)}) collective-permute-start(f32[8,128]{1,0:T(8,128)S(1)} %get-tuple-element.41.own), channel_id=1, source_target_pairs={{0,64},{32,96},{64,0},{96,32},{1,65},{33,97},{65,1},{97,33},{2,66}... | collective-permute-start | bytes 12296 | tf_op jit(solution)/shard_map/ppermute | solution.py:442
  79.4 1.7 %collective-permute-done.5.p3 = f32[8,128]{1,0:T(8,128)S(1)} collective-permute-done((f32[8,128]{1,0:T(8,128)S(1)}, f32[8,128]{1,0:T(8,128)S(1)}, u32[]{:S(2)}, u32[]{:S(2)}) %collective-permute-start.5) | collective-permute-done | bytes 4128 | tf_op jit(solution)/shard_map/ppermute | solution.py:442
  81.2 3.8 %all-to-all-done.3.x.u = bf16[32,64,128]{2,1,0:T(8,128)(2,1)S(1)} async-done(((bf16[32,64,128]{2,1,0:T(8,128)(2,1)}), bf16[32,64,128]{2,1,0:T(8,128)(2,1)S(1)}, u32[]{:S(2)}, u32[]{:S(2)}) %all-to-all-start.3) | async-done | bytes 524320 | tf_op jit(solution)/shard_map/all_to_all | solution.py:408
  85.0 10.7 %shard_map.173 = bf16[32,64,128]{2,1,0:T(8,128)(2,1)S(1)} custom-call(s32[8,720]{1,0:T(8,128)S(1)} %get-tuple-element.32.lane_out.lane_in, s32[8,720]{1,0:T(8,128)S(1)} %get-tuple-element.33.lane_in.lane_out, s32[16,720]{1,0:T(8,128)S(1)} %get-tuple-element.34.limits, bf16[32,64,128]{2,1,0:T(8,128)(2,1)S(1)} %all-to-all-done.3.x.u, ...), custom_call_target="tpu_custom_call" | custom-call | tf_op jit(solution)/shard_map/pallas_call | solution.py:237
  95.7 15.0 %all_to_all.35.parts = bf16[32,64,128]{2,1,0:T(8,128)(2,1)S(1)} all-to-all(bf16[32,64,128]{2,1,0:T(8,128)(2,1)S(1)} %shard_map.173), channel_id=1, replica_groups=mesh['freq'=4,'tile'=32] {'tile'}, dimensions={0} | all-to-all | bytes 1048576 | tf_op jit(solution)/shard_map/all_to_all | solution.py:408
  110.7 2.5 %shard_map.174 = (f32[128,4,128]{2,1,0:T(4,128)}, f32[8,128]{1,0:T(8,128)S(1)}) custom-call(s32[32,8]{1,0:T(8,128)S(1)} %convert_bitcast_fusion.ids, bf16[32,64,128]{2,1,0:T(8,128)(2,1)S(1)} %all_to_all.35.parts, f32[60,8,128]{2,1,0:T(8,128)S(1)} %get-tuple-element.42.direction), custom_call_target="tpu_custom_call" | custom-call | tf_op jit(solution)/shard_map/pallas_call | solution.py:448
  113.2 6.0 %all-to-all-start.5 = ((f32[128,4,128]{2,1,0:T(4,128)}), f32[128,4,128]{2,1,0:T(4,128)S(1)}, u32[]{:S(2)}, u32[]{:S(2)}) async-start(f32[128,4,128]{2,1,0:T(4,128)} %get-tuple-element.44), calls=%async_computation.5 | async-start | bytes 524288 | tf_op jit(solution)/shard_map/all_to_all | solution.py:408
  120.0 9.9 %all-to-all-done.5.raw = f32[128,4,128]{2,1,0:T(4,128)S(1)} async-done(((f32[128,4,128]{2,1,0:T(4,128)}), f32[128,4,128]{2,1,0:T(4,128)S(1)}, u32[]{:S(2)}, u32[]{:S(2)}) %all-to-all-start.5) | async-done | bytes 262176 | tf_op jit(solution)/shard_map/all_to_all | solution.py:408
  130.0 2.6 %shard_map.175 = bf16[64,16,128]{2,1,0:T(8,128)(2,1)} custom-call(s32[1]{0:T(128)} %bitcast.3.group, f32[128,4,128]{2,1,0:T(4,128)S(1)} %all-to-all-done.5.raw, f32[32,4,128]{2,1,0:T(4,128)S(1)} %get-tuple-element.45.m0, f32[32,4,128]{2,1,0:T(4,128)S(1)} %collective-permute-done.m1, f32[32,4,128]{2,1,0:T(4,128)S(1)} %collective-permute-done.1.m2, ...), custom_call_target="tpu_custom_call" | custom-call | tf_op jit(solution)/shard_map/pallas_call | solution.py:461
  132.6 3.4 %all-to-all-start.6 = ((bf16[64,16,128]{2,1,0:T(8,128)(2,1)}), bf16[64,16,128]{2,1,0:T(8,128)(2,1)S(1)}, u32[]{:S(2)}, u32[]{:S(2)}) async-start(bf16[64,16,128]{2,1,0:T(8,128)(2,1)} %shard_map.175), calls=%async_computation.6 | async-start | bytes 524288 | tf_op jit(solution)/shard_map/all_to_all | solution.py:408
  136.0 6.9 %all-to-all-done.6 = bf16[64,16,128]{2,1,0:T(8,128)(2,1)S(1)} async-done(((bf16[64,16,128]{2,1,0:T(8,128)(2,1)}), bf16[64,16,128]{2,1,0:T(8,128)(2,1)S(1)}, u32[]{:S(2)}, u32[]{:S(2)}) %all-to-all-start.6) | async-done | bytes 262176 | tf_op jit(solution)/shard_map/all_to_all | solution.py:408
  (37 shorter events, 11.7 us)
Async XLA Ops:
  0.6 1.0 copy-start
  1.6 0.8 copy-start.6
  2.4 0.7 copy-start.8
  4.9 16.8 %all-to-all-start = ((f32[32,4,640]{2,1,0:T(4,128)}), f32[32,4,640]{2,1,0:T(4,128)S(1)}, u32[]{:S(2)}, u32[]{:S(2)}) async-start(f32[32,4,640]{2,1,0:T(4,128)} %get-tuple-element.26), calls=%async_computation | async-start | bytes 655360 | tf_op jit(solution)/shard_map/all_to_all | solution.py:408
  12.3 0.7 copy-start.7
  13.0 0.7 copy-start.9
  23.9 15.1 %all-to-all-start.1 = ((bf16[32,64,128]{2,1,0:T(8,128)(2,1)}), bf16[32,64,128]{2,1,0:T(8,128)(2,1)S(1)}, u32[]{:S(2)}, u32[]{:S(2)}) async-start(bf16[32,64,128]{2,1,0:T(8,128)(2,1)} %get-tuple-element.35), calls=%async_computation.1 | async-start | bytes 1048576 | tf_op jit(solution)/shard_map/all_to_all | solution.py:408
  27.8 1.0 copy-start.1
  28.9 6.7 %collective-permute-start = (f32[32,4,128]{2,1,0:T(4,128)S(1)}, f32[32,4,128]{2,1,0:T(4,128)S(1)}, u32[]{:S(2)}, u32[]{:S(2)}) collective-permute-start(f32[32,4,128]{2,1,0:T(4,128)S(1)} %get-tuple-element.53), channel_id=1, source_target_pairs={{0,32},{32,64},{64,96},{96,0},{1,33},{33,65},{65,97},{97,1},{2,34}... | collective-permute-start | bytes 196616 | tf_op jit(solution)/shard_map/ppermute | solution.py:432
  30.9 7.2 %collective-permute-start.1 = (f32[32,4,128]{2,1,0:T(4,128)S(1)}, f32[32,4,128]{2,1,0:T(4,128)S(1)}, u32[]{:S(2)}, u32[]{:S(2)}) collective-permute-start(f32[32,4,128]{2,1,0:T(4,128)S(1)} %get-tuple-element.52), channel_id=1, source_target_pairs={{0,64},{32,96},{64,0},{96,32},{1,65},{33,97},{65,1},{97,33},{2,66}... | collective-permute-start | bytes 196616 | tf_op jit(solution)/shard_map/ppermute | solution.py:432
  34.5 4.3 %collective-permute-start.2 = (f32[32,4,128]{2,1,0:T(4,128)S(1)}, f32[32,4,128]{2,1,0:T(4,128)S(1)}, u32[]{:S(2)}, u32[]{:S(2)}) collective-permute-start(f32[32,4,128]{2,1,0:T(4,128)S(1)} %get-tuple-element.51), channel_id=1, source_target_pairs={{0,96},{32,0},{64,32},{96,64},{1,97},{33,1},{65,33},{97,65},{2,98}... | collective-permute-start | bytes 196616 | tf_op jit(solution)/shard_map/ppermute | solution.py:432
  50.4 18.4 %all-to-all-start.2 = ((bf16[32,64,128]{2,1,0:T(8,128)(2,1)}), bf16[32,64,128]{2,1,0:T(8,128)(2,1)S(1)}, u32[]{:S(2)}, u32[]{:S(2)}) async-start(bf16[32,64,128]{2,1,0:T(8,128)(2,1)} %shard_map.170), calls=%async_computation.2 | async-start | bytes 1048576 | tf_op jit(solution)/shard_map/all_to_all | solution.py:408
  69.7 15.3 %all-to-all-start.3 = ((bf16[32,64,128]{2,1,0:T(8,128)(2,1)}), bf16[32,64,128]{2,1,0:T(8,128)(2,1)S(1)}, u32[]{:S(2)}, u32[]{:S(2)}) async-start(bf16[32,64,128]{2,1,0:T(8,128)(2,1)} %get-tuple-element.40), calls=%async_computation.3 | async-start | bytes 1048576 | tf_op jit(solution)/shard_map/all_to_all | solution.py:408
  73.8 4.9 %collective-permute-start.3 = (f32[8,128]{1,0:T(8,128)S(1)}, f32[8,128]{1,0:T(8,128)S(1)}, u32[]{:S(2)}, u32[]{:S(2)}) collective-permute-start(f32[8,128]{1,0:T(8,128)S(1)} %get-tuple-element.41.own), channel_id=1, source_target_pairs={{0,32},{32,64},{64,96},{96,0},{1,33},{33,65},{65,97},{97,1},{2,34}... | collective-permute-start | bytes 12296 | tf_op jit(solution)/shard_map/ppermute | solution.py:442
  74.3 5.1 %collective-permute-start.4 = (f32[8,128]{1,0:T(8,128)S(1)}, f32[8,128]{1,0:T(8,128)S(1)}, u32[]{:S(2)}, u32[]{:S(2)}) collective-permute-start(f32[8,128]{1,0:T(8,128)S(1)} %get-tuple-element.41.own), channel_id=1, source_target_pairs={{0,64},{32,96},{64,0},{96,32},{1,65},{33,97},{65,1},{97,33},{2,66}... | collective-permute-start | bytes 12296 | tf_op jit(solution)/shard_map/ppermute | solution.py:442
  77.5 3.6 %collective-permute-start.5 = (f32[8,128]{1,0:T(8,128)S(1)}, f32[8,128]{1,0:T(8,128)S(1)}, u32[]{:S(2)}, u32[]{:S(2)}) collective-permute-start(f32[8,128]{1,0:T(8,128)S(1)} %get-tuple-element.41.own), channel_id=1, source_target_pairs={{0,96},{32,0},{64,32},{96,64},{1,97},{33,1},{65,33},{97,65},{2,98}... | collective-permute-start | bytes 12296 | tf_op jit(solution)/shard_map/ppermute | solution.py:442
  81.1 48.8 %copy-start.2 = (bf16[512,128]{1,0:T(8,128)(2,1)S(1)}, bf16[512,128]{1,0:T(8,128)(2,1)}, u32[]{:S(2)}) copy-start(bf16[512,128]{1,0:T(8,128)(2,1)} %constant.23.clone.fh) | copy-start | bytes 393220
  81.1 48.8 %copy-start.3 = (bf16[512,128]{1,0:T(8,128)(2,1)S(1)}, bf16[512,128]{1,0:T(8,128)(2,1)}, u32[]{:S(2)}) copy-start(bf16[512,128]{1,0:T(8,128)(2,1)} %constant.24.clone.fl) | copy-start | bytes 393220
  81.2 48.8 %copy-start.4 = (bf16[128,512]{1,0:T(8,128)(2,1)S(1)}, bf16[128,512]{1,0:T(8,128)(2,1)}, u32[]{:S(2)}) copy-start(bf16[128,512]{1,0:T(8,128)(2,1)} %constant.25.clone.bh) | copy-start | bytes 393220
  81.2 48.8 %copy-start.5 = (bf16[128,512]{1,0:T(8,128)(2,1)S(1)}, bf16[128,512]{1,0:T(8,128)(2,1)}, u32[]{:S(2)}) copy-start(bf16[128,512]{1,0:T(8,128)(2,1)} %constant.26.clone.bl) | copy-start | bytes 393220
  113.2 16.7 %all-to-all-start.5 = ((f32[128,4,128]{2,1,0:T(4,128)}), f32[128,4,128]{2,1,0:T(4,128)S(1)}, u32[]{:S(2)}, u32[]{:S(2)}) async-start(f32[128,4,128]{2,1,0:T(4,128)} %get-tuple-element.44), calls=%async_computation.5 | async-start | bytes 524288 | tf_op jit(solution)/shard_map/all_to_all | solution.py:408
  132.6 10.3 %all-to-all-start.6 = ((bf16[64,16,128]{2,1,0:T(8,128)(2,1)}), bf16[64,16,128]{2,1,0:T(8,128)(2,1)S(1)}, u32[]{:S(2)}, u32[]{:S(2)}) async-start(bf16[64,16,128]{2,1,0:T(8,128)(2,1)} %shard_map.175), calls=%async_computation.6 | async-start | bytes 524288 | tf_op jit(solution)/shard_map/all_to_all | solution.py:408

commit v4 on v3

--- a/solution.py
+++ b/solution.py
@@ -19,6 +19,7 @@
 NVS = 4
 SLOTS = 8
 GROUP = 4
+AHEAD = 2
 LEFT_COUNT = 2 * WINDOW_FREQS * NVS * 2048
 
 shrink_level = 0.5
@@ -85,26 +86,12 @@
             out[k, :, 512:576] = data[c, f]
 
 
-def model_body(group, model, out):
-    lane = iota((8, 128), 1)
-    for q in range(4):
-        d = lax.rem(q + 4 - group[0], 4)
-        for f in range(model.shape[1]):
-            lo = max(q - 1, 0) * 128
-            both = [model[c, f, :, lo : lo + (256 if 0 < q < 3 else 128 if q == 0 else 224)] for c in range(2)]
-            both = jnp.concatenate(both, axis=0)
-            if q == 0:
-                value = both
-            else:
-                if q == 3:
-                    both = jnp.concatenate([both, jnp.zeros((8, 32), F32)], axis=1)
-                value = jnp.where(
-                    lane < 8 * q,
-                    pltpu.roll(both[:, 0:128], 8 * q, 1),
-                    pltpu.roll(both[:, 128:256], 8 * q, 1),
-                )
-            out[d, 2 * f] = value[0:4]
-            out[d, 2 * f + 1] = value[4:8]
+def model_body(model, out):
+    for f in range(model.shape[1]):
+        for c in range(2):
+            rows = [model[c, f, :, 128 * q : 128 * q + 128] for q in range(3)]
+            rows.append(jnp.concatenate([model[c, f, :, 384:480], jnp.zeros((4, 32), F32)], axis=1))
+            out[2 * f + c] = jnp.concatenate(rows, axis=0).astype(BF16)
 
 
 def blocks_of(chunks, half):
@@ -167,8 +154,20 @@
     limit[...] = rank.astype(jnp.int32) + start
 
 
-def tiles_body(extra, lane_in, lane_out, limits, x, first, second, *refs):
-    rest, out = refs[:-1], refs[-1]
+def tiles_body(extra, lane_in, lane_out, limits, x, first_hbm, second_hbm, *refs):
+    rest, (out, first, second, sems) = refs[:-4], refs[-4:]
+    steps = first.shape[0] // GROUP
+
+    def copies(n):
+        span = pl.ds(n * GROUP, GROUP)
+        return [
+            pltpu.make_async_copy(source.at[span], target.at[span], sems.at[a, n])
+            for a, (source, target) in enumerate(((first_hbm, first), (second_hbm, second)))
+        ]
+
+    for n in range(AHEAD):
+        for copy in copies(n):
+            copy.start()
     tiles = first.shape[1]
     wide = RMAX * tiles
     low = low_rows()
@@ -199,7 +198,7 @@
         z = every[0:8]
         for m in range(1, SLOTS):
             z = jnp.where(source == m, every[8 * m : 8 * m + 8], z)
-        z = jnp.where(lane < limits[pl.ds(GROUP * pl.program_id(0) + f, 1)], z, 0.0)
+        z = jnp.where(lane < limits[pl.ds(f, 1)], z, 0.0)
         turn = pltpu.roll(z, 4, 0)
         turn = jnp.where(upper, -turn, turn)
         za = [jnp.where(target == m, z, 0.0) for m in range(SLOTS)]
@@ -219,8 +218,20 @@
         out[2 * f] = jnp.concatenate(real, axis=0).astype(out.dtype)
         out[2 * f + 1] = jnp.concatenate(imag, axis=0).astype(out.dtype)
 
-    for f in range(GROUP):
-        one(f)
+    def group(n, _):
+        for copy in copies(n):
+            copy.wait()
+
+        @pl.when(n + AHEAD < steps)
+        def _():
+            for copy in copies(n + AHEAD):
+                copy.start()
+
+        for f in range(GROUP):
+            one(n * GROUP + f)
+        return 0
+
+    lax.fori_loop(0, steps, group, 0)
 
 
 def lane_tables(slots, blocks, ranks):
@@ -231,25 +242,17 @@
 
 
 def tile_products(lane_in, lane_out, limits, x, first, second, *extra):
-    freqs, tiles = first.shape[0], first.shape[1]
-    whole = pl.BlockSpec(memory_space=VMEM)
-    factor = pl.BlockSpec((GROUP, tiles, 2, RMAX, TILE_EXTENT), lambda f: (f, 0, 0, 0, 0))
-    return pl.pallas_call(
+    return call(
         functools.partial(tiles_body, bool(extra)),
-        grid=(freqs // GROUP,),
-        out_shape=jax.ShapeDtypeStruct((2 * freqs, 64, 128), BF16),
-        in_specs=[
-            whole,
-            whole,
-            whole,
-            pl.BlockSpec((2 * GROUP, x.shape[1], 128), lambda f: (f, 0, 0)),
-            factor,
-            factor,
-        ]
-        + [whole] * len(extra),
-        out_specs=pl.BlockSpec((2 * GROUP, 64, 128), lambda f: (f, 0, 0)),
-        compiler_params=pltpu.CompilerParams(vmem_limit_bytes=TILES_LIMIT),
-    )(lane_in, lane_out, limits, x, first, second, *extra)
+        [jax.ShapeDtypeStruct((2 * first.shape[0], 64, 128), BF16)],
+        [VMEM] * 4 + [pltpu.HBM] * 2 + [VMEM] * len(extra),
+        [
+            VMEM(first.shape, BF16),
+            VMEM(second.shape, BF16),
+            pltpu.SemaphoreType.DMA((2, first.shape[0] // GROUP)),
+        ],
+        limit=TILES_LIMIT,
+    )(lane_in, lane_out, limits, x, first, second, *extra)[0]
 
 
 def residual_body(alpha, parts, data, out, power_out):
@@ -300,76 +303,92 @@
         chunks[2 * b + 1] = jnp.where(low, swap(head), tail)
     power = jnp.sum(jnp.sum(power, axis=0, keepdims=True), axis=1, keepdims=True)
     power = jnp.broadcast_to(power, (8, 128))
-    for d in range(64):
-        n, off = 120 * d // 128, 120 * d % 128
-        value = chunks[n]
-        if off:
-            value = pltpu.roll(value, 128 - off, 1)
-        if off > 8:
-            value = jnp.where(lane < 128 - off, value, pltpu.roll(chunks[n + 1], 128 - off, 1))
-        value = jnp.where(lane == 120, power, value)
-        j, g = d // 4, d % 4
-        out[32 * g + j] = value[0:4]
-        out[32 * g + j + 16] = value[4:8]
-
-
-def split_dot(a_high, a_low, b):
-    b_high = b.astype(BF16)
-    b_low = (b - b_high.astype(F32)).astype(BF16)
-    return (
-        jnp.dot(a_high, b_high, preferred_element_type=F32)
-        + jnp.dot(a_high, b_low, preferred_element_type=F32)
-        + jnp.dot(a_low, b_high, preferred_element_type=F32)
-    )
-
-
-def shrink_body(group, raw, m0, m1, m2, m3, lo, hi, fh, fl, bh, bl, out, model, both):
+    s1 = power.astype(BF16).astype(F32)
+    s2 = (power - s1).astype(BF16).astype(F32)
+    for j in range(16):
+        rows = []
+        for q in range(4):
+            n, off = 480 * j // 128 + q, 480 * j % 128
+            value = chunks[n]
+            if off:
+                value = pltpu.roll(value, 128 - off, 1)
+                if n + 1 < 60:
+                    after = pltpu.roll(chunks[n + 1], 128 - off, 1)
+                    value = jnp.where(lane < 128 - off, value, after)
+            rows.append(value)
+        last = jnp.where(lane < 96, rows[3], 0.0)
+        last = jnp.where(lane == 120, s1, jnp.where(lane == 121, s2, last))
+        rows[3] = jnp.where(lane == 122, power - s1 - s2, last)
+        first = [jnp.where(low, rows[q], swap(rows[q + 1])) for q in (0, 2)]
+        second = [jnp.where(low, swap(rows[q]), rows[q + 1]) for q in (0, 2)]
+        for d, value in ((j, first), (j + 16, second)):
+            value = jnp.concatenate(value, axis=0).astype(BF16)
+            for g in range(4):
+                out[32 * g + d] = value
+
+
+def halves(x):
+    high = x.astype(BF16)
+    return high, (x - high.astype(F32)).astype(BF16)
+
+
+def shrink_body(group, raw, m0, m1, m2, m3, lo, hi, fh, fl, bh, bl, v_next, m_next, wide, back):
+    g = group[0]
     for d, part in enumerate((m0, m1, m2, m3)):
-        source = lax.rem(group[0] + 4 - d, 4)
-        model[pl.ds(source * 32, 32)] = part[...]
+        source = lax.rem(g + 4 - d, 4)
+        wide[pl.ds(source * 32, 32)] = part[...].astype(F32)
     lane = iota((128, 128), 1)
     count = 2 * WINDOW_FREQS * NVS * RECEIVER_BLOCKS * TILE_EXTENT
-    sums = jnp.where(lane == 120, raw[:, 0, :], 0.0)
+    sums = raw[:, 0:16, :].astype(F32)[:, 12, :]
+    sums = jnp.where((lane >= 120) & (lane < 123), sums, 0.0)
     power = jnp.sum(jnp.sum(sums, axis=0, keepdims=True), axis=1, keepdims=True)
-    alpha = jnp.sqrt(power / count + eps)
+    inverse = 1.0 / jnp.sqrt(power / count + eps)
+    own = raw[pl.ds(g * 32, 32)].astype(F32) * inverse[None]
+    for k in range(32):
+        for q in range(4):
+            width = 128 if q < 3 else 96
+            at = slice(128 * q, 128 * q + width)
+            v_next[k % 2, k // 2, :, at] = own[k, 4 * q : 4 * q + 4, 0:width]
+    wide[...] = wide[...] + raw[...].astype(F32) * inverse[None]
     moment = iota((NT, 128), 0)
-    inside = (moment >= lo[...]) & (moment < hi[...])
-    for v in range(NVS):
-        step = raw[:, v, :] / alpha
-        both[:, v, :] = step
-        signal = split_dot(fh[...], fl[...], model[:, v, :] + step)
-        kept = signal - jnp.clip(signal, -shrink_level, shrink_level)
-        kept = jnp.where(inside, kept, 0.0)
-        both[:, NVS + v, :] = split_dot(bh[...], bl[...], kept)
-    out[...] = both[...].reshape(WINDOW_FREQS, 16, 128).astype(BF16)
-
-
-def finish_body(place, beta, back, u, u_next, v_next, m_next):
-    lane = iota((8, 128), 1)
+    table = jnp.concatenate([fh[...], fl[...]], axis=1)
+    at = pl.ds(pl.multiple_of(g * 32, 32), 32)
+    own_high, own_low = bh[at], bl[at]
+    own_both = jnp.concatenate([own_high, own_low], axis=0)
+    for q in range(4):
+        inside = (moment >= lo[q : q + 1]) & (moment < hi[q : q + 1])
+        inside = jnp.concatenate([inside, inside], axis=1)
+        for v in range(0, NVS, 2):
+            r = 4 * q + v
+            high, low = halves(jnp.concatenate([wide[:, r, :], wide[:, r + 1, :]], axis=1))
+            signal = jnp.dot(
+                table, jnp.concatenate([high, high], axis=0), preferred_element_type=F32
+            ) + jnp.dot(fh[...], low, preferred_element_type=F32)
+            kept = signal - jnp.clip(signal, -shrink_level, shrink_level)
+            high, low = halves(jnp.where(inside, kept, 0.0))
+            result = jnp.dot(own_both, high, preferred_element_type=F32)
+            result = result[0:32] + result[32:64]
+            result = result + jnp.dot(own_high, low, preferred_element_type=F32)
+            back[:, r, :] = result[:, 0:128]
+            back[:, r + 1, :] = result[:, 128:256]
+    for k in range(32):
+        for q in range(4):
+            width = 128 if q < 3 else 96
+            at = slice(128 * q, 128 * q + width)
+            m_next[k % 2, k // 2, :, at] = back[k, 4 * q : 4 * q + 4, 0:width]
+
+
+def data_body(place, beta, u, u_next):
     inverse = beta[...]
     block, half, odd = place[0] // 4, place[0] // 2 % 2 == 1, place[0] % 2 == 1
-    for f in range(16):
-        quarters = [back[g, f].astype(F32) for g in range(4)]
-        for c in range(2):
-            quarter = [x[8 * c : 8 * c + 8] for x in quarters]
-            for q in range(4):
-                value = quarter[q]
-                if q:
-                    value = pltpu.roll(value, 128 - 8 * q, 1)
-                if q < 3:
-                    value = jnp.where(
-                        lane < 120 - 8 * q, value, pltpu.roll(quarter[q + 1], 120 - 8 * q, 1)
-                    )
-                width = 128 if q < 3 else 96
-                v_next[c, f, :, 128 * q : 128 * q + width] = value[0:4, 0:width]
-                m_next[c, f, :, 128 * q : 128 * q + width] = value[4:8, 0:width]
-            every = u[2 * f + c].astype(F32)
-            part = every[0:8]
-            for b in range(1, 8):
-                part = jnp.where(block == b, every[8 * b : 8 * b + 8], part)
-            part = jnp.where(half, swap(part), part)
-            part = jnp.where(odd, pltpu.roll(part, 64, 1), part)
-            u_next[c, f] = (part * inverse)[0:4, 0:64]
+    for k in range(32):
+        every = u[k].astype(F32)
+        part = every[0:8]
+        for b in range(1, 8):
+            part = jnp.where(block == b, every[8 * b : 8 * b + 8], part)
+        part = jnp.where(half, swap(part), part)
+        part = jnp.where(odd, pltpu.roll(part, 64, 1), part)
+        u_next[k % 2, k // 2] = (part * inverse)[0:4, 0:64]
 
 
 def transform_tables():
@@ -427,12 +446,12 @@
     )(ids, rows)
     x = exchange(picked, "tile")
     model, data_rows = barrier((model, data_rows))
-    (model_parts,) = call(model_body, [shape((4, 32, 4, 128), F32)], [SMEM, VMEM])(g.reshape(1), model)
-    models = [model_parts[0]] + [
-        lax.ppermute(model_parts[d], "freq", [(i, (i + d) % 4) for i in range(4)]) for d in (1, 2, 3)
+    (own_model,) = call(model_body, [shape((32, 16, 128), BF16)], [VMEM])(model)
+    models = [own_model] + [
+        lax.ppermute(own_model, "freq", [(i, (i + d) % 4) for i in range(4)]) for d in (1, 2, 3)
     ]
-    x, models = barrier((x, models))
     parts = tile_products(lane_slot, lane_block, limits, x, v_factor, u_factor)
+    parts, models = barrier((parts, models))
     parts = exchange(parts, "tile")
     residual, power = call(
         residual_body,
@@ -447,33 +466,25 @@
     back = exchange(back, "tile")
     raw, beta = call(
         update_body,
-        [shape((128, 4, 128), F32), shape((8, 128), F32)],
+        [shape((128, 16, 128), BF16), shape((8, 128), F32)],
         [SMEM, VMEM, VMEM],
         [VMEM((64, 8, 128), F32)],
     )(ids, back, direction_rows)
     raw = exchange(raw, both)
 
-    lo = lax.dynamic_slice_in_dim(time_lo, g * 120, 120, 0)
-    hi = lo + lax.dynamic_slice_in_dim(time_len, g * 120, 120, 0)
-    lo = jnp.pad(lo, (0, 8)).reshape(1, 128)
-    hi = jnp.pad(hi, (0, 8)).reshape(1, 128)
+    (u_next,) = call(data_body, [shape(data_vec.shape, F32)], [SMEM, VMEM, VMEM])(
+        place.reshape(1), beta, u_all
+    )
+    lo = jnp.pad(time_lo, (0, 32)).reshape(4, 128)
+    hi = jnp.pad(time_lo + time_len, (0, 32)).reshape(4, 128)
     tables = [jnp.asarray(a) for a in transform_tables()]
-    (shrunk,) = call(
+    v_next, m_next = call(
         shrink_body,
-        [shape((WINDOW_FREQS, 16, 128), BF16)],
+        [shape(direction.shape, F32), shape(direction.shape, F32)],
         [SMEM] + [VMEM] * 11,
-        [VMEM((128, 4, 128), F32), VMEM((128, 8, 128), F32)],
+        [VMEM((128, 16, 128), F32), VMEM((32, 16, 128), F32)],
     )(g.reshape(1), raw, *models, lo, hi, *tables)
-    shrunk = exchange(shrunk, "freq").reshape(4, 16, 16, 128)
-    return call(
-        finish_body,
-        [
-            shape(data_vec.shape, F32),
-            shape(direction.shape, F32),
-            shape(direction.shape, F32),
-        ],
-        [SMEM, VMEM, VMEM, VMEM],
-    )(place.reshape(1), beta, shrunk, u_all)
+    return u_next, v_next, m_next
 
 
 def solution(mesh):

time: 145 us -> 136 us (0.938)
  waiting for transfers between devices: 45.1 us -> 38.7 us
  starting transfers between devices: 42.7 us -> 38.7 us
  blocking collectives: 15 us -> 16.7 us
    all_to_all x6 -> x5, starting transfers between devices: 32 us -> 25.6 us  [exchange(): return lax.all_to_all(x, axis, split_axis=0, concat_axis=0, tiled=True)]
    ppermute x3, waiting for transfers between devices: 3.26 us -> 0.01 us  [on_device(): lax.ppermute(own_model, 'freq', [(i, (i + d) % 4) for i in range(4)])]
    all_to_all x6 -> x5, waiting for transfers between devices: 38.7 us -> 36.1 us  [exchange(): return lax.all_to_all(x, axis, split_axis=0, concat_axis=0, tiled=True)]
    ppermute x3, starting transfers between devices: 4.2 us -> 6.58 us  [on_device(): lax.ppermute(power, 'freq', [(i, (i + d) % 4) for i in range(4)])]
    all_to_all x1, blocking collectives: 15 us -> 16.7 us  [exchange(): return lax.all_to_all(x, axis, split_axis=0, concat_axis=0, tiled=True)]
    unnamed x20 -> x24, local copies, waits for them, and re-layouts: 4.76 us -> 4.77 us
  transfers between devices with their start and end apart: 12 -> 11, of which waited for: 12 -> 7; matrix products, arithmetic and copies ran while one was open for 1% -> 0% of each run, Pallas kernels for 1% -> 9%
where the time goes in v4:
time: 136 us; the launch traced here: 135 us
  starting transfers between devices  38.7 us (28%)
  waiting for transfers between devices  38.7 us (28%)
  Pallas kernels  34.6 us (25%)
  blocking collectives  16.7 us (12%)
  local copies, waits for them, and re-layouts  4.86 us (4%)
  between operations  1.52 us (1%)
    all_to_all x5, waiting for transfers between devices, exchange(): return lax.all_to_all(x, axis, split_axis=0, concat_axis=0, tiled=True)  36.1 us
    all_to_all x5, starting transfers between devices, exchange(): return lax.all_to_all(x, axis, split_axis=0, concat_axis=0, tiled=True)  25.6 us
    pallas_call x2, Pallas kernels, tile_products(): call(functools.partial(tiles_body, bool(extra)), [jax.ShapeDtypeStruct((2...  20.3 us
    all_to_all x1, blocking collectives, exchange(): return lax.all_to_all(x, axis, split_axis=0, concat_axis=0, tiled=True)  16.7 us
    ppermute x3, starting transfers between devices, on_device(): lax.ppermute(power, 'freq', [(i, (i + d) % 4) for i in range(4)])  6.58 us
    ppermute x3, starting transfers between devices, on_device(): lax.ppermute(own_model, 'freq', [(i, (i + d) % 4) for i in range(4)])  6.58 us
    pallas_call x1, Pallas kernels, on_device(): call(shrink_body, [shape(direction.shape, F32), shape(direction.shape, F3...  5.32 us
    unnamed x24, local copies, waits for them, and re-layouts  4.77 us
  transfers between devices with their start and end apart: 11, of which 7 were waited for; matrix products, arithmetic and copies ran while one was open for 0% of the time, Pallas kernels for 9%

profile of v4, /device:TPU:0, one launch (start us, length us, event | category | flops | bytes accessed | tf_op | source)
XLA Modules:
  0.0 135.1 jit_solution(3643117373647785089)
XLA Ops:
  3.1 1.8 %shard_map.166 = (f32[32,4,640]{2,1,0:T(4,128)}, s32[15]{0:T(128)S(1)}) custom-call(s32[15]{0:T(128)S(1)} %copy-done.8, f32[2,16,4,480]{3,2,1,0:T(4,128)S(1)} %copy-done, f32[2,16,4,64]{3,2,1,0:T(4,128)S(1)} %copy-done.6), custom_call_target="tpu_custom_call" | custom-call | tf_op jit(solution)/shard_map/pallas_call | solution.py:429
  4.9 7.4 %all-to-all-start = ((f32[32,4,640]{2,1,0:T(4,128)}), f32[32,4,640]{2,1,0:T(4,128)S(1)}, u32[]{:S(2)}, u32[]{:S(2)}) async-start(f32[32,4,640]{2,1,0:T(4,128)} %get-tuple-element.28), calls=%async_computation | async-start | bytes 655360 | tf_op jit(solution)/shard_map/all_to_all | solution.py:427
  14.4 7.4 %all-to-all-done.rows = f32[32,4,640]{2,1,0:T(4,128)S(1)} async-done(((f32[32,4,640]{2,1,0:T(4,128)}), f32[32,4,640]{2,1,0:T(4,128)S(1)}, u32[]{:S(2)}, u32[]{:S(2)}) %all-to-all-start) | async-done | bytes 327712 | tf_op jit(solution)/shard_map/all_to_all | solution.py:427
  21.9 2.0 %shard_map.168 = (bf16[32,64,128]{2,1,0:T(8,128)(2,1)}, f32[60,8,128]{2,1,0:T(8,128)S(1)}, f32[8,8,128]{2,1,0:T(8,128)S(1)}) custom-call(s32[32,8]{1,0:T(8,128)S(1)} %convert_bitcast_fusion.ids, f32[32,4,640]{2,1,0:T(4,128)S(1)} %all-to-all-done.rows), custom_call_target="tpu_custom_call" | custom-call | tf_op jit(solution)/shard_map/pallas_call | solution.py:442
  23.9 3.9 %all-to-all-start.1 = ((bf16[32,64,128]{2,1,0:T(8,128)(2,1)}), bf16[32,64,128]{2,1,0:T(8,128)(2,1)S(1)}, u32[]{:S(2)}, u32[]{:S(2)}) async-start(bf16[32,64,128]{2,1,0:T(8,128)(2,1)} %get-tuple-element.37), calls=%async_computation.1 | async-start | bytes 1048576 | tf_op jit(solution)/shard_map/all_to_all | solution.py:427
  28.8 2.0 %collective-permute-start = (bf16[32,16,128]{2,1,0:T(8,128)(2,1)S(1)}, bf16[32,16,128]{2,1,0:T(8,128)(2,1)S(1)}, u32[]{:S(2)}, u32[]{:S(2)}) collective-permute-start(bf16[32,16,128]{2,1,0:T(8,128)(2,1)S(1)} %shard_map.170.m0), channel_id=1, source_target_pairs={{0,32},{32,64},{64,96},{96,0},{1,33},{33,65},{65,97},{97,1},{2,34}... | collective-permute-start | bytes 393224 | tf_op jit(solution)/shard_map/ppermute | solution.py:451
  30.8 3.6 %collective-permute-start.1 = (bf16[32,16,128]{2,1,0:T(8,128)(2,1)S(1)}, bf16[32,16,128]{2,1,0:T(8,128)(2,1)S(1)}, u32[]{:S(2)}, u32[]{:S(2)}) collective-permute-start(bf16[32,16,128]{2,1,0:T(8,128)(2,1)S(1)} %shard_map.170.m0), channel_id=1, source_target_pairs={{0,64},{32,96},{64,0},{96,32},{1,65},{33,97},{65,1},{97,33},{2,66}... | collective-permute-start | bytes 393224 | tf_op jit(solution)/shard_map/ppermute | solution.py:451
  34.4 1.0 collective-permute-start.2
  35.4 3.6 %all-to-all-done.1.x = bf16[32,64,128]{2,1,0:T(8,128)(2,1)S(1)} async-done(((bf16[32,64,128]{2,1,0:T(8,128)(2,1)}), bf16[32,64,128]{2,1,0:T(8,128)(2,1)S(1)}, u32[]{:S(2)}, u32[]{:S(2)}) %all-to-all-start.1) | async-done | bytes 524320 | tf_op jit(solution)/shard_map/all_to_all | solution.py:427
  39.0 10.6 %shard_map.169 = bf16[32,64,128]{2,1,0:T(8,128)(2,1)} custom-call(s32[8,720]{1,0:T(8,128)S(1)} %get-tuple-element.35.lane_in.lane_out, s32[8,720]{1,0:T(8,128)S(1)} %get-tuple-element.34.lane_out.lane_in, s32[16,720]{1,0:T(8,128)S(1)} %get-tuple-element.36.limits, bf16[32,64,128]{2,1,0:T(8,128)(2,1)S(1)} %all-to-all-done.1.x, ...), custom_call_target="tpu_custom_call" | custom-call | tf_op jit(solution)/shard_map/pallas_call | solution.py:245
  49.6 4.0 %all-to-all-start.2 = ((bf16[32,64,128]{2,1,0:T(8,128)(2,1)}), bf16[32,64,128]{2,1,0:T(8,128)(2,1)S(1)}, u32[]{:S(2)}, u32[]{:S(2)}) async-start(bf16[32,64,128]{2,1,0:T(8,128)(2,1)} %shard_map.169), calls=%async_computation.2 | async-start | bytes 1048576 | tf_op jit(solution)/shard_map/all_to_all | solution.py:427
  54.3 10.5 %all-to-all-done.2.parts = bf16[32,64,128]{2,1,0:T(8,128)(2,1)S(1)} async-done(((bf16[32,64,128]{2,1,0:T(8,128)(2,1)}), bf16[32,64,128]{2,1,0:T(8,128)(2,1)S(1)}, u32[]{:S(2)}, u32[]{:S(2)}) %all-to-all-start.2) | async-done | bytes 524320 | tf_op jit(solution)/shard_map/all_to_all | solution.py:427
  65.7 4.1 %all-to-all-start.3 = ((bf16[32,64,128]{2,1,0:T(8,128)(2,1)}), bf16[32,64,128]{2,1,0:T(8,128)(2,1)S(1)}, u32[]{:S(2)}, u32[]{:S(2)}) async-start(bf16[32,64,128]{2,1,0:T(8,128)(2,1)} %get-tuple-element.42), calls=%async_computation.3 | async-start | bytes 1048576 | tf_op jit(solution)/shard_map/all_to_all | solution.py:427
  69.8 2.0 %collective-permute-start.3 = (f32[8,128]{1,0:T(8,128)S(1)}, f32[8,128]{1,0:T(8,128)S(1)}, u32[]{:S(2)}, u32[]{:S(2)}) collective-permute-start(f32[8,128]{1,0:T(8,128)S(1)} %get-tuple-element.43.own), channel_id=1, source_target_pairs={{0,32},{32,64},{64,96},{96,0},{1,33},{33,65},{65,97},{97,1},{2,34}... | collective-permute-start | bytes 12296 | tf_op jit(solution)/shard_map/ppermute | solution.py:461
  71.8 3.6 %collective-permute-start.4 = (f32[8,128]{1,0:T(8,128)S(1)}, f32[8,128]{1,0:T(8,128)S(1)}, u32[]{:S(2)}, u32[]{:S(2)}) collective-permute-start(f32[8,128]{1,0:T(8,128)S(1)} %get-tuple-element.43.own), channel_id=1, source_target_pairs={{0,64},{32,96},{64,0},{96,32},{1,65},{33,97},{65,1},{97,33},{2,66}... | collective-permute-start | bytes 12296 | tf_op jit(solution)/shard_map/ppermute | solution.py:461
  75.4 1.0 collective-permute-start.5
  77.0 2.0 %collective-permute-done.5.p3 = f32[8,128]{1,0:T(8,128)S(1)} collective-permute-done((f32[8,128]{1,0:T(8,128)S(1)}, f32[8,128]{1,0:T(8,128)S(1)}, u32[]{:S(2)}, u32[]{:S(2)}) %collective-permute-start.5) | collective-permute-done | bytes 4128 | tf_op jit(solution)/shard_map/ppermute | solution.py:461
  79.1 1.9 %all-to-all-done.3.x.u = bf16[32,64,128]{2,1,0:T(8,128)(2,1)S(1)} async-done(((bf16[32,64,128]{2,1,0:T(8,128)(2,1)}), bf16[32,64,128]{2,1,0:T(8,128)(2,1)S(1)}, u32[]{:S(2)}, u32[]{:S(2)}) %all-to-all-start.3) | async-done | bytes 524320 | tf_op jit(solution)/shard_map/all_to_all | solution.py:427
  81.0 9.8 %shard_map.173 = bf16[32,64,128]{2,1,0:T(8,128)(2,1)S(1)} custom-call(s32[8,720]{1,0:T(8,128)S(1)} %get-tuple-element.34.lane_out.lane_in, s32[8,720]{1,0:T(8,128)S(1)} %get-tuple-element.35.lane_in.lane_out, s32[16,720]{1,0:T(8,128)S(1)} %get-tuple-element.36.limits, bf16[32,64,128]{2,1,0:T(8,128)(2,1)S(1)} %all-to-all-done.3.x.u, ...), custom_call_target="tpu_custom_call" | custom-call | tf_op jit(solution)/shard_map/pallas_call | solution.py:245
  90.7 16.7 %all_to_all.30.parts = bf16[32,64,128]{2,1,0:T(8,128)(2,1)S(1)} all-to-all(bf16[32,64,128]{2,1,0:T(8,128)(2,1)S(1)} %shard_map.173), channel_id=1, replica_groups=mesh['freq'=4,'tile'=32] {'tile'}, dimensions={0} | all-to-all | bytes 1048576 | tf_op jit(solution)/shard_map/all_to_all | solution.py:427
  107.4 2.7 %shard_map.174 = (bf16[128,16,128]{2,1,0:T(8,128)(2,1)}, f32[8,128]{1,0:T(8,128)S(1)}) custom-call(s32[32,8]{1,0:T(8,128)S(1)} %convert_bitcast_fusion.ids, bf16[32,64,128]{2,1,0:T(8,128)(2,1)S(1)} %all_to_all.30.parts, f32[60,8,128]{2,1,0:T(8,128)S(1)} %get-tuple-element.44.direction), custom_call_target="tpu_custom_call" | custom-call | tf_op jit(solution)/shard_map/pallas_call | solution.py:467
  110.1 6.2 %all-to-all-start.5 = ((bf16[128,16,128]{2,1,0:T(8,128)(2,1)}), bf16[128,16,128]{2,1,0:T(8,128)(2,1)S(1)}, u32[]{:S(2)}, u32[]{:S(2)}) async-start(bf16[128,16,128]{2,1,0:T(8,128)(2,1)} %get-tuple-element.46), calls=%async_computation.5 | async-start | bytes 1048576 | tf_op jit(solution)/shard_map/all_to_all | solution.py:427
  117.1 12.7 %all-to-all-done.5.raw = bf16[128,16,128]{2,1,0:T(8,128)(2,1)S(1)} async-done(((bf16[128,16,128]{2,1,0:T(8,128)(2,1)}), bf16[128,16,128]{2,1,0:T(8,128)(2,1)S(1)}, u32[]{:S(2)}, u32[]{:S(2)}) %all-to-all-start.5) | async-done | bytes 524320 | tf_op jit(solution)/shard_map/all_to_all | solution.py:427
  129.8 5.3 %shard_map.176 = (f32[2,16,4,480]{3,2,1,0:T(4,128)}, f32[2,16,4,480]{3,2,1,0:T(4,128)}) custom-call(s32[1]{0:T(128)} %bitcast.3.group, bf16[128,16,128]{2,1,0:T(8,128)(2,1)S(1)} %all-to-all-done.5.raw, bf16[32,16,128]{2,1,0:T(8,128)(2,1)S(1)} %shard_map.170.m0, bf16[32,16,128]{2,1,0:T(8,128)(2,1)S(1)} %collective-permute-done.m1, ...), custom_call_target="tpu_custom_call" | custom-call | tf_op jit(solution)/shard_map/pallas_call | solution.py:481
  (38 shorter events, 7.9 us)
Async XLA Ops:
  0.6 1.0 copy-start
  1.6 0.8 copy-start.6
  2.4 0.7 copy-start.8
  4.9 16.8 %all-to-all-start = ((f32[32,4,640]{2,1,0:T(4,128)}), f32[32,4,640]{2,1,0:T(4,128)S(1)}, u32[]{:S(2)}, u32[]{:S(2)}) async-start(f32[32,4,640]{2,1,0:T(4,128)} %get-tuple-element.28), calls=%async_computation | async-start | bytes 655360 | tf_op jit(solution)/shard_map/all_to_all | solution.py:427
  12.3 0.7 copy-start.7
  13.0 0.7 copy-start.9
  23.9 15.1 %all-to-all-start.1 = ((bf16[32,64,128]{2,1,0:T(8,128)(2,1)}), bf16[32,64,128]{2,1,0:T(8,128)(2,1)S(1)}, u32[]{:S(2)}, u32[]{:S(2)}) async-start(bf16[32,64,128]{2,1,0:T(8,128)(2,1)} %get-tuple-element.37), calls=%async_computation.1 | async-start | bytes 1048576 | tf_op jit(solution)/shard_map/all_to_all | solution.py:427
  27.8 1.0 copy-start.1
  28.8 20.8 %collective-permute-start = (bf16[32,16,128]{2,1,0:T(8,128)(2,1)S(1)}, bf16[32,16,128]{2,1,0:T(8,128)(2,1)S(1)}, u32[]{:S(2)}, u32[]{:S(2)}) collective-permute-start(bf16[32,16,128]{2,1,0:T(8,128)(2,1)S(1)} %shard_map.170.m0), channel_id=1, source_target_pairs={{0,32},{32,64},{64,96},{96,0},{1,33},{33,65},{65,97},{97,1},{2,34}... | collective-permute-start | bytes 393224 | tf_op jit(solution)/shard_map/ppermute | solution.py:451
  30.8 18.8 %collective-permute-start.1 = (bf16[32,16,128]{2,1,0:T(8,128)(2,1)S(1)}, bf16[32,16,128]{2,1,0:T(8,128)(2,1)S(1)}, u32[]{:S(2)}, u32[]{:S(2)}) collective-permute-start(bf16[32,16,128]{2,1,0:T(8,128)(2,1)S(1)} %shard_map.170.m0), channel_id=1, source_target_pairs={{0,64},{32,96},{64,0},{96,32},{1,65},{33,97},{65,1},{97,33},{2,66}... | collective-permute-start | bytes 393224 | tf_op jit(solution)/shard_map/ppermute | solution.py:451
  34.4 15.2 %collective-permute-start.2 = (bf16[32,16,128]{2,1,0:T(8,128)(2,1)S(1)}, bf16[32,16,128]{2,1,0:T(8,128)(2,1)S(1)}, u32[]{:S(2)}, u32[]{:S(2)}) collective-permute-start(bf16[32,16,128]{2,1,0:T(8,128)(2,1)S(1)} %shard_map.170.m0), channel_id=1, source_target_pairs={{0,96},{32,0},{64,32},{96,64},{1,97},{33,1},{65,33},{97,65},{2,98}... | collective-permute-start | bytes 393224 | tf_op jit(solution)/shard_map/ppermute | solution.py:451
  49.6 15.2 %all-to-all-start.2 = ((bf16[32,64,128]{2,1,0:T(8,128)(2,1)}), bf16[32,64,128]{2,1,0:T(8,128)(2,1)S(1)}, u32[]{:S(2)}, u32[]{:S(2)}) async-start(bf16[32,64,128]{2,1,0:T(8,128)(2,1)} %shard_map.169), calls=%async_computation.2 | async-start | bytes 1048576 | tf_op jit(solution)/shard_map/all_to_all | solution.py:427
  65.7 15.3 %all-to-all-start.3 = ((bf16[32,64,128]{2,1,0:T(8,128)(2,1)}), bf16[32,64,128]{2,1,0:T(8,128)(2,1)S(1)}, u32[]{:S(2)}, u32[]{:S(2)}) async-start(bf16[32,64,128]{2,1,0:T(8,128)(2,1)} %get-tuple-element.42), calls=%async_computation.3 | async-start | bytes 1048576 | tf_op jit(solution)/shard_map/all_to_all | solution.py:427
  69.8 6.6 %collective-permute-start.3 = (f32[8,128]{1,0:T(8,128)S(1)}, f32[8,128]{1,0:T(8,128)S(1)}, u32[]{:S(2)}, u32[]{:S(2)}) collective-permute-start(f32[8,128]{1,0:T(8,128)S(1)} %get-tuple-element.43.own), channel_id=1, source_target_pairs={{0,32},{32,64},{64,96},{96,0},{1,33},{33,65},{65,97},{97,1},{2,34}... | collective-permute-start | bytes 12296 | tf_op jit(solution)/shard_map/ppermute | solution.py:461
  71.8 5.2 %collective-permute-start.4 = (f32[8,128]{1,0:T(8,128)S(1)}, f32[8,128]{1,0:T(8,128)S(1)}, u32[]{:S(2)}, u32[]{:S(2)}) collective-permute-start(f32[8,128]{1,0:T(8,128)S(1)} %get-tuple-element.43.own), channel_id=1, source_target_pairs={{0,64},{32,96},{64,0},{96,32},{1,65},{33,97},{65,1},{97,33},{2,66}... | collective-permute-start | bytes 12296 | tf_op jit(solution)/shard_map/ppermute | solution.py:461
  75.4 3.6 %collective-permute-start.5 = (f32[8,128]{1,0:T(8,128)S(1)}, f32[8,128]{1,0:T(8,128)S(1)}, u32[]{:S(2)}, u32[]{:S(2)}) collective-permute-start(f32[8,128]{1,0:T(8,128)S(1)} %get-tuple-element.43.own), channel_id=1, source_target_pairs={{0,96},{32,0},{64,32},{96,64},{1,97},{33,1},{65,33},{97,65},{2,98}... | collective-permute-start | bytes 12296 | tf_op jit(solution)/shard_map/ppermute | solution.py:461
  79.0 37.3 %copy-start.10 = (s32[480]{0:T(512)S(1)}, s32[480]{0:T(512)}, u32[]{:S(2)}) copy-start(s32[480]{0:T(512)} %param.24) | copy-start | bytes 5764
  79.0 37.3 %copy-start.11 = (s32[480]{0:T(512)S(1)}, s32[480]{0:T(512)}, u32[]{:S(2)}) copy-start(s32[480]{0:T(512)} %param.25) | copy-start | bytes 5764
  79.0 50.8 %copy-start.2 = (bf16[512,128]{1,0:T(8,128)(2,1)S(1)}, bf16[512,128]{1,0:T(8,128)(2,1)}, u32[]{:S(2)}) copy-start(bf16[512,128]{1,0:T(8,128)(2,1)} %constant.19.clone.fh) | copy-start | bytes 393220
  79.0 50.8 %copy-start.3 = (bf16[512,128]{1,0:T(8,128)(2,1)S(1)}, bf16[512,128]{1,0:T(8,128)(2,1)}, u32[]{:S(2)}) copy-start(bf16[512,128]{1,0:T(8,128)(2,1)} %constant.20.clone.fl) | copy-start | bytes 393220
  79.0 50.8 %copy-start.4 = (bf16[128,512]{1,0:T(8,128)(2,1)S(1)}, bf16[128,512]{1,0:T(8,128)(2,1)}, u32[]{:S(2)}) copy-start(bf16[128,512]{1,0:T(8,128)(2,1)} %constant.21.clone.bh) | copy-start | bytes 393220
  79.0 50.8 %copy-start.5 = (bf16[128,512]{1,0:T(8,128)(2,1)S(1)}, bf16[128,512]{1,0:T(8,128)(2,1)}, u32[]{:S(2)}) copy-start(bf16[128,512]{1,0:T(8,128)(2,1)} %constant.22.clone.bl) | copy-start | bytes 393220
  110.1 19.7 %all-to-all-start.5 = ((bf16[128,16,128]{2,1,0:T(8,128)(2,1)}), bf16[128,16,128]{2,1,0:T(8,128)(2,1)S(1)}, u32[]{:S(2)}, u32[]{:S(2)}) async-start(bf16[128,16,128]{2,1,0:T(8,128)(2,1)} %get-tuple-element.46), calls=%async_computation.5 | async-start | bytes 1048576 | tf_op jit(solution)/shard_map/all_to_all | solution.py:427

commit v5 on v4

--- a/solution.py
+++ b/solution.py
@@ -57,7 +57,7 @@
     )
 
 
-def pack_body(rb, direction, data, out, slot_of, mark, ids):
+def pack_body(rb, direction, out, slot_of, mark, ids):
     def clear(b, _):
         mark[b] = -1
         return 0
@@ -77,13 +77,12 @@
     lane = iota((4, 128), 1)
     listed = jnp.zeros((4, 128), F32)
     for m in range(SLOTS):
-        listed = jnp.where(lane == 64 + m, ids[m].astype(F32), listed)
+        listed = jnp.where(lane == 96 + m, ids[m].astype(F32), listed)
     for f in range(direction.shape[1]):
         for c in range(2):
             k = 2 * f + c
+            out[k, :, 384:512] = listed
             out[k, :, 0:480] = direction[c, f]
-            out[k, :, 512:640] = listed
-            out[k, :, 512:576] = data[c, f]
 
 
 def model_body(model, out):
@@ -104,15 +103,14 @@
     return blocks
 
 
-def spread_body(ids, rows, out, direction, data):
-    lane = iota((8, 640), 1)
+def spread_body(ids, rows, data, out, direction):
+    lane = iota((8, 512), 1)
     chunks = [None] * 60
-    tails = []
+    empty = jnp.zeros((8, 128), F32)
     for j in range(16):
         both = jnp.concatenate([rows[j], rows[j + 16]], axis=0)
-        tails.append(both[:, 512:640])
         shift, first = 480 * j % 128, 480 * j // 128
-        moved = jnp.where(lane < 480, both, 0.0)
+        moved = jnp.concatenate([jnp.where(lane < 480, both, 0.0), empty], axis=1)
         if shift:
             moved = pltpu.roll(moved, shift, 1)
         for q in range((shift + 479) // 128 + 1):
@@ -121,20 +119,17 @@
             chunks[n] = piece if chunks[n] is None else chunks[n] + piece
     for b, block in enumerate(blocks_of(chunks, 30)):
         direction[b] = block
-    left = iota((8, 128), 1) < 64
-    ends = [jnp.where(left, tails[2 * n], pltpu.roll(tails[2 * n + 1], 64, 1)) for n in range(8)]
-    for b, block in enumerate(blocks_of(ends, 4)):
-        data[b] = block
 
     def one(i, _):
-        picked = [direction[ids[i, m]] for m in range(SLOTS)]
+        picked = [direction[ids[i, m]] for m in range(SLOTS - 1)]
+        picked.append(data[i])
         out[i] = jnp.concatenate(picked, axis=0).astype(BF16)
         return 0
 
     lax.fori_loop(0, 32, one, 0, unroll=4)
 
 
-def lanes_body(slots, blocks, ranks, lane_slot, lane_block, limit):
+def lanes_body(slots, blocks, ranks, data, lane_slot, lane_block, limit, data_rows):
     tiles = ranks.shape[1]
     wide = RMAX * tiles
     lane = iota((8, wide), 1)
@@ -152,6 +147,11 @@
     for t in range(1, tiles):
         start = jnp.where(lane >= RMAX * t, RMAX * t, start)
     limit[...] = rank.astype(jnp.int32) + start
+    for k in range(32):
+        own = data[k % 2, k // 2]
+        high = own.astype(BF16).astype(F32)
+        own = jnp.concatenate([high, own - high], axis=1)
+        data_rows[k] = jnp.concatenate([own, jnp.zeros((4, 128), F32)], axis=0)
 
 
 def tiles_body(extra, lane_in, lane_out, limits, x, first_hbm, second_hbm, *refs):
@@ -234,11 +234,14 @@
     lax.fori_loop(0, steps, group, 0)
 
 
-def lane_tables(slots, blocks, ranks):
+def lane_tables(slots, blocks, ranks, data):
     wide = RMAX * ranks.shape[1]
     table = jax.ShapeDtypeStruct((8, wide), jnp.int32)
     limit = jax.ShapeDtypeStruct((ranks.shape[0], wide), jnp.int32)
-    return call(lanes_body, [table, table, limit], [SMEM, SMEM, VMEM])(slots, blocks, ranks)
+    rows = jax.ShapeDtypeStruct((32, 8, 128), F32)
+    return call(lanes_body, [table, table, limit, rows], [SMEM, SMEM, VMEM, VMEM])(
+        slots, blocks, ranks, data
+    )
 
 
 def tile_products(lane_in, lane_out, limits, x, first, second, *extra):
@@ -255,11 +258,18 @@
     )(lane_in, lane_out, limits, x, first, second, *extra)[0]
 
 
-def residual_body(alpha, parts, data, out, power_out):
+def residual_body(alpha, parts, x, out, power_out):
     total = parts[0].astype(F32)
     for i in range(1, 32):
         total = total + parts[i].astype(F32)
-    u = total - alpha[0] * data[...].reshape(64, 128)
+    low, left = low_rows(), iota((8, 128), 1) < 64
+    data = []
+    for b in range(8):
+        shards = [x[4 * b + n].astype(F32)[56:64] for n in range(4)]
+        shards = [shard + pltpu.roll(shard, 64, 1) for shard in shards]
+        even, odd = jnp.where(left, shards[0], shards[1]), jnp.where(left, shards[2], shards[3])
+        data.append(jnp.where(low, even, swap(odd)))
+    u = total - alpha[0] * jnp.concatenate(data, axis=0)
     power = jnp.sum(jnp.sum(u * u, axis=0, keepdims=True), axis=1, keepdims=True)
     power_out[...] = jnp.broadcast_to(power, (8, 128))
     ub = u.astype(BF16)
@@ -428,24 +438,24 @@
 
     packed, slots = call(
         pack_body,
-        [shape((32, 4, 640), F32), shape((15,), jnp.int32)],
-        [SMEM, VMEM, VMEM],
+        [shape((32, 4, 512), F32), shape((15,), jnp.int32)],
+        [SMEM, VMEM],
         [SMEM((64,), jnp.int32), SMEM((SLOTS,), jnp.int32)],
         [VMEM, SMEM],
-    )(tile_receiver_block, direction, data_vec)
+    )(tile_receiver_block, direction)
     rows = exchange(packed, "tile")
     barrier = lax.optimization_barrier
-    lanes = lane_tables(slots, tile_source_block, ranks)
-    ids = rows[:, 0, 576 : 576 + SLOTS].astype(jnp.int32)
+    lanes = lane_tables(slots, tile_source_block, ranks, data_vec)
+    ids = rows[:, 0, 480 : 480 + SLOTS].astype(jnp.int32)
     ids, lanes = barrier((ids, lanes))
-    lane_slot, lane_block, limits = lanes
-    picked, direction_rows, data_rows = call(
+    lane_slot, lane_block, limits, data_rows = lanes
+    picked, direction_rows = call(
         spread_body,
-        [shape((32, 64, 128), BF16), shape((60, 8, 128), F32), shape((8, 8, 128), F32)],
-        [SMEM, VMEM],
-    )(ids, rows)
+        [shape((32, 64, 128), BF16), shape((60, 8, 128), F32)],
+        [SMEM, VMEM, VMEM],
+    )(ids, rows, data_rows)
     x = exchange(picked, "tile")
-    model, data_rows = barrier((model, data_rows))
+    model, direction_rows = barrier((model, direction_rows))
     (own_model,) = call(model_body, [shape((32, 16, 128), BF16)], [VMEM])(model)
     models = [own_model] + [
         lax.ppermute(own_model, "freq", [(i, (i + d) % 4) for i in range(4)]) for d in (1, 2, 3)
@@ -457,7 +467,7 @@
         residual_body,
         [shape((32, 64, 128), BF16), shape((8, 128), F32)],
         [SMEM, VMEM, VMEM],
-    )(alpha.reshape(1), parts, data_rows)
+    )(alpha.reshape(1), parts, x)
     others = [lax.ppermute(power, "freq", [(i, (i + d) % 4) for i in range(4)]) for d in (1, 2, 3)]
     u_all = exchange(residual, "tile")
     (powers,) = call(powers_body, [shape((8, 128), F32)], [VMEM] * 4)(power, *others)

time: 136 us -> 135 us (level)
  no operation moved by 1% of the time
where the time goes in v5:
time: 135 us; the launch traced here: 134 us
  starting transfers between devices  38.7 us (29%)
  waiting for transfers between devices  37.4 us (28%)
  Pallas kernels  34.6 us (26%)
  blocking collectives  16.6 us (12%)
  local copies, waits for them, and re-layouts  4.86 us (4%)
  between operations  1.52 us (1%)
    all_to_all x5, waiting for transfers between devices, exchange(): return lax.all_to_all(x, axis, split_axis=0, concat_axis=0, tiled=True)  34.8 us
    all_to_all x5, starting transfers between devices, exchange(): return lax.all_to_all(x, axis, split_axis=0, concat_axis=0, tiled=True)  25.6 us
    pallas_call x2, Pallas kernels, tile_products(): call(functools.partial(tiles_body, bool(extra)), [jax.ShapeDtypeStruct((2...  20.3 us
    all_to_all x1, blocking collectives, exchange(): return lax.all_to_all(x, axis, split_axis=0, concat_axis=0, tiled=True)  16.6 us
    ppermute x3, starting transfers between devices, on_device(): lax.ppermute(own_model, 'freq', [(i, (i + d) % 4) for i in range(4)])  6.58 us
    ppermute x3, starting transfers between devices, on_device(): lax.ppermute(power, 'freq', [(i, (i + d) % 4) for i in range(4)])  6.57 us
    pallas_call x1, Pallas kernels, on_device(): call(shrink_body, [shape(direction.shape, F32), shape(direction.shape, F3...  5.32 us
    unnamed x24, local copies, waits for them, and re-layouts  4.77 us
  transfers between devices with their start and end apart: 11, of which 7 were waited for; matrix products, arithmetic and copies ran while one was open for 0% of the time, Pallas kernels for 9%

profile of v5, /device:TPU:0, one launch (start us, length us, event | category | flops | bytes accessed | tf_op | source)
XLA Modules:
  0.0 133.8 jit_solution(16339849438250152296)
XLA Ops:
  2.2 1.8 %shard_map.166 = (f32[32,4,512]{2,1,0:T(4,128)}, s32[15]{0:T(128)S(1)}) custom-call(s32[15]{0:T(128)S(1)} %copy-done.8, f32[2,16,4,480]{3,2,1,0:T(4,128)S(1)} %copy-done.1), custom_call_target="tpu_custom_call" | custom-call | tf_op jit(solution)/shard_map/pallas_call | solution.py:439
  4.0 7.4 %all-to-all-start = ((f32[32,4,512]{2,1,0:T(4,128)}), f32[32,4,512]{2,1,0:T(4,128)S(1)}, u32[]{:S(2)}, u32[]{:S(2)}) async-start(f32[32,4,512]{2,1,0:T(4,128)} %get-tuple-element.29), calls=%async_computation | async-start | bytes 524288 | tf_op jit(solution)/shard_map/all_to_all | solution.py:437
  14.3 6.1 %all-to-all-done.rows = f32[32,4,512]{2,1,0:T(4,128)S(1)} async-done(((f32[32,4,512]{2,1,0:T(4,128)}), f32[32,4,512]{2,1,0:T(4,128)S(1)}, u32[]{:S(2)}, u32[]{:S(2)}) %all-to-all-start) | async-done | bytes 262176 | tf_op jit(solution)/shard_map/all_to_all | solution.py:437
  20.5 2.0 %shard_map.168 = (bf16[32,64,128]{2,1,0:T(8,128)(2,1)}, f32[60,8,128]{2,1,0:T(8,128)S(1)}) custom-call(s32[32,8]{1,0:T(8,128)S(1)} %convert_bitcast_fusion.ids, f32[32,4,512]{2,1,0:T(4,128)S(1)} %all-to-all-done.rows, f32[32,8,128]{2,1,0:T(8,128)S(1)} %get-tuple-element.39.data), custom_call_target="tpu_custom_call" | custom-call | tf_op jit(solution)/shard_map/pallas_call | solution.py:452
  22.5 3.9 %all-to-all-start.1 = ((bf16[32,64,128]{2,1,0:T(8,128)(2,1)}), bf16[32,64,128]{2,1,0:T(8,128)(2,1)S(1)}, u32[]{:S(2)}, u32[]{:S(2)}) async-start(bf16[32,64,128]{2,1,0:T(8,128)(2,1)} %get-tuple-element.40), calls=%async_computation.1 | async-start | bytes 1048576 | tf_op jit(solution)/shard_map/all_to_all | solution.py:437
  27.4 2.0 %collective-permute-start = (bf16[32,16,128]{2,1,0:T(8,128)(2,1)S(1)}, bf16[32,16,128]{2,1,0:T(8,128)(2,1)S(1)}, u32[]{:S(2)}, u32[]{:S(2)}) collective-permute-start(bf16[32,16,128]{2,1,0:T(8,128)(2,1)S(1)} %shard_map.170.m0), channel_id=1, source_target_pairs={{0,32},{32,64},{64,96},{96,0},{1,33},{33,65},{65,97},{97,1},{2,34}... | collective-permute-start | bytes 393224 | tf_op jit(solution)/shard_map/ppermute | solution.py:461
  29.4 3.6 %collective-permute-start.1 = (bf16[32,16,128]{2,1,0:T(8,128)(2,1)S(1)}, bf16[32,16,128]{2,1,0:T(8,128)(2,1)S(1)}, u32[]{:S(2)}, u32[]{:S(2)}) collective-permute-start(bf16[32,16,128]{2,1,0:T(8,128)(2,1)S(1)} %shard_map.170.m0), channel_id=1, source_target_pairs={{0,64},{32,96},{64,0},{96,32},{1,65},{33,97},{65,1},{97,33},{2,66}... | collective-permute-start | bytes 393224 | tf_op jit(solution)/shard_map/ppermute | solution.py:461
  33.0 1.0 collective-permute-start.2
  34.0 3.6 %all-to-all-done.1.x = bf16[32,64,128]{2,1,0:T(8,128)(2,1)S(1)} async-done(((bf16[32,64,128]{2,1,0:T(8,128)(2,1)}), bf16[32,64,128]{2,1,0:T(8,128)(2,1)S(1)}, u32[]{:S(2)}, u32[]{:S(2)}) %all-to-all-start.1) | async-done | bytes 524320 | tf_op jit(solution)/shard_map/all_to_all | solution.py:437
  37.6 10.6 %shard_map.169 = bf16[32,64,128]{2,1,0:T(8,128)(2,1)} custom-call(s32[8,720]{1,0:T(8,128)S(1)} %get-tuple-element.37.lane_in.lane_out, s32[8,720]{1,0:T(8,128)S(1)} %get-tuple-element.36.lane_out.lane_in, s32[16,720]{1,0:T(8,128)S(1)} %get-tuple-element.38.limits, bf16[32,64,128]{2,1,0:T(8,128)(2,1)S(1)} %all-to-all-done.1.x, ...), custom_call_target="tpu_custom_call" | custom-call | tf_op jit(solution)/shard_map/pallas_call | solution.py:248
  48.2 4.0 %all-to-all-start.2 = ((bf16[32,64,128]{2,1,0:T(8,128)(2,1)}), bf16[32,64,128]{2,1,0:T(8,128)(2,1)S(1)}, u32[]{:S(2)}, u32[]{:S(2)}) async-start(bf16[32,64,128]{2,1,0:T(8,128)(2,1)} %shard_map.169), calls=%async_computation.2 | async-start | bytes 1048576 | tf_op jit(solution)/shard_map/all_to_all | solution.py:437
  52.9 10.5 %all-to-all-done.2.parts = bf16[32,64,128]{2,1,0:T(8,128)(2,1)S(1)} async-done(((bf16[32,64,128]{2,1,0:T(8,128)(2,1)}), bf16[32,64,128]{2,1,0:T(8,128)(2,1)S(1)}, u32[]{:S(2)}, u32[]{:S(2)}) %all-to-all-start.2) | async-done | bytes 524320 | tf_op jit(solution)/shard_map/all_to_all | solution.py:437
  64.4 4.1 %all-to-all-start.3 = ((bf16[32,64,128]{2,1,0:T(8,128)(2,1)}), bf16[32,64,128]{2,1,0:T(8,128)(2,1)S(1)}, u32[]{:S(2)}, u32[]{:S(2)}) async-start(bf16[32,64,128]{2,1,0:T(8,128)(2,1)} %get-tuple-element.44), calls=%async_computation.3 | async-start | bytes 1048576 | tf_op jit(solution)/shard_map/all_to_all | solution.py:437
  68.5 2.0 %collective-permute-start.3 = (f32[8,128]{1,0:T(8,128)S(1)}, f32[8,128]{1,0:T(8,128)S(1)}, u32[]{:S(2)}, u32[]{:S(2)}) collective-permute-start(f32[8,128]{1,0:T(8,128)S(1)} %get-tuple-element.45.own), channel_id=1, source_target_pairs={{0,32},{32,64},{64,96},{96,0},{1,33},{33,65},{65,97},{97,1},{2,34}... | collective-permute-start | bytes 12296 | tf_op jit(solution)/shard_map/ppermute | solution.py:471
  70.4 3.6 %collective-permute-start.4 = (f32[8,128]{1,0:T(8,128)S(1)}, f32[8,128]{1,0:T(8,128)S(1)}, u32[]{:S(2)}, u32[]{:S(2)}) collective-permute-start(f32[8,128]{1,0:T(8,128)S(1)} %get-tuple-element.45.own), channel_id=1, source_target_pairs={{0,64},{32,96},{64,0},{96,32},{1,65},{33,97},{65,1},{97,33},{2,66}... | collective-permute-start | bytes 12296 | tf_op jit(solution)/shard_map/ppermute | solution.py:471
  74.0 1.0 collective-permute-start.5
  75.6 2.0 %collective-permute-done.5.p3 = f32[8,128]{1,0:T(8,128)S(1)} collective-permute-done((f32[8,128]{1,0:T(8,128)S(1)}, f32[8,128]{1,0:T(8,128)S(1)}, u32[]{:S(2)}, u32[]{:S(2)}) %collective-permute-start.5) | collective-permute-done | bytes 4128 | tf_op jit(solution)/shard_map/ppermute | solution.py:471
  77.7 1.9 %all-to-all-done.3.x.u = bf16[32,64,128]{2,1,0:T(8,128)(2,1)S(1)} async-done(((bf16[32,64,128]{2,1,0:T(8,128)(2,1)}), bf16[32,64,128]{2,1,0:T(8,128)(2,1)S(1)}, u32[]{:S(2)}, u32[]{:S(2)}) %all-to-all-start.3) | async-done | bytes 524320 | tf_op jit(solution)/shard_map/all_to_all | solution.py:437
  79.6 9.8 %shard_map.173 = bf16[32,64,128]{2,1,0:T(8,128)(2,1)S(1)} custom-call(s32[8,720]{1,0:T(8,128)S(1)} %get-tuple-element.36.lane_out.lane_in, s32[8,720]{1,0:T(8,128)S(1)} %get-tuple-element.37.lane_in.lane_out, s32[16,720]{1,0:T(8,128)S(1)} %get-tuple-element.38.limits, bf16[32,64,128]{2,1,0:T(8,128)(2,1)S(1)} %all-to-all-done.3.x.u, ...), custom_call_target="tpu_custom_call" | custom-call | tf_op jit(solution)/shard_map/pallas_call | solution.py:248
  89.4 16.6 %all_to_all.30.parts = bf16[32,64,128]{2,1,0:T(8,128)(2,1)S(1)} all-to-all(bf16[32,64,128]{2,1,0:T(8,128)(2,1)S(1)} %shard_map.173), channel_id=1, replica_groups=mesh['freq'=4,'tile'=32] {'tile'}, dimensions={0} | all-to-all | bytes 1048576 | tf_op jit(solution)/shard_map/all_to_all | solution.py:437
  106.1 2.7 %shard_map.174 = (bf16[128,16,128]{2,1,0:T(8,128)(2,1)}, f32[8,128]{1,0:T(8,128)S(1)}) custom-call(s32[32,8]{1,0:T(8,128)S(1)} %convert_bitcast_fusion.ids, bf16[32,64,128]{2,1,0:T(8,128)(2,1)S(1)} %all_to_all.30.parts, f32[60,8,128]{2,1,0:T(8,128)S(1)} %get-tuple-element.46.direction), custom_call_target="tpu_custom_call" | custom-call | tf_op jit(solution)/shard_map/pallas_call | solution.py:477
  108.7 6.2 %all-to-all-start.5 = ((bf16[128,16,128]{2,1,0:T(8,128)(2,1)}), bf16[128,16,128]{2,1,0:T(8,128)(2,1)S(1)}, u32[]{:S(2)}, u32[]{:S(2)}) async-start(bf16[128,16,128]{2,1,0:T(8,128)(2,1)} %get-tuple-element.48), calls=%async_computation.5 | async-start | bytes 1048576 | tf_op jit(solution)/shard_map/all_to_all | solution.py:437
  115.8 12.7 %all-to-all-done.5.raw = bf16[128,16,128]{2,1,0:T(8,128)(2,1)S(1)} async-done(((bf16[128,16,128]{2,1,0:T(8,128)(2,1)}), bf16[128,16,128]{2,1,0:T(8,128)(2,1)S(1)}, u32[]{:S(2)}, u32[]{:S(2)}) %all-to-all-start.5) | async-done | bytes 524320 | tf_op jit(solution)/shard_map/all_to_all | solution.py:437
  128.5 5.3 %shard_map.176 = (f32[2,16,4,480]{3,2,1,0:T(4,128)}, f32[2,16,4,480]{3,2,1,0:T(4,128)}) custom-call(s32[1]{0:T(128)} %bitcast.3.group, bf16[128,16,128]{2,1,0:T(8,128)(2,1)S(1)} %all-to-all-done.5.raw, bf16[32,16,128]{2,1,0:T(8,128)(2,1)S(1)} %shard_map.170.m0, bf16[32,16,128]{2,1,0:T(8,128)(2,1)S(1)} %collective-permute-done.m1, ...), custom_call_target="tpu_custom_call" | custom-call | tf_op jit(solution)/shard_map/pallas_call | solution.py:491
  (38 shorter events, 8.0 us)
Async XLA Ops:
  0.6 1.0 copy-start.1
  1.6 0.7 copy-start.8
  4.0 16.4 %all-to-all-start = ((f32[32,4,512]{2,1,0:T(4,128)}), f32[32,4,512]{2,1,0:T(4,128)S(1)}, u32[]{:S(2)}, u32[]{:S(2)}) async-start(f32[32,4,512]{2,1,0:T(4,128)} %get-tuple-element.29), calls=%async_computation | async-start | bytes 524288 | tf_op jit(solution)/shard_map/all_to_all | solution.py:437
  11.5 0.8 copy-start.6
  12.3 0.7 copy-start.7
  13.0 0.7 copy-start.9
  22.5 15.1 %all-to-all-start.1 = ((bf16[32,64,128]{2,1,0:T(8,128)(2,1)}), bf16[32,64,128]{2,1,0:T(8,128)(2,1)S(1)}, u32[]{:S(2)}, u32[]{:S(2)}) async-start(bf16[32,64,128]{2,1,0:T(8,128)(2,1)} %get-tuple-element.40), calls=%async_computation.1 | async-start | bytes 1048576 | tf_op jit(solution)/shard_map/all_to_all | solution.py:437
  26.4 1.0 copy-start
  27.4 20.8 %collective-permute-start = (bf16[32,16,128]{2,1,0:T(8,128)(2,1)S(1)}, bf16[32,16,128]{2,1,0:T(8,128)(2,1)S(1)}, u32[]{:S(2)}, u32[]{:S(2)}) collective-permute-start(bf16[32,16,128]{2,1,0:T(8,128)(2,1)S(1)} %shard_map.170.m0), channel_id=1, source_target_pairs={{0,32},{32,64},{64,96},{96,0},{1,33},{33,65},{65,97},{97,1},{2,34}... | collective-permute-start | bytes 393224 | tf_op jit(solution)/shard_map/ppermute | solution.py:461
  29.4 18.8 %collective-permute-start.1 = (bf16[32,16,128]{2,1,0:T(8,128)(2,1)S(1)}, bf16[32,16,128]{2,1,0:T(8,128)(2,1)S(1)}, u32[]{:S(2)}, u32[]{:S(2)}) collective-permute-start(bf16[32,16,128]{2,1,0:T(8,128)(2,1)S(1)} %shard_map.170.m0), channel_id=1, source_target_pairs={{0,64},{32,96},{64,0},{96,32},{1,65},{33,97},{65,1},{97,33},{2,66}... | collective-permute-start | bytes 393224 | tf_op jit(solution)/shard_map/ppermute | solution.py:461
  33.0 15.2 %collective-permute-start.2 = (bf16[32,16,128]{2,1,0:T(8,128)(2,1)S(1)}, bf16[32,16,128]{2,1,0:T(8,128)(2,1)S(1)}, u32[]{:S(2)}, u32[]{:S(2)}) collective-permute-start(bf16[32,16,128]{2,1,0:T(8,128)(2,1)S(1)} %shard_map.170.m0), channel_id=1, source_target_pairs={{0,96},{32,0},{64,32},{96,64},{1,97},{33,1},{65,33},{97,65},{2,98}... | collective-permute-start | bytes 393224 | tf_op jit(solution)/shard_map/ppermute | solution.py:461
  48.2 15.2 %all-to-all-start.2 = ((bf16[32,64,128]{2,1,0:T(8,128)(2,1)}), bf16[32,64,128]{2,1,0:T(8,128)(2,1)S(1)}, u32[]{:S(2)}, u32[]{:S(2)}) async-start(bf16[32,64,128]{2,1,0:T(8,128)(2,1)} %shard_map.169), calls=%async_computation.2 | async-start | bytes 1048576 | tf_op jit(solution)/shard_map/all_to_all | solution.py:437
  64.4 15.3 %all-to-all-start.3 = ((bf16[32,64,128]{2,1,0:T(8,128)(2,1)}), bf16[32,64,128]{2,1,0:T(8,128)(2,1)S(1)}, u32[]{:S(2)}, u32[]{:S(2)}) async-start(bf16[32,64,128]{2,1,0:T(8,128)(2,1)} %get-tuple-element.44), calls=%async_computation.3 | async-start | bytes 1048576 | tf_op jit(solution)/shard_map/all_to_all | solution.py:437
  68.5 6.6 %collective-permute-start.3 = (f32[8,128]{1,0:T(8,128)S(1)}, f32[8,128]{1,0:T(8,128)S(1)}, u32[]{:S(2)}, u32[]{:S(2)}) collective-permute-start(f32[8,128]{1,0:T(8,128)S(1)} %get-tuple-element.45.own), channel_id=1, source_target_pairs={{0,32},{32,64},{64,96},{96,0},{1,33},{33,65},{65,97},{97,1},{2,34}... | collective-permute-start | bytes 12296 | tf_op jit(solution)/shard_map/ppermute | solution.py:471
  70.4 5.2 %collective-permute-start.4 = (f32[8,128]{1,0:T(8,128)S(1)}, f32[8,128]{1,0:T(8,128)S(1)}, u32[]{:S(2)}, u32[]{:S(2)}) collective-permute-start(f32[8,128]{1,0:T(8,128)S(1)} %get-tuple-element.45.own), channel_id=1, source_target_pairs={{0,64},{32,96},{64,0},{96,32},{1,65},{33,97},{65,1},{97,33},{2,66}... | collective-permute-start | bytes 12296 | tf_op jit(solution)/shard_map/ppermute | solution.py:471
  74.0 3.6 %collective-permute-start.5 = (f32[8,128]{1,0:T(8,128)S(1)}, f32[8,128]{1,0:T(8,128)S(1)}, u32[]{:S(2)}, u32[]{:S(2)}) collective-permute-start(f32[8,128]{1,0:T(8,128)S(1)} %get-tuple-element.45.own), channel_id=1, source_target_pairs={{0,96},{32,0},{64,32},{96,64},{1,97},{33,1},{65,33},{97,65},{2,98}... | collective-permute-start | bytes 12296 | tf_op jit(solution)/shard_map/ppermute | solution.py:471
  77.6 37.3 %copy-start.10 = (s32[480]{0:T(512)S(1)}, s32[480]{0:T(512)}, u32[]{:S(2)}) copy-start(s32[480]{0:T(512)} %param.24) | copy-start | bytes 5764
  77.7 37.3 %copy-start.11 = (s32[480]{0:T(512)S(1)}, s32[480]{0:T(512)}, u32[]{:S(2)}) copy-start(s32[480]{0:T(512)} %param.25) | copy-start | bytes 5764
  77.7 50.8 %copy-start.2 = (bf16[512,128]{1,0:T(8,128)(2,1)S(1)}, bf16[512,128]{1,0:T(8,128)(2,1)}, u32[]{:S(2)}) copy-start(bf16[512,128]{1,0:T(8,128)(2,1)} %constant.19.clone.fh) | copy-start | bytes 393220
  77.7 50.8 %copy-start.3 = (bf16[512,128]{1,0:T(8,128)(2,1)S(1)}, bf16[512,128]{1,0:T(8,128)(2,1)}, u32[]{:S(2)}) copy-start(bf16[512,128]{1,0:T(8,128)(2,1)} %constant.20.clone.fl) | copy-start | bytes 393220
  77.7 50.8 %copy-start.4 = (bf16[128,512]{1,0:T(8,128)(2,1)S(1)}, bf16[128,512]{1,0:T(8,128)(2,1)}, u32[]{:S(2)}) copy-start(bf16[128,512]{1,0:T(8,128)(2,1)} %constant.21.clone.bh) | copy-start | bytes 393220
  77.7 50.8 %copy-start.5 = (bf16[128,512]{1,0:T(8,128)(2,1)S(1)}, bf16[128,512]{1,0:T(8,128)(2,1)}, u32[]{:S(2)}) copy-start(bf16[128,512]{1,0:T(8,128)(2,1)} %constant.22.clone.bl) | copy-start | bytes 393220
  108.7 19.7 %all-to-all-start.5 = ((bf16[128,16,128]{2,1,0:T(8,128)(2,1)}), bf16[128,16,128]{2,1,0:T(8,128)(2,1)S(1)}, u32[]{:S(2)}, u32[]{:S(2)}) async-start(bf16[128,16,128]{2,1,0:T(8,128)(2,1)} %get-tuple-element.48), calls=%async_computation.5 | async-start | bytes 1048576 | tf_op jit(solution)/shard_map/all_to_all | solution.py:437

commit v6 on v5

--- a/solution.py
+++ b/solution.py
@@ -57,27 +57,20 @@
     )
 
 
-def pack_body(rb, direction, out, slot_of, mark, ids):
-    def clear(b, _):
-        mark[b] = -1
-        return 0
-
-    lax.fori_loop(0, 64, clear, 0)
-    for m in range(SLOTS):
-        ids[m] = 0
-    count = jnp.int32(0)
-    for t in range(rb.shape[0]):
-        b = rb[t]
-        seen = mark[b]
-        slot = jnp.minimum(jnp.where(seen < 0, count, seen), SLOTS - 1)
-        mark[b] = slot
-        ids[slot] = b
-        slot_of[t] = slot
-        count = count + jnp.where(seen < 0, 1, 0)
+def pack_body(rb, direction, out, slot_of):
+    blocks = [rb[t] for t in range(rb.shape[0])]
     lane = iota((4, 128), 1)
     listed = jnp.zeros((4, 128), F32)
-    for m in range(SLOTS):
-        listed = jnp.where(lane == 96 + m, ids[m].astype(F32), listed)
+    slots = []
+    count = jnp.int32(0)
+    for t, b in enumerate(blocks):
+        slot = count
+        for earlier, at in zip(blocks[:t], slots):
+            slot = jnp.where(b == earlier, at, slot)
+        slots.append(slot)
+        slot_of[t] = slot
+        count = jnp.maximum(count, slot + 1)
+        listed = jnp.where(lane == 96 + slot, b.astype(F32), listed)
     for f in range(direction.shape[1]):
         for c in range(2):
             k = 2 * f + c
@@ -440,7 +433,7 @@
         pack_body,
         [shape((32, 4, 512), F32), shape((15,), jnp.int32)],
         [SMEM, VMEM],
-        [SMEM((64,), jnp.int32), SMEM((SLOTS,), jnp.int32)],
+        (),
         [VMEM, SMEM],
     )(tile_receiver_block, direction)
     rows = exchange(packed, "tile")

time: 135 us -> 134 us (level)
  no operation moved by 1% of the time
where the time goes in v6:
time: 134 us; the launch traced here: 133 us
  starting transfers between devices  38.8 us (29%)
  waiting for transfers between devices  37.4 us (28%)
  Pallas kernels  34.2 us (26%)
  blocking collectives  16.7 us (12%)
  local copies, waits for them, and re-layouts  4.86 us (4%)
  between operations  1.52 us (1%)
    all_to_all x5, waiting for transfers between devices, exchange(): return lax.all_to_all(x, axis, split_axis=0, concat_axis=0, tiled=True)  34.8 us
    all_to_all x5, starting transfers between devices, exchange(): return lax.all_to_all(x, axis, split_axis=0, concat_axis=0, tiled=True)  25.6 us
    pallas_call x2, Pallas kernels, tile_products(): call(functools.partial(tiles_body, bool(extra)), [jax.ShapeDtypeStruct((2...  20.3 us
    all_to_all x1, blocking collectives, exchange(): return lax.all_to_all(x, axis, split_axis=0, concat_axis=0, tiled=True)  16.7 us
    ppermute x3, starting transfers between devices, on_device(): lax.ppermute(power, 'freq', [(i, (i + d) % 4) for i in range(4)])  6.58 us
    ppermute x3, starting transfers between devices, on_device(): lax.ppermute(own_model, 'freq', [(i, (i + d) % 4) for i in range(4)])  6.58 us
    pallas_call x1, Pallas kernels, on_device(): call(shrink_body, [shape(direction.shape, F32), shape(direction.shape, F3...  5.32 us
    unnamed x24, local copies, waits for them, and re-layouts  4.77 us
  transfers between devices with their start and end apart: 11, of which 7 were waited for; matrix products, arithmetic and copies ran while one was open for 0% of the time, Pallas kernels for 9%

profile of v6, /device:TPU:0, one launch (start us, length us, event | category | flops | bytes accessed | tf_op | source)
XLA Modules:
  0.0 133.4 jit_solution(6090879375929552267)
XLA Ops:
  2.2 1.4 %shard_map.166 = (f32[32,4,512]{2,1,0:T(4,128)}, s32[15]{0:T(128)S(1)}) custom-call(s32[15]{0:T(128)S(1)} %copy-done.8, f32[2,16,4,480]{3,2,1,0:T(4,128)S(1)} %copy-done.1), custom_call_target="tpu_custom_call" | custom-call | tf_op jit(solution)/shard_map/pallas_call | solution.py:432
  3.6 7.4 %all-to-all-start = ((f32[32,4,512]{2,1,0:T(4,128)}), f32[32,4,512]{2,1,0:T(4,128)S(1)}, u32[]{:S(2)}, u32[]{:S(2)}) async-start(f32[32,4,512]{2,1,0:T(4,128)} %get-tuple-element.29), calls=%async_computation | async-start | bytes 524288 | tf_op jit(solution)/shard_map/all_to_all | solution.py:430
  14.0 6.1 %all-to-all-done.rows = f32[32,4,512]{2,1,0:T(4,128)S(1)} async-done(((f32[32,4,512]{2,1,0:T(4,128)}), f32[32,4,512]{2,1,0:T(4,128)S(1)}, u32[]{:S(2)}, u32[]{:S(2)}) %all-to-all-start) | async-done | bytes 262176 | tf_op jit(solution)/shard_map/all_to_all | solution.py:430
  20.1 2.0 %shard_map.168 = (bf16[32,64,128]{2,1,0:T(8,128)(2,1)}, f32[60,8,128]{2,1,0:T(8,128)S(1)}) custom-call(s32[32,8]{1,0:T(8,128)S(1)} %convert_bitcast_fusion.ids, f32[32,4,512]{2,1,0:T(4,128)S(1)} %all-to-all-done.rows, f32[32,8,128]{2,1,0:T(8,128)S(1)} %get-tuple-element.39.data), custom_call_target="tpu_custom_call" | custom-call | tf_op jit(solution)/shard_map/pallas_call | solution.py:445
  22.1 3.9 %all-to-all-start.1 = ((bf16[32,64,128]{2,1,0:T(8,128)(2,1)}), bf16[32,64,128]{2,1,0:T(8,128)(2,1)S(1)}, u32[]{:S(2)}, u32[]{:S(2)}) async-start(bf16[32,64,128]{2,1,0:T(8,128)(2,1)} %get-tuple-element.40), calls=%async_computation.1 | async-start | bytes 1048576 | tf_op jit(solution)/shard_map/all_to_all | solution.py:430
  27.0 2.0 %collective-permute-start = (bf16[32,16,128]{2,1,0:T(8,128)(2,1)S(1)}, bf16[32,16,128]{2,1,0:T(8,128)(2,1)S(1)}, u32[]{:S(2)}, u32[]{:S(2)}) collective-permute-start(bf16[32,16,128]{2,1,0:T(8,128)(2,1)S(1)} %shard_map.170.m0), channel_id=1, source_target_pairs={{0,32},{32,64},{64,96},{96,0},{1,33},{33,65},{65,97},{97,1},{2,34}... | collective-permute-start | bytes 393224 | tf_op jit(solution)/shard_map/ppermute | solution.py:454
  29.0 3.6 %collective-permute-start.1 = (bf16[32,16,128]{2,1,0:T(8,128)(2,1)S(1)}, bf16[32,16,128]{2,1,0:T(8,128)(2,1)S(1)}, u32[]{:S(2)}, u32[]{:S(2)}) collective-permute-start(bf16[32,16,128]{2,1,0:T(8,128)(2,1)S(1)} %shard_map.170.m0), channel_id=1, source_target_pairs={{0,64},{32,96},{64,0},{96,32},{1,65},{33,97},{65,1},{97,33},{2,66}... | collective-permute-start | bytes 393224 | tf_op jit(solution)/shard_map/ppermute | solution.py:454
  32.6 1.0 collective-permute-start.2
  33.6 3.6 %all-to-all-done.1.x = bf16[32,64,128]{2,1,0:T(8,128)(2,1)S(1)} async-done(((bf16[32,64,128]{2,1,0:T(8,128)(2,1)}), bf16[32,64,128]{2,1,0:T(8,128)(2,1)S(1)}, u32[]{:S(2)}, u32[]{:S(2)}) %all-to-all-start.1) | async-done | bytes 524320 | tf_op jit(solution)/shard_map/all_to_all | solution.py:430
  37.2 10.6 %shard_map.169 = bf16[32,64,128]{2,1,0:T(8,128)(2,1)} custom-call(s32[8,720]{1,0:T(8,128)S(1)} %get-tuple-element.37.lane_in.lane_out, s32[8,720]{1,0:T(8,128)S(1)} %get-tuple-element.36.lane_out.lane_in, s32[16,720]{1,0:T(8,128)S(1)} %get-tuple-element.38.limits, bf16[32,64,128]{2,1,0:T(8,128)(2,1)S(1)} %all-to-all-done.1.x, ...), custom_call_target="tpu_custom_call" | custom-call | tf_op jit(solution)/shard_map/pallas_call | solution.py:241
  47.8 4.0 %all-to-all-start.2 = ((bf16[32,64,128]{2,1,0:T(8,128)(2,1)}), bf16[32,64,128]{2,1,0:T(8,128)(2,1)S(1)}, u32[]{:S(2)}, u32[]{:S(2)}) async-start(bf16[32,64,128]{2,1,0:T(8,128)(2,1)} %shard_map.169), calls=%async_computation.2 | async-start | bytes 1048576 | tf_op jit(solution)/shard_map/all_to_all | solution.py:430
  52.5 10.5 %all-to-all-done.2.parts = bf16[32,64,128]{2,1,0:T(8,128)(2,1)S(1)} async-done(((bf16[32,64,128]{2,1,0:T(8,128)(2,1)}), bf16[32,64,128]{2,1,0:T(8,128)(2,1)S(1)}, u32[]{:S(2)}, u32[]{:S(2)}) %all-to-all-start.2) | async-done | bytes 524320 | tf_op jit(solution)/shard_map/all_to_all | solution.py:430
  64.0 4.1 %all-to-all-start.3 = ((bf16[32,64,128]{2,1,0:T(8,128)(2,1)}), bf16[32,64,128]{2,1,0:T(8,128)(2,1)S(1)}, u32[]{:S(2)}, u32[]{:S(2)}) async-start(bf16[32,64,128]{2,1,0:T(8,128)(2,1)} %get-tuple-element.44), calls=%async_computation.3 | async-start | bytes 1048576 | tf_op jit(solution)/shard_map/all_to_all | solution.py:430
  68.1 2.0 %collective-permute-start.3 = (f32[8,128]{1,0:T(8,128)S(1)}, f32[8,128]{1,0:T(8,128)S(1)}, u32[]{:S(2)}, u32[]{:S(2)}) collective-permute-start(f32[8,128]{1,0:T(8,128)S(1)} %get-tuple-element.45.own), channel_id=1, source_target_pairs={{0,32},{32,64},{64,96},{96,0},{1,33},{33,65},{65,97},{97,1},{2,34}... | collective-permute-start | bytes 12296 | tf_op jit(solution)/shard_map/ppermute | solution.py:464
  70.0 3.6 %collective-permute-start.4 = (f32[8,128]{1,0:T(8,128)S(1)}, f32[8,128]{1,0:T(8,128)S(1)}, u32[]{:S(2)}, u32[]{:S(2)}) collective-permute-start(f32[8,128]{1,0:T(8,128)S(1)} %get-tuple-element.45.own), channel_id=1, source_target_pairs={{0,64},{32,96},{64,0},{96,32},{1,65},{33,97},{65,1},{97,33},{2,66}... | collective-permute-start | bytes 12296 | tf_op jit(solution)/shard_map/ppermute | solution.py:464
  73.6 1.0 collective-permute-start.5
  75.2 2.0 %collective-permute-done.5.p3 = f32[8,128]{1,0:T(8,128)S(1)} collective-permute-done((f32[8,128]{1,0:T(8,128)S(1)}, f32[8,128]{1,0:T(8,128)S(1)}, u32[]{:S(2)}, u32[]{:S(2)}) %collective-permute-start.5) | collective-permute-done | bytes 4128 | tf_op jit(solution)/shard_map/ppermute | solution.py:464
  77.3 1.9 %all-to-all-done.3.x.u = bf16[32,64,128]{2,1,0:T(8,128)(2,1)S(1)} async-done(((bf16[32,64,128]{2,1,0:T(8,128)(2,1)}), bf16[32,64,128]{2,1,0:T(8,128)(2,1)S(1)}, u32[]{:S(2)}, u32[]{:S(2)}) %all-to-all-start.3) | async-done | bytes 524320 | tf_op jit(solution)/shard_map/all_to_all | solution.py:430
  79.2 9.8 %shard_map.173 = bf16[32,64,128]{2,1,0:T(8,128)(2,1)S(1)} custom-call(s32[8,720]{1,0:T(8,128)S(1)} %get-tuple-element.36.lane_out.lane_in, s32[8,720]{1,0:T(8,128)S(1)} %get-tuple-element.37.lane_in.lane_out, s32[16,720]{1,0:T(8,128)S(1)} %get-tuple-element.38.limits, bf16[32,64,128]{2,1,0:T(8,128)(2,1)S(1)} %all-to-all-done.3.x.u, ...), custom_call_target="tpu_custom_call" | custom-call | tf_op jit(solution)/shard_map/pallas_call | solution.py:241
  89.0 16.7 %all_to_all.30.parts = bf16[32,64,128]{2,1,0:T(8,128)(2,1)S(1)} all-to-all(bf16[32,64,128]{2,1,0:T(8,128)(2,1)S(1)} %shard_map.173), channel_id=1, replica_groups=mesh['freq'=4,'tile'=32] {'tile'}, dimensions={0} | all-to-all | bytes 1048576 | tf_op jit(solution)/shard_map/all_to_all | solution.py:430
  105.7 2.7 %shard_map.174 = (bf16[128,16,128]{2,1,0:T(8,128)(2,1)}, f32[8,128]{1,0:T(8,128)S(1)}) custom-call(s32[32,8]{1,0:T(8,128)S(1)} %convert_bitcast_fusion.ids, bf16[32,64,128]{2,1,0:T(8,128)(2,1)S(1)} %all_to_all.30.parts, f32[60,8,128]{2,1,0:T(8,128)S(1)} %get-tuple-element.46.direction), custom_call_target="tpu_custom_call" | custom-call | tf_op jit(solution)/shard_map/pallas_call | solution.py:470
  108.3 6.2 %all-to-all-start.5 = ((bf16[128,16,128]{2,1,0:T(8,128)(2,1)}), bf16[128,16,128]{2,1,0:T(8,128)(2,1)S(1)}, u32[]{:S(2)}, u32[]{:S(2)}) async-start(bf16[128,16,128]{2,1,0:T(8,128)(2,1)} %get-tuple-element.48), calls=%async_computation.5 | async-start | bytes 1048576 | tf_op jit(solution)/shard_map/all_to_all | solution.py:430
  115.4 12.7 %all-to-all-done.5.raw = bf16[128,16,128]{2,1,0:T(8,128)(2,1)S(1)} async-done(((bf16[128,16,128]{2,1,0:T(8,128)(2,1)}), bf16[128,16,128]{2,1,0:T(8,128)(2,1)S(1)}, u32[]{:S(2)}, u32[]{:S(2)}) %all-to-all-start.5) | async-done | bytes 524320 | tf_op jit(solution)/shard_map/all_to_all | solution.py:430
  128.1 5.3 %shard_map.176 = (f32[2,16,4,480]{3,2,1,0:T(4,128)}, f32[2,16,4,480]{3,2,1,0:T(4,128)}) custom-call(s32[1]{0:T(128)} %bitcast.3.group, bf16[128,16,128]{2,1,0:T(8,128)(2,1)S(1)} %all-to-all-done.5.raw, bf16[32,16,128]{2,1,0:T(8,128)(2,1)S(1)} %shard_map.170.m0, bf16[32,16,128]{2,1,0:T(8,128)(2,1)S(1)} %collective-permute-done.m1, ...), custom_call_target="tpu_custom_call" | custom-call | tf_op jit(solution)/shard_map/pallas_call | solution.py:484
  (38 shorter events, 8.0 us)
Async XLA Ops:
  0.6 1.0 copy-start.1
  1.6 0.7 copy-start.8
  3.6 16.4 %all-to-all-start = ((f32[32,4,512]{2,1,0:T(4,128)}), f32[32,4,512]{2,1,0:T(4,128)S(1)}, u32[]{:S(2)}, u32[]{:S(2)}) async-start(f32[32,4,512]{2,1,0:T(4,128)} %get-tuple-element.29), calls=%async_computation | async-start | bytes 524288 | tf_op jit(solution)/shard_map/all_to_all | solution.py:430
  11.1 0.8 copy-start.6
  11.9 0.7 copy-start.7
  12.6 0.7 copy-start.9
  22.1 15.1 %all-to-all-start.1 = ((bf16[32,64,128]{2,1,0:T(8,128)(2,1)}), bf16[32,64,128]{2,1,0:T(8,128)(2,1)S(1)}, u32[]{:S(2)}, u32[]{:S(2)}) async-start(bf16[32,64,128]{2,1,0:T(8,128)(2,1)} %get-tuple-element.40), calls=%async_computation.1 | async-start | bytes 1048576 | tf_op jit(solution)/shard_map/all_to_all | solution.py:430
  26.0 1.0 copy-start
  27.0 20.8 %collective-permute-start = (bf16[32,16,128]{2,1,0:T(8,128)(2,1)S(1)}, bf16[32,16,128]{2,1,0:T(8,128)(2,1)S(1)}, u32[]{:S(2)}, u32[]{:S(2)}) collective-permute-start(bf16[32,16,128]{2,1,0:T(8,128)(2,1)S(1)} %shard_map.170.m0), channel_id=1, source_target_pairs={{0,32},{32,64},{64,96},{96,0},{1,33},{33,65},{65,97},{97,1},{2,34}... | collective-permute-start | bytes 393224 | tf_op jit(solution)/shard_map/ppermute | solution.py:454
  29.0 18.8 %collective-permute-start.1 = (bf16[32,16,128]{2,1,0:T(8,128)(2,1)S(1)}, bf16[32,16,128]{2,1,0:T(8,128)(2,1)S(1)}, u32[]{:S(2)}, u32[]{:S(2)}) collective-permute-start(bf16[32,16,128]{2,1,0:T(8,128)(2,1)S(1)} %shard_map.170.m0), channel_id=1, source_target_pairs={{0,64},{32,96},{64,0},{96,32},{1,65},{33,97},{65,1},{97,33},{2,66}... | collective-permute-start | bytes 393224 | tf_op jit(solution)/shard_map/ppermute | solution.py:454
  32.6 15.2 %collective-permute-start.2 = (bf16[32,16,128]{2,1,0:T(8,128)(2,1)S(1)}, bf16[32,16,128]{2,1,0:T(8,128)(2,1)S(1)}, u32[]{:S(2)}, u32[]{:S(2)}) collective-permute-start(bf16[32,16,128]{2,1,0:T(8,128)(2,1)S(1)} %shard_map.170.m0), channel_id=1, source_target_pairs={{0,96},{32,0},{64,32},{96,64},{1,97},{33,1},{65,33},{97,65},{2,98}... | collective-permute-start | bytes 393224 | tf_op jit(solution)/shard_map/ppermute | solution.py:454
  47.8 15.2 %all-to-all-start.2 = ((bf16[32,64,128]{2,1,0:T(8,128)(2,1)}), bf16[32,64,128]{2,1,0:T(8,128)(2,1)S(1)}, u32[]{:S(2)}, u32[]{:S(2)}) async-start(bf16[32,64,128]{2,1,0:T(8,128)(2,1)} %shard_map.169), calls=%async_computation.2 | async-start | bytes 1048576 | tf_op jit(solution)/shard_map/all_to_all | solution.py:430
  64.0 15.3 %all-to-all-start.3 = ((bf16[32,64,128]{2,1,0:T(8,128)(2,1)}), bf16[32,64,128]{2,1,0:T(8,128)(2,1)S(1)}, u32[]{:S(2)}, u32[]{:S(2)}) async-start(bf16[32,64,128]{2,1,0:T(8,128)(2,1)} %get-tuple-element.44), calls=%async_computation.3 | async-start | bytes 1048576 | tf_op jit(solution)/shard_map/all_to_all | solution.py:430
  68.1 6.6 %collective-permute-start.3 = (f32[8,128]{1,0:T(8,128)S(1)}, f32[8,128]{1,0:T(8,128)S(1)}, u32[]{:S(2)}, u32[]{:S(2)}) collective-permute-start(f32[8,128]{1,0:T(8,128)S(1)} %get-tuple-element.45.own), channel_id=1, source_target_pairs={{0,32},{32,64},{64,96},{96,0},{1,33},{33,65},{65,97},{97,1},{2,34}... | collective-permute-start | bytes 12296 | tf_op jit(solution)/shard_map/ppermute | solution.py:464
  70.0 5.2 %collective-permute-start.4 = (f32[8,128]{1,0:T(8,128)S(1)}, f32[8,128]{1,0:T(8,128)S(1)}, u32[]{:S(2)}, u32[]{:S(2)}) collective-permute-start(f32[8,128]{1,0:T(8,128)S(1)} %get-tuple-element.45.own), channel_id=1, source_target_pairs={{0,64},{32,96},{64,0},{96,32},{1,65},{33,97},{65,1},{97,33},{2,66}... | collective-permute-start | bytes 12296 | tf_op jit(solution)/shard_map/ppermute | solution.py:464
  73.6 3.6 %collective-permute-start.5 = (f32[8,128]{1,0:T(8,128)S(1)}, f32[8,128]{1,0:T(8,128)S(1)}, u32[]{:S(2)}, u32[]{:S(2)}) collective-permute-start(f32[8,128]{1,0:T(8,128)S(1)} %get-tuple-element.45.own), channel_id=1, source_target_pairs={{0,96},{32,0},{64,32},{96,64},{1,97},{33,1},{65,33},{97,65},{2,98}... | collective-permute-start | bytes 12296 | tf_op jit(solution)/shard_map/ppermute | solution.py:464
  77.2 37.3 %copy-start.10 = (s32[480]{0:T(512)S(1)}, s32[480]{0:T(512)}, u32[]{:S(2)}) copy-start(s32[480]{0:T(512)} %param.24) | copy-start | bytes 5764
  77.3 37.3 %copy-start.11 = (s32[480]{0:T(512)S(1)}, s32[480]{0:T(512)}, u32[]{:S(2)}) copy-start(s32[480]{0:T(512)} %param.25) | copy-start | bytes 5764
  77.3 50.8 %copy-start.2 = (bf16[512,128]{1,0:T(8,128)(2,1)S(1)}, bf16[512,128]{1,0:T(8,128)(2,1)}, u32[]{:S(2)}) copy-start(bf16[512,128]{1,0:T(8,128)(2,1)} %constant.19.clone.fh) | copy-start | bytes 393220
  77.3 50.8 %copy-start.3 = (bf16[512,128]{1,0:T(8,128)(2,1)S(1)}, bf16[512,128]{1,0:T(8,128)(2,1)}, u32[]{:S(2)}) copy-start(bf16[512,128]{1,0:T(8,128)(2,1)} %constant.20.clone.fl) | copy-start | bytes 393220
  77.3 50.8 %copy-start.4 = (bf16[128,512]{1,0:T(8,128)(2,1)S(1)}, bf16[128,512]{1,0:T(8,128)(2,1)}, u32[]{:S(2)}) copy-start(bf16[128,512]{1,0:T(8,128)(2,1)} %constant.21.clone.bh) | copy-start | bytes 393220
  77.3 50.8 %copy-start.5 = (bf16[128,512]{1,0:T(8,128)(2,1)S(1)}, bf16[128,512]{1,0:T(8,128)(2,1)}, u32[]{:S(2)}) copy-start(bf16[128,512]{1,0:T(8,128)(2,1)} %constant.22.clone.bl) | copy-start | bytes 393220
  108.3 19.7 %all-to-all-start.5 = ((bf16[128,16,128]{2,1,0:T(8,128)(2,1)}), bf16[128,16,128]{2,1,0:T(8,128)(2,1)S(1)}, u32[]{:S(2)}, u32[]{:S(2)}) async-start(bf16[128,16,128]{2,1,0:T(8,128)(2,1)} %get-tuple-element.48), calls=%async_computation.5 | async-start | bytes 1048576 | tf_op jit(solution)/shard_map/all_to_all | solution.py:430
